TPU v7x, 256 devices: a whole 4x4x8 slice. The times are simulated.
256 devices in a mesh: row: 32 (over y, z_lo, x), col: 8 (over z_hi, core).
Axes of the slice: x: 4, y: 4, z: 8 (z_hi: 4, z_lo: 2; z = z_hi * 2 + z_lo), core: 2. Of those that a mesh axis runs over, the one named last changes fastest.
Arguments:
- window_factors: bfloat16 [4, 512, 1536], P(None, 'col', 'row'), may hold values from -6 to 6
- factors: bfloat16 [512, 512, 1536], P('col', 'row'), may hold values from -0.15625 to 0.15625
- amplitudes: bfloat16 [512, 512, 512], P(None, 'row', 'col'), may hold values from -0.01171875 to 0.01171875
Outputs:
- ladder: float32 [512, 4, 512], P('col', None, 'row')
All inputs are finite; a program needn't handle non-finite values.
Results may differ from a plain program's by a relative error of at most 0.0029.
Values may be sent and summed in bfloat16 or wider, within the bound.
No kernel may reach another device: no remote copies, remote signals or barrier semaphores. Data moves between devices by JAX's collectives and lax.ppermute only.
A program may use at most 64 MiB of HBM per device.

v0:
```python
import jax
import jax.numpy as jnp
from jax import lax
from jax.sharding import PartitionSpec as P


def build_slab(window_piece, local_rows, depth_count, virt_count):
    window_count, orbital_rows, aux_count = window_piece.shape
    product = lax.dot_general(
        window_piece.reshape(window_count * orbital_rows, aux_count),
        local_rows,
        (((1,), (1,)), ((), ())),
        preferred_element_type=jnp.float32,
    )
    return product.astype(jnp.bfloat16).reshape(window_count, orbital_rows, depth_count, virt_count)


def per_device(window_factors, factors, amplitudes):
    depth_count, virt_count, aux_total = factors.shape
    local_rows = factors.reshape(depth_count * virt_count, aux_total)
    window_count = window_factors.shape[0]
    full_aux = lax.all_gather(window_factors, "row", axis=2, tiled=True)
    integrals = build_slab(
        lax.all_gather(full_aux, "col", axis=1, tiled=True), local_rows, depth_count, virt_count
    )
    regrouped = lax.all_to_all(integrals, "row", split_axis=1, concat_axis=3, tiled=True)
    pair_count = amplitudes.shape[0]
    flat_amps = amplitudes.reshape(pair_count, -1)
    flat_slab = regrouped.reshape(window_count, -1, regrouped.shape[3])
    by_virtual = lax.psum_scatter(
        jnp.einsum("ik,akb->iab", flat_amps, flat_slab, preferred_element_type=jnp.float32),
        "row",
        scatter_dimension=2,
        tiled=True,
    )
    return lax.psum_scatter(by_virtual, "col", scatter_dimension=0, tiled=True)


def solution(mesh):
    return jax.shard_map(
        per_device,
        mesh=mesh,
        in_specs=(P(None, "col", "row"), P("col", "row", None), P(None, "row", "col")),
        out_specs=P("col", None, "row"),
        check_vma=False,
    )
```

profile of v0, /device:TPU:1, one launch (start us, length us, event | category | flops | bytes accessed | tf_op | source)
XLA Modules:
  0.0 544.9 jit_solution(15161252252403851855)
XLA Ops:
  6.5 0.0 copy-start
  6.5 0.0 all-gather.2.cloned.1.call-start
  6.5 1.0 copy.22
  7.5 83.2 %all_gather.6 = bf16[4,64,1536]{1,0,2:T(4,128)(2,1)} all-gather(bf16[4,64,48]{1,0,2:T(4,128)(2,1)S(1)} %copy.22), channel_id=1, replica_groups=mesh['row'=32,'col'=8] {'row'}, dimensions={2}, use_global_device_ids=true | all-gather | bytes 811008 | tf_op jit(solution)/shard_map/all_gather | solution.py:22
  90.7 3.4 copy.23
  94.1 0.0 all-gather.2.cloned.1.call-update
  94.2 0.0 reduce-scatter.5.cloned.1.call-start
  94.2 81.1 %all-gather.2.cloned.1.call-done = bf16[4,512,1536]{2,1,0:T(8,128)(2,1)} async-done(((bf16[4,64,1536]{2,1,0:T(8,128)(2,1)}), bf16[4,512,1536]{2,1,0:T(8,128)(2,1)}) %all-gather.2.cloned.1.call-update) | async-done | bytes 6291472 | tf_op jit(solution)/shard_map/all_gather | solution.py:24
  175.3 0.0 copy-done
  175.3 11.2 %convolution_convert_fusion = bf16[2048,1024]{1,0:T(8,128)(2,1)} fusion(bf16[2048,1536]{1,0:T(8,128)(2,1)} %bitcast.29, bf16[1024,1536]{1,0:T(8,128)(2,1)S(1)} %bitcast.25), kind=kOutput, calls=%fused_computation | convolution fusion | flops 6444548096 | bytes 13631488 | tf_op jit(solution)/shard_map/dot_general | solution.py:9
  186.5 6.5 %copy.24 = bf16[2048,1024]{0,1:T(8,128)(2,1)} copy(bf16[2048,1024]{1,0:T(8,128)(2,1)} %convolution_convert_fusion) | data formatting | bytes 8388608 | tf_op jit(solution)/shard_map/convert_element_type | solution.py:15
  193.0 7.9 %reshape.18 = bf16[4,512,64,16]{1,0,3,2:T(4,128)(2,1)} reshape(bf16[2048,1024]{0,1:T(8,128)(2,1)} %copy.24) | data formatting | bytes 8388608 | tf_op jit(solution)/shard_map/reshape | solution.py:15
  200.9 15.8 %copy.25 = bf16[4,512,64,16]{2,3,0,1:T(8,128)(2,1)} copy(bf16[4,512,64,16]{1,0,3,2:T(4,128)(2,1)} %reshape.18) | data formatting | bytes 8388608 | tf_op jit(solution)/shard_map/reshape | solution.py:15
  216.6 13.9 %reshape.24 = bf16[32,2,32768]{2,1,0:T(2,128)(2,1)} reshape(bf16[512,4,16,64]{3,2,1,0:T(8,128)(2,1)} %bitcast.26) | data formatting | bytes 8388608
  230.5 56.7 %all_to_all.15 = bf16[32,2,32768]{2,1,0:T(2,128)(2,1)} all-to-all(bf16[32,2,32768]{2,1,0:T(2,128)(2,1)} %reshape.24), channel_id=1, replica_groups=mesh['row'=32,'col'=8] {'row'}, dimensions={0} | all-to-all | bytes 8388608 | tf_op jit(solution)/shard_map/all_to_all | solution.py:26
  287.2 13.7 %reshape.25 = bf16[512,4,16,64]{3,2,1,0:T(8,128)(2,1)} reshape(bf16[32,2,32768]{2,1,0:T(2,128)(2,1)} %all_to_all.15) | data formatting | bytes 8388608
  300.9 16.3 %copy.27 = bf16[4,16,64,32,16]{2,1,4,3,0:T(8,128)(2,1)} copy(bf16[4,16,64,32,16]{2,4,0,1,3:T(8,128)(2,1)} %bitcast.27) | data formatting | bytes 8388608 | tf_op jit(solution)/shard_map/all_to_all | solution.py:26
  317.2 11.9 %reshape.19 = bf16[4,1024,512]{1,2,0:T(8,128)(2,1)} reshape(bf16[4,16,64,32,16]{2,1,4,3,0:T(8,128)(2,1)} %copy.27) | data formatting | bytes 8388608 | tf_op jit(solution)/shard_map/reshape | solution.py:29
  329.1 0.0 copy-start.1
  329.1 7.0 %convolution_bitcast_fusion = f32[512,4,512]{0,2,1:T(8,128)} fusion(bf16[4,1024,512]{1,2,0:T(8,128)(2,1)} %reshape.19, bf16[512,1024,1]{0,1,2:T(8,128)(2,1)} %bitcast.30), kind=kOutput, calls=%fused_computation.1 | convolution fusion | flops 2147483648 | bytes 9437184 | tf_op jit(solution)/shard_map/ik,akb->iab/dot_general | solution.py:31
  336.0 0.0 reduce-scatter.5.cloned.1.call-update
  336.0 0.0 reduce-scatter.7.cloned.1.call-start
  336.1 143.8 %reduce-scatter.5.cloned.1.call-done = f32[512,4,16]{0,2,1:T(8,128)} async-done(((f32[512,4,512]{0,2,1:T(8,128)}), f32[512,4,16]{0,2,1:T(8,128)}) %reduce-scatter.5.cloned.1.call-update) | async-done | bytes 131088 | tf_op jit(solution)/shard_map/reduce_scatter | solution.py:30
  479.9 1.7 copy.34
  481.6 0.0 reduce-scatter.7.cloned.1.call-update
  481.6 55.3 %reduce-scatter.7.cloned.1.call-done = f32[64,64]{1,0:T(8,128)} async-done(((f32[512,64]{1,0:T(8,128)}), f32[64,64]{1,0:T(8,128)}) %reduce-scatter.7.cloned.1.call-update) | async-done | bytes 16400
  536.9 1.5 copy.35
  538.4 0.0 copy-done.1
Async XLA Ops:
  6.5 168.8 %copy-start = (bf16[64,16,1536]{2,1,0:T(8,128)(2,1)S(1)}, bf16[64,16,1536]{2,1,0:T(8,128)(2,1)}, u32[]{:S(2)}) copy-start(bf16[64,16,1536]{2,1,0:T(8,128)(2,1)} %param.4) | copy-start | bytes 9437188
  6.5 168.8 %all-gather.2.cloned.1.call-start = ((), (), s32[]{:S(2)}) async-start(), calls=%async_computation.3 | async-start | bytes 7077888 | tf_op jit(solution)/shard_map/all_gather | solution.py:24
  94.2 385.7 %reduce-scatter.5.cloned.1.call-start = ((), (), s32[]{:S(2)}) async-start(), calls=%async_computation.4 | async-start | bytes 4325376 | tf_op jit(solution)/shard_map/reduce_scatter | solution.py:30
  329.1 209.3 %copy-start.1 = (bf16[64,16,1536]{2,1,0:T(8,128)(2,1)S(1)}, bf16[64,16,1536]{2,1,0:T(8,128)(2,1)}, u32[]{:S(2)}) copy-start(bf16[64,16,1536]{2,1,0:T(8,128)(2,1)} %param.4) | copy-start | bytes 9437188
  336.0 200.9 %reduce-scatter.7.cloned.1.call-start = ((), (), s32[]{:S(2)}) async-start(), calls=%async_computation.5 | async-start | bytes 294912
Sparse Core Ops, SparseCore 0:
  94.3 81.0 all-gather.1
  336.2 143.6 reduce-scatter.4
  482.4 54.5 reduce-scatter.6
where the time goes:
time: 547 us; the launch traced here: 545 us
  waiting for transfers between devices  280 us (51%)
  blocking collectives  140 us (26%)
  local copies, waits for them, and re-layouts  93.4 us (17%)
  matrix products  18.1 us (3%)
  between operations  13.1 us (2%)
    reduce_scatter x1, waiting for transfers between devices, per_device(): lax.psum_scatter(jnp.einsum('ik,akb->iab', flat_amps, flat_slab, preferre...  144 us
    all_gather x1, blocking collectives, per_device(): full_aux = lax.all_gather(window_factors, 'row', axis=2, tiled=True)  83.2 us
    all_gather x1, waiting for transfers between devices, per_device(): lax.all_gather(full_aux, 'col', axis=1, tiled=True)  81.1 us
    all_to_all x1, blocking collectives, per_device(): lax.all_to_all(integrals, 'row', split_axis=1, concat_axis=3, tiled=True)  56.7 us
    unnamed x4, waiting for transfers between devices  55.3 us
    unnamed x9, local copies, waits for them, and re-layouts  31.7 us
    reshape x2, local copies, waits for them, and re-layouts, build_slab(): product.astype(jnp.bfloat16)  23.6 us
    all_to_all x1, local copies, waits for them, and re-layouts, per_device(): lax.all_to_all(integrals, 'row', split_axis=1, concat_axis=3, tiled=True)  16.3 us
  transfers between devices with their start and end apart: 3, of which 3 were waited for; matrix products, arithmetic and copies ran while one was open for 0% of the time, Pallas kernels for 0%

commit v1 on v0

v1 whole, which is shorter than its diff:
```python
import jax
import jax.numpy as jnp
from jax import lax
from jax.experimental import pallas as pl
from jax.experimental.pallas import tpu as pltpu
from jax.sharding import PartitionSpec as P

BF16 = jnp.bfloat16
F32 = jnp.float32


def dot(left, right):
    return lax.dot_general(left, right, (((1,), (0,)), ((), ())), preferred_element_type=F32)


def regroup_kernel(amps_ref, out_ref):
    rows, step = amps_ref.shape[0], out_ref.shape[0]
    c_count = 16
    d_count = rows // c_count
    first = pl.program_id(0) * step
    dest = lax.broadcasted_iota(jnp.int32, (step, rows), 0) + first
    src = lax.broadcasted_iota(jnp.int32, (step, rows), 1)
    wanted = (dest % c_count) * d_count + dest // c_count
    select = jnp.where(src == wanted, 1.0, 0.0).astype(BF16)
    out_ref[...] = dot(select, amps_ref[...]).astype(BF16)


def regroup(amps):
    rows, pairs = amps.shape
    step = 256
    return pl.pallas_call(
        regroup_kernel,
        out_shape=jax.ShapeDtypeStruct((rows, pairs), BF16),
        grid=(rows // step,),
        in_specs=[pl.BlockSpec((rows, pairs), lambda g: (0, 0))],
        out_specs=pl.BlockSpec((step, pairs), lambda g: (g, 0)),
        name="regroup_amplitudes",
    )(amps)


def ladder_kernel(own_f, other_f, own_t, other_t, w_ref, out_ref, total):
    g = pl.program_id(0)
    last = pl.num_programs(0) - 1
    half = pl.num_programs(0) // 2

    @pl.when(g == 0)
    def _():
        total[...] = jnp.zeros_like(total)

    def step(f_ref, t_ref):
        factors = f_ref[...].reshape(512, 1536)
        amps = t_ref[...].reshape(512, 512)
        for a in range(2):
            window = w_ref[:, a].reshape(1536, 512)
            integrals = dot(factors, window).astype(BF16)
            total[a] += dot(integrals, amps)

    @pl.when(g < half)
    def _():
        step(own_f, own_t)

    @pl.when(g >= half)
    def _():
        step(other_f, other_t)

    @pl.when(g == last)
    def _():
        for a in range(2):
            out_ref[:, a] = total[a].reshape(32, 16, 512).astype(BF16)


def ladder_part(own_f, other_f, own_t, other_t, window):
    def early(g):
        return (0, jnp.minimum(g, 1), 0, 0)

    def late(g):
        return (0, jnp.maximum(g - 2, 0), 0, 0)

    return pl.pallas_call(
        ladder_kernel,
        out_shape=jax.ShapeDtypeStruct((32, 2, 16, 512), BF16),
        grid=(4,),
        in_specs=[
            pl.BlockSpec((32, 1, 16, 1536), early),
            pl.BlockSpec((32, 1, 16, 1536), late),
            pl.BlockSpec((32, 1, 16, 512), early),
            pl.BlockSpec((32, 1, 16, 512), late),
            pl.BlockSpec((32, 2, 48, 512), lambda g: (0, 0, 0, 0)),
        ],
        out_specs=pl.BlockSpec((32, 2, 16, 512), lambda g: (0, 0, 0, 0)),
        scratch_shapes=[pltpu.VMEM((2, 512, 512), F32)],
        compiler_params=pltpu.CompilerParams(vmem_limit_bytes=48 * 1024 * 1024),
        cost_estimate=pl.CostEstimate(flops=8_600_000_000, bytes_accessed=13_000_000, transcendentals=0),
        name="ladder_part",
    )(own_f, other_f, own_t, other_t, window)


def sum_kernel(parts_ref, out_ref):
    out_ref[...] = jnp.sum(parts_ref[...].astype(F32), axis=0)


def sum_parts(parts):
    return pl.pallas_call(
        sum_kernel,
        out_shape=jax.ShapeDtypeStruct(parts.shape[1:], F32),
        name="sum_parts",
    )(parts)


def exchange(x, axis):
    return lax.all_to_all(x, axis, split_axis=0, concat_axis=0, tiled=True)


SWAP = [(q, q ^ 1) for q in range(8)]


def per_device(window_factors, factors, amplitudes):
    core = lax.axis_index("col") & 1
    window = jnp.transpose(window_factors, (0, 2, 1))
    window = lax.all_gather(window, "col", axis=0, tiled=False)
    window = lax.dynamic_slice_in_dim(window, core * 2, 2, axis=1)
    window = jnp.transpose(window, (1, 2, 0, 3)).reshape(2, 48, 512)
    window = exchange(jnp.broadcast_to(window[None], (32, 2, 48, 512)), "row")

    amps = jnp.transpose(amplitudes, (1, 2, 0)).reshape(1024, 512)
    own_t = exchange(regroup(amps).reshape(32, 2, 16, 512), "row")
    own_f = exchange(factors.reshape(32, 2, 16, 1536), "row")
    other_t = lax.ppermute(own_t, "col", SWAP)
    other_f = lax.ppermute(own_f, "col", SWAP)

    part = ladder_part(own_f, other_f, own_t, other_t, window)
    part = sum_parts(exchange(part, "row"))
    part = jnp.transpose(part.reshape(2, 16, 8, 64), (2, 0, 1, 3))
    part = exchange(part, "col")
    out = jnp.sum(part.reshape(4, 4, 16, 64), axis=0)
    return jnp.transpose(out, (2, 0, 1))


def solution(mesh):
    return jax.shard_map(
        per_device,
        mesh=mesh,
        in_specs=(P(None, "col", "row"), P("col", "row", None), P(None, "row", "col")),
        out_specs=P("col", None, "row"),
        check_vma=False,
    )
```

time: 547 us -> 197 us (0.36)
  waiting for transfers between devices: 280 us -> 41 us
  local copies, waits for them, and re-layouts: 93.4 us -> 3.96 us
  blocking collectives: 140 us -> 115 us
  Pallas kernels: 0 us -> 18.7 us
  matrix products: 18.1 us -> 0 us
  starting transfers between devices: 0.09 us -> 16.3 us
  between operations: 13.1 us -> 0.09 us
    reduce_scatter x1 -> x0, waiting for transfers between devices: 144 us -> none  [per_device(): lax.psum_scatter(jnp.einsum('ik,akb->iab', flat_amps, flat_slab, preferre...]
    all_gather x1 -> x0, waiting for transfers between devices: 81.1 us -> none  [per_device(): lax.all_gather(full_aux, 'col', axis=1, tiled=True)]
    unnamed x4 -> x0, waiting for transfers between devices: 55.3 us -> none
    reshape x3 -> x2, local copies, waits for them, and re-layouts: 35.5 us -> 0.95 us  [per_device(): part = jnp.transpose(part.reshape(2, 16, 8, 64), (2, 0, 1, 3))]
    all_to_all x0 -> x2, waiting for transfers between devices: none -> 34.3 us  [exchange(): return lax.all_to_all(x, axis, split_axis=0, concat_axis=0, tiled=True)]
    unnamed x9 -> x4, local copies, waits for them, and re-layouts: 31.7 us -> 0.21 us
    all_gather x1, blocking collectives: 83.2 us -> 53.4 us  [per_device(): window = lax.all_gather(window, 'col', axis=0, tiled=False)]
    pallas_call x0 -> x3, Pallas kernels: none -> 18.7 us  [the longest x1 12.7 us: ladder_part(): pl.pallas_call(ladder_kernel, out_shape=jax.ShapeDtypeStruct((32, 2, 16,...]
  transfers between devices with their start and end apart: 3 -> 4, of which waited for: 3 -> 2; matrix products, arithmetic and copies ran while one was open for 0% -> 0% of each run, Pallas kernels for 0% -> 0%
where the time goes in v1:
time: 197 us
  blocking collectives  115 us (58%)
  waiting for transfers between devices  41 us (21%)
  Pallas kernels  18.7 us (9%)
  starting transfers between devices  16.3 us (8%)
  local copies, waits for them, and re-layouts  3.96 us (2%)
    all_to_all x3, blocking collectives, exchange(): return lax.all_to_all(x, axis, split_axis=0, concat_axis=0, tiled=True)  61.8 us
    all_gather x1, blocking collectives, per_device(): window = lax.all_gather(window, 'col', axis=0, tiled=False)  53.4 us
    all_to_all x2, waiting for transfers between devices, exchange(): return lax.all_to_all(x, axis, split_axis=0, concat_axis=0, tiled=True)  34.3 us
    all_to_all x2, starting transfers between devices, exchange(): return lax.all_to_all(x, axis, split_axis=0, concat_axis=0, tiled=True)  15.7 us
    pallas_call x1, Pallas kernels, ladder_part(): pl.pallas_call(ladder_kernel, out_shape=jax.ShapeDtypeStruct((32, 2, 16,...  12.7 us
    ppermute x1, waiting for transfers between devices, per_device(): other_t = lax.ppermute(own_t, 'col', SWAP)  6.61 us
    pallas_call x1, Pallas kernels, regroup(): pl.pallas_call(regroup_kernel, out_shape=jax.ShapeDtypeStruct((rows, pair...  4.03 us
  transfers between devices with their start and end apart: 4, of which 2 were waited for; matrix products, arithmetic and copies ran while one was open for 0% of the time, Pallas kernels for 0%

profile of v1, /device:TPU:1, one launch (start us, length us, event | category | flops | bytes accessed | tf_op | source)
XLA Modules:
  0.0 196.7 jit_solution(11249952473857580193)
XLA Ops:
  0.0 4.0 %regroup_amplitudes.1 = bf16[1024,512]{1,0:T(8,128)(2,1)} custom-call(bf16[1024,512]{1,0:T(8,128)(2,1)} %bitcast.20), custom_call_target="tpu_custom_call" | custom-call | tf_op jit(solution)/shard_map/regroup_amplitudes/pallas_call | solution.py:31
  4.0 24.7 %all_to_all.25.own_t = bf16[32,2,16,512]{3,2,1,0:T(8,128)(2,1)S(1)} all-to-all(bf16[32,2,16,512]{3,2,1,0:T(8,128)(2,1)} %bitcast.18), channel_id=1, replica_groups=mesh['row'=32,'col'=8] {'row'}, dimensions={0} | all-to-all | bytes 2097152 | tf_op jit(solution)/shard_map/all_to_all | solution.py:111
  28.8 0.0 copy-start
  28.8 6.1 %all-to-all-start = ((bf16[32,2,16,1536]{3,2,1,0:T(8,128)(2,1)}), bf16[32,2,16,1536]{3,2,1,0:T(8,128)(2,1)}, u32[]{:S(2)}, u32[]{:S(2)}) async-start(bf16[32,2,16,1536]{3,2,1,0:T(8,128)(2,1)} %bitcast.19), calls=%async_computation | async-start | bytes 6291456 | tf_op jit(solution)/shard_map/all_to_all | solution.py:111
  34.9 0.0 copy-done
  34.9 53.4 %all-gather = bf16[32,48,64]{2,1,0:T(8,128)(2,1)S(1)} all-gather(bf16[4,48,64]{2,1,0:T(8,128)(2,1)S(1)} %bitcast.24), channel_id=2, replica_groups=mesh['row'=32,'col'=8] {'col'}, dimensions={0}, use_global_device_ids=true | all-gather | bytes 221184 | tf_op jit(solution)/shard_map/all_gather | solution.py:120
  88.3 0.1 copy.7
  88.4 0.2 broadcast_in_dim.7
  88.6 0.0 all-to-all-done.own_f
  88.6 2.0 %broadcast_in_dim.8 = bf16[32,2,48,512]{3,2,1,0:T(8,128)(2,1)} broadcast(bf16[2,48,512]{2,1,0:T(8,128)(2,1)S(1)} %broadcast_in_dim.7), dimensions={1,2,3} | broadcast | bytes 3244032 | tf_op jit(solution)/shard_map/broadcast_in_dim | solution.py:123
  90.6 9.6 %all-to-all-start.2 = ((bf16[32,2,48,512]{3,2,1,0:T(8,128)(2,1)}), bf16[32,2,48,512]{3,2,1,0:T(8,128)(2,1)}, u32[]{:S(2)}, u32[]{:S(2)}) async-start(bf16[32,2,48,512]{3,2,1,0:T(8,128)(2,1)} %broadcast_in_dim.8), calls=%async_computation.2 | async-start | bytes 6291456 | tf_op jit(solution)/shard_map/all_to_all | solution.py:111
  100.2 0.5 collective-permute-start
  100.8 0.1 collective-permute-start.1
  100.9 6.6 %collective-permute-done.1.other_t = bf16[32,2,16,512]{3,2,1,0:T(8,128)(2,1)S(1)} collective-permute-done((bf16[32,2,16,512]{3,2,1,0:T(8,128)(2,1)S(1)}, bf16[32,2,16,512]{3,2,1,0:T(8,128)(2,1)S(1)}, u32[]{:S(2)}, u32[]{:S(2)}) %collective-permute-start.1) | collective-permute-done | bytes 1048608 | tf_op jit(solution)/shard_map/ppermute | solution.py:128
  107.5 34.3 %all-to-all-done.2.w_ref = bf16[32,2,48,512]{3,2,1,0:T(8,128)(2,1)} async-done(((bf16[32,2,48,512]{3,2,1,0:T(8,128)(2,1)}), bf16[32,2,48,512]{3,2,1,0:T(8,128)(2,1)}, u32[]{:S(2)}, u32[]{:S(2)}) %all-to-all-start.2) | async-done | bytes 3145760 | tf_op jit(solution)/shard_map/all_to_all | solution.py:111
  141.8 0.0 collective-permute-done.other_f
  141.8 12.7 %ladder_part.1 = bf16[32,2,16,512]{3,2,1,0:T(8,128)(2,1)S(1)} custom-call(bf16[32,2,16,1536]{3,2,1,0:T(8,128)(2,1)} %all-to-all-done.own_f, bf16[32,2,16,1536]{3,2,1,0:T(8,128)(2,1)} %collective-permute-done.other_f, bf16[32,2,16,512]{3,2,1,0:T(8,128)(2,1)S(1)} %all_to_all.25.own_t, bf16[32,2,16,512]{3,2,1,0:T(8,128)(2,1)S(1)} %collective-permute-done.1.other_t, ...), custom_call_target="tpu_custom_call" | custom-call | flops 8600000512 | bytes 13000000 | tf_op jit(solution)/shard_map/ladder_part/pallas_call | solution.py:79
  154.5 22.9 %all_to_all.26.parts_ref = bf16[32,2,16,512]{3,2,1,0:T(8,128)(2,1)} all-to-all(bf16[32,2,16,512]{3,2,1,0:T(8,128)(2,1)S(1)} %ladder_part.1), channel_id=1, replica_groups=mesh['row'=32,'col'=8] {'row'}, dimensions={0} | all-to-all | bytes 2097152 | tf_op jit(solution)/shard_map/all_to_all | solution.py:111
  177.4 2.0 %sum_parts.1 = f32[2,16,512]{2,1,0:T(8,128)} custom-call(bf16[32,2,16,512]{3,2,1,0:T(8,128)(2,1)} %all_to_all.26.parts_ref), custom_call_target="tpu_custom_call" | custom-call | tf_op jit(solution)/shard_map/sum_parts/pallas_call | solution.py:103
  179.4 0.9 reshape.19
  180.4 0.1 reshape.22
  180.5 14.2 %all_to_all.27 = f32[8,1,2048]{2,1,0:T(1,128)S(1)} all-to-all(f32[8,1,2048]{2,1,0:T(1,128)S(1)} %reshape.22), channel_id=1, replica_groups=mesh['row'=32,'col'=8] {'col'}, dimensions={0} | all-to-all | bytes 131072 | tf_op jit(solution)/shard_map/all_to_all | solution.py:111
  194.7 0.5 broadcast
  195.2 0.8 reduce
  196.0 0.1 reshape.23
  196.1 0.6 bitcast_reduce_fusion
  (2 shorter events, 0.0 us)
Async XLA Ops:
  28.8 6.1 %copy-start = (bf16[4,64,48]{1,2,0:T(8,128)(2,1)S(1)}, bf16[4,64,48]{1,2,0:T(8,128)(2,1)}, u32[]{:S(2)}) copy-start(bf16[4,64,48]{1,2,0:T(8,128)(2,1)} %param.3) | copy-start | bytes 73732
  28.8 59.8 %all-to-all-start = ((bf16[32,2,16,1536]{3,2,1,0:T(8,128)(2,1)}), bf16[32,2,16,1536]{3,2,1,0:T(8,128)(2,1)}, u32[]{:S(2)}, u32[]{:S(2)}) async-start(bf16[32,2,16,1536]{3,2,1,0:T(8,128)(2,1)} %bitcast.19), calls=%async_computation | async-start | bytes 6291456 | tf_op jit(solution)/shard_map/all_to_all | solution.py:111
  90.6 51.2 %all-to-all-start.2 = ((bf16[32,2,48,512]{3,2,1,0:T(8,128)(2,1)}), bf16[32,2,48,512]{3,2,1,0:T(8,128)(2,1)}, u32[]{:S(2)}, u32[]{:S(2)}) async-start(bf16[32,2,48,512]{3,2,1,0:T(8,128)(2,1)} %broadcast_in_dim.8), calls=%async_computation.2 | async-start | bytes 6291456 | tf_op jit(solution)/shard_map/all_to_all | solution.py:111
  100.2 41.6 %collective-permute-start = (bf16[32,2,16,1536]{3,2,1,0:T(8,128)(2,1)}, bf16[32,2,16,1536]{3,2,1,0:T(8,128)(2,1)}, u32[]{:S(2)}, u32[]{:S(2)}) collective-permute-start(bf16[32,2,16,1536]{3,2,1,0:T(8,128)(2,1)} %all-to-all-done.own_f), channel_id=1, source_target_pairs={{0,1},{1,0},{2,3},{3,2},{4,5},{5,4},{6,7},{7,6},{8,9},{9,8},{10,11... | collective-permute-start | bytes 9437192 | tf_op jit(solution)/shard_map/ppermute | solution.py:129
  100.8 6.7 %collective-permute-start.1 = (bf16[32,2,16,512]{3,2,1,0:T(8,128)(2,1)S(1)}, bf16[32,2,16,512]{3,2,1,0:T(8,128)(2,1)S(1)}, u32[]{:S(2)}, u32[]{:S(2)}) collective-permute-start(bf16[32,2,16,512]{3,2,1,0:T(8,128)(2,1)S(1)} %all_to_all.25.own_t), channel_id=1, source_target_pairs={{0,1},{1,0},{2,3},{3,2},{4,5},{5,4},{6,7},{7,6},{8,9},{9,8},{10,11... | collective-permute-start | bytes 3145736 | tf_op jit(solution)/shard_map/ppermute | solution.py:128

commit v2 on v1

v2 whole, which is shorter than its diff:
```python
import jax
import jax.numpy as jnp
from jax import lax
from jax.experimental import pallas as pl
from jax.experimental.pallas import tpu as pltpu
from jax.sharding import Mesh
from jax.sharding import PartitionSpec as P

BF16 = jnp.bfloat16
F32 = jnp.float32
PLANE = ("y", "x")
MIB = 1024 * 1024


def dot(left, right):
    return lax.dot_general(left, right, (((1,), (0,)), ((), ())), preferred_element_type=F32)


def regroup_kernel(amps_ref, out_ref):
    rows, step = amps_ref.shape[0], out_ref.shape[0]
    c_count = 16
    d_count = rows // c_count
    first = pl.program_id(0) * step
    dest = lax.broadcasted_iota(jnp.int32, (step, rows), 0) + first
    src = lax.broadcasted_iota(jnp.int32, (step, rows), 1)
    wanted = (dest % c_count) * d_count + dest // c_count
    select = jnp.where(src == wanted, 1.0, 0.0).astype(BF16)
    out_ref[...] = dot(select, amps_ref[...]).astype(BF16)


def regroup(amps):
    rows, pairs = amps.shape
    step = 256
    return pl.pallas_call(
        regroup_kernel,
        out_shape=jax.ShapeDtypeStruct((rows, pairs), BF16),
        grid=(rows // step,),
        in_specs=[pl.BlockSpec((rows, pairs), lambda g: (0, 0))],
        out_specs=pl.BlockSpec((step, pairs), lambda g: (g, 0)),
        name="regroup_amplitudes",
    )(amps)


def ladder_kernel(f_ref, own_t, far_t, own_w, far_w, *rest):
    start, (out_ref, window, amps, total) = rest[:-4], rest[-4:]
    g = pl.program_id(0)
    zl = lax.axis_index("zl")

    @pl.when(g == 0)
    def _():
        for y in range(4):
            for ref, side in ((own_w, zl), (far_w, 1 - zl)):
                at = pl.multiple_of((2 * y + side) * 192, 192)
                for a in range(2):
                    window[a, pl.ds(at, 192)] = ref[4 * y : 4 * y + 4, a].reshape(192, 512)
        if start:
            total[...] = start[0][...]
        else:
            total[...] = jnp.zeros_like(total)

    for y in range(4):
        for ref, side in ((own_t, zl), (far_t, 1 - zl)):
            at = pl.multiple_of((2 * y + side) * 64, 64)
            for d in range(2):
                amps[d, pl.ds(at, 64)] = ref[4 * y : 4 * y + 4, d].reshape(64, 512)
    factors = f_ref[...].reshape(512, 1536)
    for a in range(2):
        integrals = dot(factors, window[a]).astype(BF16).reshape(16, 2, 16, 512)
        for d in range(2):
            total[a] += dot(integrals[:, d].reshape(256, 512), amps[d])

    @pl.when(g == pl.num_programs(0) - 1)
    def _():
        if start:
            for a in range(2):
                out_ref[:, a] = total[a].reshape(16, 16, 512).astype(BF16)
        else:
            out_ref[...] = total[...]


def ladder_part(factors, own_t, far_t, own_w, far_w, *start):
    def pair(g):
        return (0, g, 0, 0)

    def whole(g):
        return (0, 0, 0, 0)

    out_shape = (16, 2, 16, 512) if start else (2, 256, 512)
    return pl.pallas_call(
        ladder_kernel,
        out_shape=jax.ShapeDtypeStruct(out_shape, BF16 if start else F32),
        grid=(2,),
        in_specs=[
            pl.BlockSpec((16, 2, 16, 1536), pair),
            pl.BlockSpec((16, 2, 16, 512), pair),
            pl.BlockSpec((16, 2, 16, 512), pair),
            pl.BlockSpec((16, 2, 48, 512), whole),
            pl.BlockSpec((16, 2, 48, 512), whole),
        ]
        + [pl.BlockSpec((2, 256, 512), lambda g: (0, 0, 0)) for _ in start],
        out_specs=pl.BlockSpec(out_shape, lambda g: (0,) * len(out_shape)),
        scratch_shapes=[
            pltpu.VMEM((2, 1536, 512), BF16),
            pltpu.VMEM((2, 512, 512), BF16),
            pltpu.VMEM((2, 256, 512), F32),
        ],
        compiler_params=pltpu.CompilerParams(vmem_limit_bytes=40 * MIB),
        cost_estimate=pl.CostEstimate(flops=43_000_000_000, bytes_accessed=9_000_000, transcendentals=0),
        name="ladder_part",
    )(factors, own_t, far_t, own_w, far_w, *start)


def sum_kernel(parts_ref, out_ref):
    out_ref[...] = jnp.sum(parts_ref[...].astype(F32), axis=0)


def sum_parts(parts):
    return pl.pallas_call(
        sum_kernel,
        out_shape=jax.ShapeDtypeStruct(parts.shape[1:], F32),
        name="sum_parts",
    )(parts)


def exchange(x, axis):
    return lax.all_to_all(x, axis, split_axis=0, concat_axis=0, tiled=True)


def other(x, axis):
    return lax.ppermute(x, axis, [(0, 1), (1, 0)])


def per_device(window_factors, factors, amplitudes):
    core = lax.axis_index("core")
    amps = jnp.transpose(amplitudes, (1, 2, 0)).reshape(1024, 512)
    own_t = exchange(regroup(amps).reshape(16, 4, 16, 512), PLANE)
    far_t = other(own_t, "zl")

    window = jnp.transpose(window_factors, (0, 2, 1))
    window = lax.all_gather(window, ("zh", "core"), axis=0, tiled=False)
    window = lax.dynamic_slice_in_dim(window, core * 2, 2, axis=1)
    window = jnp.transpose(window, (1, 2, 0, 3)).reshape(2, 48, 512)
    window, _ = lax.optimization_barrier((window, own_t))
    own_w = exchange(jnp.broadcast_to(window[None], (16, 2, 48, 512)), PLANE)
    far_w = other(own_w, "zl")

    factors, _, far_t = lax.optimization_barrier((factors, own_w, far_t))
    own_f = exchange(factors.reshape(16, 4, 16, 1536), PLANE)
    part = ladder_part(own_f, own_t, far_t, own_w, far_w)
    part = ladder_part(other(own_f, "core"), other(own_t, "core"), other(far_t, "core"), own_w, far_w, part)

    part = sum_parts(exchange(part, PLANE))
    part = jnp.transpose(part.reshape(2, 16, 8, 64), (2, 0, 1, 3))
    part = exchange(part, ("zh", "core"))
    out = jnp.sum(part.reshape(4, 4, 16, 64), axis=0)
    return jnp.transpose(out, (2, 0, 1))


def solution(mesh):
    fine = Mesh(mesh.devices.reshape(4, 2, 4, 4, 2), ("y", "zl", "x", "zh", "core"))
    row, col = ("y", "zl", "x"), ("zh", "core")
    return jax.shard_map(
        per_device,
        mesh=fine,
        in_specs=(P(None, col, row), P(col, row, None), P(None, row, col)),
        out_specs=P(col, None, row),
        check_vma=False,
    )
```

time: 197 us -> 168 us (0.85)
  blocking collectives: 115 us -> 46.9 us
  waiting for transfers between devices: 41 us -> 64.5 us
  starting transfers between devices: 16.3 us -> 27.3 us
  local copies, waits for them, and re-layouts: 3.96 us -> 7.19 us
    all_gather x1, blocking collectives: 53.4 us -> 19.2 us  [per_device(): window = lax.all_gather(window, ('zh', 'core'), axis=0, tiled=False)]
    all_to_all x3 -> x2, blocking collectives: 61.8 us -> 27.7 us  [exchange(): return lax.all_to_all(x, axis, split_axis=0, concat_axis=0, tiled=True)]
    ppermute x2 -> x5, waiting for transfers between devices: 6.61 us -> 23.7 us  [other(): return lax.ppermute(x, axis, [(0, 1), (1, 0)])]
    all_to_all x2 -> x3, waiting for transfers between devices: 34.3 us -> 40.9 us  [exchange(): return lax.all_to_all(x, axis, split_axis=0, concat_axis=0, tiled=True)]
    ppermute x2 -> x5, starting transfers between devices: 0.63 us -> 6.89 us  [other(): return lax.ppermute(x, axis, [(0, 1), (1, 0)])]
    all_to_all x2 -> x3, starting transfers between devices: 15.7 us -> 20.4 us  [exchange(): return lax.all_to_all(x, axis, split_axis=0, concat_axis=0, tiled=True)]
    unnamed x4 -> x14, local copies, waits for them, and re-layouts: 0.21 us -> 4 us
    pallas_call x1 -> x2, Pallas kernels: 12.7 us -> 14.2 us  [ladder_part(): pl.pallas_call(ladder_kernel, out_shape=jax.ShapeDtypeStruct(out_shape, B...]
  transfers between devices with their start and end apart: 4 -> 8, of which waited for: 2 -> 3; matrix products, arithmetic and copies ran while one was open for 0% -> 0% of each run, Pallas kernels for 0% -> 4%
where the time goes in v2:
time: 168 us
  waiting for transfers between devices  64.5 us (38%)
  blocking collectives  46.9 us (28%)
  starting transfers between devices  27.3 us (16%)
  Pallas kernels  20 us (12%)
  local copies, waits for them, and re-layouts  7.19 us (4%)
    all_to_all x3, waiting for transfers between devices, exchange(): return lax.all_to_all(x, axis, split_axis=0, concat_axis=0, tiled=True)  40.9 us
    all_to_all x2, blocking collectives, exchange(): return lax.all_to_all(x, axis, split_axis=0, concat_axis=0, tiled=True)  27.7 us
    ppermute x5, waiting for transfers between devices, other(): return lax.ppermute(x, axis, [(0, 1), (1, 0)])  23.7 us
    all_to_all x3, starting transfers between devices, exchange(): return lax.all_to_all(x, axis, split_axis=0, concat_axis=0, tiled=True)  20.4 us
    all_gather x1, blocking collectives, per_device(): window = lax.all_gather(window, ('zh', 'core'), axis=0, tiled=False)  19.2 us
    pallas_call x2, Pallas kernels, ladder_part(): pl.pallas_call(ladder_kernel, out_shape=jax.ShapeDtypeStruct(out_shape, B...  14.2 us
    ppermute x5, starting transfers between devices, other(): return lax.ppermute(x, axis, [(0, 1), (1, 0)])  6.89 us
    pallas_call x1, Pallas kernels, regroup(): pl.pallas_call(regroup_kernel, out_shape=jax.ShapeDtypeStruct((rows, pair...  4.05 us
  transfers between devices with their start and end apart: 8, of which 3 were waited for; matrix products, arithmetic and copies ran while one was open for 0% of the time, Pallas kernels for 4%

profile of v2, /device:TPU:1, one launch (start us, length us, event | category | flops | bytes accessed | tf_op | source)
XLA Modules:
  0.0 167.5 jit_solution(15466031367630964451)
XLA Ops:
  0.0 0.0 copy-start.5
  0.0 4.1 %regroup_amplitudes.1 = bf16[1024,512]{1,0:T(8,128)(2,1)} custom-call(bf16[1024,512]{1,0:T(8,128)(2,1)} %bitcast.20), custom_call_target="tpu_custom_call" | custom-call | tf_op jit(solution)/shard_map/regroup_amplitudes/pallas_call | solution.py:34
  4.1 7.6 %all-to-all-start = ((bf16[16,4,16,512]{3,2,1,0:T(8,128)(2,1)}), bf16[16,4,16,512]{3,2,1,0:T(8,128)(2,1)S(1)}, u32[]{:S(2)}, u32[]{:S(2)}) async-start(bf16[16,4,16,512]{3,2,1,0:T(8,128)(2,1)} %bitcast.18), calls=%async_computation | async-start | bytes 2097152 | tf_op jit(solution)/shard_map/all_to_all | solution.py:126
  11.6 0.0 copy-done.5
  11.7 19.2 %all-gather = bf16[32,48,64]{2,1,0:T(8,128)(2,1)S(1)} all-gather(bf16[4,48,64]{2,1,0:T(8,128)(2,1)S(1)} %bitcast.24), channel_id=2, replica_groups=mesh['y'=4,'zl'=2,'x'=4,'zh'=4,'core'=2] {'zh','core'}, dimensions={0}, use_global_device_ids=true | all-gather | bytes 221184 | tf_op jit(solution)/shard_map/all_gather | solution.py:140
  30.9 0.1 copy.7
  31.0 0.2 reshape.19
  31.2 0.0 all-to-all-done.own_t
  31.2 0.0 copy-start.3
  31.2 1.5 broadcast_in_dim.2
  32.6 6.9 %all-to-all-start.1 = ((bf16[16,2,48,512]{3,2,1,0:T(8,128)(2,1)}), bf16[16,2,48,512]{3,2,1,0:T(8,128)(2,1)S(1)}, u32[]{:S(2)}, u32[]{:S(2)}) async-start(bf16[16,2,48,512]{3,2,1,0:T(8,128)(2,1)} %broadcast_in_dim.2), calls=%async_computation.1 | async-start | bytes 3145728 | tf_op jit(solution)/shard_map/all_to_all | solution.py:126
  39.6 0.8 collective-permute-start
  40.4 23.6 %collective-permute-done.far_t = bf16[16,4,16,512]{3,2,1,0:T(8,128)(2,1)} collective-permute-done((bf16[16,4,16,512]{3,2,1,0:T(8,128)(2,1)S(1)}, bf16[16,4,16,512]{3,2,1,0:T(8,128)(2,1)}, u32[]{:S(2)}, u32[]{:S(2)}) %collective-permute-start) | collective-permute-done | bytes 1048608 | tf_op jit(solution)/shard_map/ppermute | solution.py:130
  64.0 0.4 all-to-all-done.1.own_w
  64.4 0.0 copy-start
  64.4 0.0 copy-done.3
  64.4 1.1 copy-done
  65.5 5.9 %all-to-all-start.2 = ((bf16[16,4,16,1536]{3,2,1,0:T(8,128)(2,1)}), bf16[16,4,16,1536]{3,2,1,0:T(8,128)(2,1)S(1)}, u32[]{:S(2)}, u32[]{:S(2)}) async-start(bf16[16,4,16,1536]{3,2,1,0:T(8,128)(2,1)} %bitcast.19), calls=%async_computation.2 | async-start | bytes 6291456 | tf_op jit(solution)/shard_map/all_to_all | solution.py:126
  71.5 0.8 collective-permute-start.4
  72.3 2.2 %collective-permute-start.2 = (bf16[16,4,16,512]{3,2,1,0:T(8,128)(2,1)}, bf16[16,4,16,512]{3,2,1,0:T(8,128)(2,1)}, u32[]{:S(2)}, u32[]{:S(2)}) collective-permute-start(bf16[16,4,16,512]{3,2,1,0:T(8,128)(2,1)} %copy-done.3), channel_id=1, source_target_pairs={{0,1},{1,0},{2,3},{3,2},{4,5},{5,4},{6,7},{7,6},{8,9},{9,8},{10,11... | collective-permute-start | bytes 3145736 | tf_op jit(solution)/shard_map/ppermute | solution.py:130
  74.5 0.0 collective-permute-start.3
  74.5 40.5 %all-to-all-done.2.f_ref = bf16[16,4,16,1536]{3,2,1,0:T(8,128)(2,1)S(1)} async-done(((bf16[16,4,16,1536]{3,2,1,0:T(8,128)(2,1)}), bf16[16,4,16,1536]{3,2,1,0:T(8,128)(2,1)S(1)}, u32[]{:S(2)}, u32[]{:S(2)}) %all-to-all-start.2) | async-done | bytes 3145760 | tf_op jit(solution)/shard_map/all_to_all | solution.py:126
  115.0 3.1 %collective-permute-start.1 = (bf16[16,4,16,1536]{3,2,1,0:T(8,128)(2,1)S(1)}, bf16[16,4,16,1536]{3,2,1,0:T(8,128)(2,1)S(1)}, u32[]{:S(2)}, u32[]{:S(2)}) collective-permute-start(bf16[16,4,16,1536]{3,2,1,0:T(8,128)(2,1)S(1)} %all-to-all-done.2.f_ref), channel_id=1, source_target_pairs={{0,1},{1,0},{2,3},{3,2},{4,5},{5,4},{6,7},{7,6},{8,9},{9,8},{10,11... | collective-permute-start | bytes 9437192 | tf_op jit(solution)/shard_map/ppermute | solution.py:130
  118.0 0.0 collective-permute-done.4.far_w
  118.0 0.0 copy-start.1
  118.0 1.4 copy-done.1
  119.4 0.0 copy-start.4
  119.4 1.2 copy-done.4
  120.7 0.0 copy-start.2
  120.7 7.1 %ladder_part.2.rest_0_ = f32[2,256,512]{2,1,0:T(8,128)S(1)} custom-call(bf16[16,4,16,1536]{3,2,1,0:T(8,128)(2,1)S(1)} %all-to-all-done.2.f_ref, bf16[16,4,16,512]{3,2,1,0:T(8,128)(2,1)S(1)} %copy-done.4, bf16[16,4,16,512]{3,2,1,0:T(8,128)(2,1)} %collective-permute-done.far_t, bf16[16,2,48,512]{3,2,1,0:T(8,128)(2,1)S(1)} %copy-done.1, ...), custom_call_target="tpu_custom_call" | custom-call | flops 43000000512 | bytes 9000000 | tf_op jit(solution)/shard_map/ladder_part/pallas_call | solution.py:89
  127.8 0.0 collective-permute-done.2.own_t
  127.8 0.0 collective-permute-done.3.far_t
  127.8 0.0 collective-permute-done.1.f_ref
  127.8 0.0 copy-done.2
  127.8 7.2 %ladder_part.3 = bf16[16,2,16,512]{3,2,1,0:T(8,128)(2,1)S(1)} custom-call(bf16[16,4,16,1536]{3,2,1,0:T(8,128)(2,1)S(1)} %collective-permute-done.1.f_ref, bf16[16,4,16,512]{3,2,1,0:T(8,128)(2,1)} %collective-permute-done.2.own_t, bf16[16,4,16,512]{3,2,1,0:T(8,128)(2,1)} %collective-permute-done.3.far_t, bf16[16,2,48,512]{3,2,1,0:T(8,128)(2,1)S(1)} %copy-done.2, ...), custom_call_target="tpu_custom_call" | custom-call | flops 43000000512 | bytes 9000000 | tf_op jit(solution)/shard_map/ladder_part/pallas_call | solution.py:89
  135.0 14.7 %all_to_all.25.parts_ref = bf16[16,2,16,512]{3,2,1,0:T(8,128)(2,1)} all-to-all(bf16[16,2,16,512]{3,2,1,0:T(8,128)(2,1)S(1)} %ladder_part.3), channel_id=1, replica_groups=mesh['y'=4,'zl'=2,'x'=4,'zh'=4,'core'=2] {'y','x'}, dimensions={0} | all-to-all | bytes 1048576 | tf_op jit(solution)/shard_map/all_to_all | solution.py:126
  149.7 1.7 %sum_parts.1 = f32[2,16,512]{2,1,0:T(8,128)} custom-call(bf16[16,2,16,512]{3,2,1,0:T(8,128)(2,1)} %all_to_all.25.parts_ref), custom_call_target="tpu_custom_call" | custom-call | tf_op jit(solution)/shard_map/sum_parts/pallas_call | solution.py:118
  151.4 0.9 reshape.23
  152.4 0.1 reshape.26
  152.5 13.0 %all_to_all.26 = f32[8,1,2048]{2,1,0:T(1,128)S(1)} all-to-all(f32[8,1,2048]{2,1,0:T(1,128)S(1)} %reshape.26), channel_id=1, replica_groups=mesh['y'=4,'zl'=2,'x'=4,'zh'=4,'core'=2] {'zh','core'}, dimensions={0} | all-to-all | bytes 131072 | tf_op jit(solution)/shard_map/all_to_all | solution.py:126
  165.5 0.5 broadcast.1
  166.0 0.8 reduce
  166.8 0.1 reshape.27
  166.9 0.6 bitcast_reduce_fusion
  (2 shorter events, 0.0 us)
Async XLA Ops:
  0.0 11.6 %copy-start.5 = (bf16[4,64,48]{1,2,0:T(8,128)(2,1)S(1)}, bf16[4,64,48]{1,2,0:T(8,128)(2,1)}, u32[]{:S(2)}) copy-start(bf16[4,64,48]{1,2,0:T(8,128)(2,1)} %param.3) | copy-start | bytes 73732
  4.1 27.1 %all-to-all-start = ((bf16[16,4,16,512]{3,2,1,0:T(8,128)(2,1)}), bf16[16,4,16,512]{3,2,1,0:T(8,128)(2,1)S(1)}, u32[]{:S(2)}, u32[]{:S(2)}) async-start(bf16[16,4,16,512]{3,2,1,0:T(8,128)(2,1)} %bitcast.18), calls=%async_computation | async-start | bytes 2097152 | tf_op jit(solution)/shard_map/all_to_all | solution.py:126
  31.2 33.2 %copy-start.3 = (bf16[16,4,16,512]{3,2,1,0:T(8,128)(2,1)}, bf16[16,4,16,512]{3,2,1,0:T(8,128)(2,1)S(1)}, u32[]{:S(2)}) copy-start(bf16[16,4,16,512]{3,2,1,0:T(8,128)(2,1)S(1)} %all-to-all-done.own_t) | copy-start | bytes 3145732
  32.6 31.7 %all-to-all-start.1 = ((bf16[16,2,48,512]{3,2,1,0:T(8,128)(2,1)}), bf16[16,2,48,512]{3,2,1,0:T(8,128)(2,1)S(1)}, u32[]{:S(2)}, u32[]{:S(2)}) async-start(bf16[16,2,48,512]{3,2,1,0:T(8,128)(2,1)} %broadcast_in_dim.2), calls=%async_computation.1 | async-start | bytes 3145728 | tf_op jit(solution)/shard_map/all_to_all | solution.py:126
  39.6 24.5 %collective-permute-start = (bf16[16,4,16,512]{3,2,1,0:T(8,128)(2,1)S(1)}, bf16[16,4,16,512]{3,2,1,0:T(8,128)(2,1)}, u32[]{:S(2)}, u32[]{:S(2)}) collective-permute-start(bf16[16,4,16,512]{3,2,1,0:T(8,128)(2,1)S(1)} %all-to-all-done.own_t), channel_id=1, source_target_pairs={{0,32},{32,0},{1,33},{33,1},{2,34},{34,2},{3,35},{35,3},{4,36},{36... | collective-permute-start | bytes 3145736 | tf_op jit(solution)/shard_map/ppermute | solution.py:130
  64.4 1.2 copy-start
  65.5 49.4 %all-to-all-start.2 = ((bf16[16,4,16,1536]{3,2,1,0:T(8,128)(2,1)}), bf16[16,4,16,1536]{3,2,1,0:T(8,128)(2,1)S(1)}, u32[]{:S(2)}, u32[]{:S(2)}) async-start(bf16[16,4,16,1536]{3,2,1,0:T(8,128)(2,1)} %bitcast.19), calls=%async_computation.2 | async-start | bytes 6291456 | tf_op jit(solution)/shard_map/all_to_all | solution.py:126
  71.5 46.6 %collective-permute-start.4 = (bf16[16,2,48,512]{3,2,1,0:T(8,128)(2,1)}, bf16[16,2,48,512]{3,2,1,0:T(8,128)(2,1)}, u32[]{:S(2)}, u32[]{:S(2)}) collective-permute-start(bf16[16,2,48,512]{3,2,1,0:T(8,128)(2,1)} %copy-done), channel_id=1, source_target_pairs={{0,32},{32,0},{1,33},{33,1},{2,34},{34,2},{3,35},{35,3},{4,36},{36... | collective-permute-start | bytes 4718600 | tf_op jit(solution)/shard_map/ppermute | solution.py:130
  72.3 55.5 %collective-permute-start.2 = (bf16[16,4,16,512]{3,2,1,0:T(8,128)(2,1)}, bf16[16,4,16,512]{3,2,1,0:T(8,128)(2,1)}, u32[]{:S(2)}, u32[]{:S(2)}) collective-permute-start(bf16[16,4,16,512]{3,2,1,0:T(8,128)(2,1)} %copy-done.3), channel_id=1, source_target_pairs={{0,1},{1,0},{2,3},{3,2},{4,5},{5,4},{6,7},{7,6},{8,9},{9,8},{10,11... | collective-permute-start | bytes 3145736 | tf_op jit(solution)/shard_map/ppermute | solution.py:130
  74.5 53.3 %collective-permute-start.3 = (bf16[16,4,16,512]{3,2,1,0:T(8,128)(2,1)}, bf16[16,4,16,512]{3,2,1,0:T(8,128)(2,1)}, u32[]{:S(2)}, u32[]{:S(2)}) collective-permute-start(bf16[16,4,16,512]{3,2,1,0:T(8,128)(2,1)} %collective-permute-done.far_t), channel_id=1, source_target_pairs={{0,1},{1,0},{2,3},{3,2},{4,5},{5,4},{6,7},{7,6},{8,9},{9,8},{10,11... | collective-permute-start | bytes 3145736 | tf_op jit(solution)/shard_map/ppermute | solution.py:130
  115.0 12.8 %collective-permute-start.1 = (bf16[16,4,16,1536]{3,2,1,0:T(8,128)(2,1)S(1)}, bf16[16,4,16,1536]{3,2,1,0:T(8,128)(2,1)S(1)}, u32[]{:S(2)}, u32[]{:S(2)}) collective-permute-start(bf16[16,4,16,1536]{3,2,1,0:T(8,128)(2,1)S(1)} %all-to-all-done.2.f_ref), channel_id=1, source_target_pairs={{0,1},{1,0},{2,3},{3,2},{4,5},{5,4},{6,7},{7,6},{8,9},{9,8},{10,11... | collective-permute-start | bytes 9437192 | tf_op jit(solution)/shard_map/ppermute | solution.py:130
  118.0 1.4 copy-start.1
  119.4 1.2 copy-start.4
  120.7 7.1 %copy-start.2 = (bf16[16,2,48,512]{3,2,1,0:T(8,128)(2,1)S(1)}, bf16[16,2,48,512]{3,2,1,0:T(8,128)(2,1)}, u32[]{:S(2)}) copy-start(bf16[16,2,48,512]{3,2,1,0:T(8,128)(2,1)} %copy-done) | copy-start | bytes 4718596

commit v3 on v0

v3 whole, which is shorter than its diff:
```python
import jax
import jax.numpy as jnp
from jax import lax
from jax.experimental import pallas as pl
from jax.experimental.pallas import tpu as pltpu
from jax.sharding import Mesh
from jax.sharding import PartitionSpec as P

BF16 = jnp.bfloat16
F32 = jnp.float32
PLANE = ("y", "x")
ROW = ("y", "zl", "x")
RING = ("zl", "zh")
MIB = 1024 * 1024


def in_hbm(*arrays):
    return [pltpu.with_memory_space_constraint(a, pltpu.HBM) for a in arrays]


def dot(left, right):
    return lax.dot_general(left, right, (((1,), (0,)), ((), ())), preferred_element_type=F32)


def spread_kernel(own_ref, far_ref, out_ref):
    core = lax.axis_index("core")
    for a in range(2):
        mine, theirs = own_ref[2 * core + a], far_ref[2 * core + a]
        first = jnp.where(core == 0, mine, theirs)
        second = jnp.where(core == 0, theirs, mine)
        block = jnp.concatenate([first, second], axis=-1)
        for s in range(16):
            out_ref[s, a] = block


def spread(own, far):
    return pl.pallas_call(
        spread_kernel,
        out_shape=jax.ShapeDtypeStruct((16, 2, 48, 128), BF16),
        name="spread_window",
    )(own, far)


def regroup_kernel(t_ref, out_ref):
    dest = lax.broadcasted_iota(jnp.int32, (256, 256), 0)
    src = lax.broadcasted_iota(jnp.int32, (256, 256), 1)
    select = jnp.where(src == (dest % 16) * 16 + dest // 16, 1.0, 0.0).astype(BF16)
    rows = dot(select, t_ref[...].reshape(256, 512)).astype(BF16).reshape(4, 4, 16, 512)
    out_ref[0:4] = rows
    out_ref[4:8] = rows


def regroup(amps):
    return pl.pallas_call(
        regroup_kernel,
        out_shape=jax.ShapeDtypeStruct((32, 4, 16, 512), BF16),
        grid=(4,),
        in_specs=[pl.BlockSpec((16, 16, 512), lambda g: (0, g, 0))],
        out_specs=pl.BlockSpec((8, 4, 16, 512), lambda g: (g, 0, 0, 0)),
        name="regroup_amplitudes",
    )(amps)


def integrals_kernel(own_f, far_f, *rest):
    blocks, (own_v, far_v, window) = rest[:-3], rest[-3:]
    g = pl.program_id(0)

    @pl.when(g == 0)
    def _():
        z = 2 * lax.axis_index("zh") + lax.axis_index("zl")
        for step, ref in zip((0, -1, 1, -2, 2, -3, 3, 4, 4), blocks):
            at = (z + step + 8) % 8
            row, lane = (at % 2) * 192, pl.multiple_of((at // 2) * 128, 128)
            count = ref.shape[0] // 4
            first = 2 if ref is blocks[8] else 0
            for y in range(count):
                rows = pl.ds(pl.multiple_of((y + first) * 384 + row, 192), 192)
                for a in range(2):
                    window[a, rows, pl.ds(lane, 128)] = ref[4 * y : 4 * y + 4, a].reshape(192, 128)

    def step(f_ref, out_ref):
        factors = f_ref[...].reshape(512, 1536)
        for a in range(2):
            integrals = dot(factors, window[a]).astype(BF16).reshape(16, 2, 16, 512)
            for d in range(2):
                out_ref[d, a] = integrals[:, d].reshape(256, 512)

    @pl.when(g < 2)
    def _():
        step(own_f, own_v)

    @pl.when(g >= 2)
    def _():
        step(far_f, far_v)


def build_integrals(own_f, far_f, blocks):
    return pl.pallas_call(
        integrals_kernel,
        out_shape=[pltpu.VMEM((4, 2, 256, 512), BF16)] * 2,
        grid=(4,),
        in_specs=[
            pl.BlockSpec((16, 2, 16, 1536), lambda g: (0, jnp.minimum(g, 1), 0, 0)),
            pl.BlockSpec((16, 2, 16, 1536), lambda g: (0, jnp.maximum(g - 2, 0), 0, 0)),
        ]
        + [pl.BlockSpec(b.shape, lambda g: (0, 0, 0, 0)) for b in blocks],
        out_specs=[
            pl.BlockSpec((2, 2, 256, 512), lambda g: (jnp.minimum(g, 1), 0, 0, 0)),
            pl.BlockSpec((2, 2, 256, 512), lambda g: (jnp.maximum(g - 2, 0), 0, 0, 0)),
        ],
        scratch_shapes=[pltpu.VMEM((2, 1536, 512), BF16)],
        compiler_params=pltpu.CompilerParams(vmem_limit_bytes=28 * MIB),
        cost_estimate=pl.CostEstimate(flops=6_500_000_000, bytes_accessed=14_000_000, transcendentals=0),
        name="build_integrals",
    )(own_f, far_f, *in_hbm(*blocks))


def ladder_kernel(t_ref, v_ref, *rest):
    start, out_ref = rest[:-1], rest[-1]
    for a in range(2):
        rows = slice(256 * a, 256 * a + 256)
        total = start[0][rows] if start else 0.0
        for d in range(4):
            total = total + dot(v_ref[d, a], t_ref[:, d].reshape(512, 512))
        if start:
            out_ref[:, a] = total.reshape(16, 16, 512).astype(BF16)
        else:
            out_ref[rows] = total


def ladder_part(*operands):
    out_shape = (16, 2, 16, 512) if len(operands) == 3 else (512, 512)
    return pl.pallas_call(
        ladder_kernel,
        out_shape=jax.ShapeDtypeStruct(out_shape, BF16 if len(operands) == 3 else F32),
        in_specs=[pl.BlockSpec(memory_space=pltpu.VMEM)] * len(operands),
        out_specs=pl.BlockSpec(memory_space=pltpu.VMEM),
        compiler_params=pltpu.CompilerParams(vmem_limit_bytes=16 * MIB),
        cost_estimate=pl.CostEstimate(flops=100_000_000_000, bytes_accessed=5_000_000, transcendentals=0),
        name="ladder_part",
    )(*operands)


def sum_kernel(parts_ref, out_ref):
    total = jnp.sum(parts_ref[...].astype(F32), axis=0)
    for q in range(8):
        lanes = slice(64 * q, 64 * q + 64)
        out_ref[q] = jnp.concatenate([total[0, :, lanes], total[1, :, lanes]], axis=-1)


def sum_parts(parts):
    return pl.pallas_call(
        sum_kernel,
        out_shape=jax.ShapeDtypeStruct((8, 16, 128), F32),
        name="sum_parts",
    )(parts)


def finish_kernel(parts_ref, out_ref):
    for core in range(2):
        both = parts_ref[core] + parts_ref[2 + core] + parts_ref[4 + core] + parts_ref[6 + core]
        out_ref[2 * core] = both[:, :64]
        out_ref[2 * core + 1] = both[:, 64:]


def finish(parts):
    return pl.pallas_call(
        finish_kernel,
        out_shape=jax.ShapeDtypeStruct((4, 16, 64), F32),
        name="finish",
    )(parts)


def exchange(x, axis):
    return lax.all_to_all(x, axis, split_axis=0, concat_axis=0, tiled=True)


def other(x, axis):
    return lax.ppermute(x, axis, [(0, 1), (1, 0)])


def shift(x, step):
    def flat(z):
        return (z % 2) * 4 + (z // 2) % 4

    return lax.ppermute(x, RING, [(flat(z), flat((z + step) % 8)) for z in range(8)])


def per_device(window_factors, factors, amplitudes):
    window = jnp.transpose(window_factors, (0, 2, 1))
    own_w = exchange(spread(window, other(window, "core")), PLANE)
    own_t = regroup(jnp.transpose(amplitudes, (1, 2, 0)))
    factors, own_w, own_t = lax.optimization_barrier((factors, own_w, own_t))
    own_f = exchange(factors.reshape(16, 4, 16, 1536), PLANE)

    blocks, up, down = [own_w], own_w, own_w
    for _ in range(3):
        up, down = shift(up, 1), shift(down, -1)
        blocks += [up, down]
    blocks += [shift(up[:8], 1), shift(down[8:], -1)]
    own_t, own_f, *blocks = lax.optimization_barrier((own_t, own_f, *blocks))
    amps = exchange(own_t, ROW)
    own_v, far_v = build_integrals(own_f, other(own_f, "core"), blocks)
    part = ladder_part(amps, own_v)
    part = ladder_part(other(amps, "core"), far_v, part)

    part = sum_parts(exchange(part, PLANE))
    return jnp.transpose(finish(exchange(part, ("zh", "core"))), (2, 0, 1))


def solution(mesh):
    fine = Mesh(mesh.devices.reshape(4, 2, 4, 4, 2), ("y", "zl", "x", "zh", "core"))
    row, col = ROW, ("zh", "core")
    return jax.shard_map(
        per_device,
        mesh=fine,
        in_specs=(P(None, col, row), P(col, row, None), P(None, row, col)),
        out_specs=P(col, None, row),
        check_vma=False,
    )
```

time: 547 us -> 148 us (0.27)
  waiting for transfers between devices: 280 us -> 46.8 us
  blocking collectives: 140 us -> 32.9 us
  local copies, waits for them, and re-layouts: 93.4 us -> 5.69 us
  starting transfers between devices: 0.09 us -> 38.2 us
  Pallas kernels: 0 us -> 23.4 us
  matrix products: 18.1 us -> 0 us
  between operations: 13.1 us -> 0.15 us
    reduce_scatter x1 -> x0, waiting for transfers between devices: 144 us -> none  [per_device(): lax.psum_scatter(jnp.einsum('ik,akb->iab', flat_amps, flat_slab, preferre...]
    all_gather x1 -> x0, blocking collectives: 83.2 us -> none  [per_device(): full_aux = lax.all_gather(window_factors, 'row', axis=2, tiled=True)]
    all_gather x1 -> x0, waiting for transfers between devices: 81.1 us -> none  [per_device(): lax.all_gather(full_aux, 'col', axis=1, tiled=True)]
    unnamed x4 -> x0, waiting for transfers between devices: 55.3 us -> none
    reshape x3 -> x0, local copies, waits for them, and re-layouts: 35.5 us -> none  [the longest x2 23.6 us: build_slab(): product.astype(jnp.bfloat16)]
    ppermute x0 -> x11, waiting for transfers between devices: none -> 30.5 us  [the longest x8 24.2 us: shift(): lax.ppermute(x, RING, [(flat(z), flat((z + step) % 8)) for z in range(8)])]
    unnamed x9 -> x26, local copies, waits for them, and re-layouts: 31.7 us -> 5.66 us
    ppermute x0 -> x11, starting transfers between devices: none -> 24.6 us  [the longest x8 13.9 us: shift(): lax.ppermute(x, RING, [(flat(z), flat((z + step) % 8)) for z in range(8)])]
  transfers between devices with their start and end apart: 3 -> 14, of which waited for: 3 -> 9; matrix products, arithmetic and copies ran while one was open for 0% -> 0% of each run, Pallas kernels for 0% -> 12%
where the time goes in v3:
time: 148 us; the launch traced here: 147 us
  waiting for transfers between devices  46.8 us (32%)
  starting transfers between devices  38.2 us (26%)
  blocking collectives  32.9 us (22%)
  Pallas kernels  23.4 us (16%)
  local copies, waits for them, and re-layouts  5.69 us (4%)
    all_to_all x2, blocking collectives, exchange(): return lax.all_to_all(x, axis, split_axis=0, concat_axis=0, tiled=True)  32.9 us
    ppermute x8, waiting for transfers between devices, shift(): lax.ppermute(x, RING, [(flat(z), flat((z + step) % 8)) for z in range(8)])  24.2 us
    all_to_all x3, waiting for transfers between devices, exchange(): return lax.all_to_all(x, axis, split_axis=0, concat_axis=0, tiled=True)  16.3 us
    ppermute x8, starting transfers between devices, shift(): lax.ppermute(x, RING, [(flat(z), flat((z + step) % 8)) for z in range(8)])  13.9 us
    all_to_all x3, starting transfers between devices, exchange(): return lax.all_to_all(x, axis, split_axis=0, concat_axis=0, tiled=True)  13.6 us
    ppermute x3, starting transfers between devices, other(): return lax.ppermute(x, axis, [(0, 1), (1, 0)])  10.7 us
    pallas_call x1, Pallas kernels, build_integrals(): pl.pallas_call(integrals_kernel, out_shape=[pltpu.VMEM((4, 2, 256, 512),...  10.1 us
    ppermute x3, waiting for transfers between devices, other(): return lax.ppermute(x, axis, [(0, 1), (1, 0)])  6.38 us
  transfers between devices with their start and end apart: 14, of which 9 were waited for; matrix products, arithmetic and copies ran while one was open for 0% of the time, Pallas kernels for 12%

profile of v3, /device:TPU:1, one launch (start us, length us, event | category | flops | bytes accessed | tf_op | source)
XLA Modules:
  0.0 147.2 jit_solution(995138866573811486)
XLA Ops:
  0.0 3.2 %collective-permute-start = (bf16[4,48,64]{2,1,0:T(8,128)(2,1)}, bf16[4,48,64]{2,1,0:T(8,128)(2,1)S(1)}, u32[]{:S(2)}, u32[]{:S(2)}) collective-permute-start(bf16[4,48,64]{2,1,0:T(8,128)(2,1)} %bitcast.6), channel_id=1, source_target_pairs={{0,1},{1,0},{2,3},{3,2},{4,5},{5,4},{6,7},{7,6},{8,9},{9,8},{10,11... | collective-permute-start | bytes 73736 | tf_op jit(solution)/shard_map/ppermute | solution.py:179
  3.2 1.1 collective-permute-done.far_ref
  4.3 0.6 copy-done.7
  4.9 1.7 %spread_window.1 = bf16[16,2,48,128]{3,2,1,0:T(8,128)(2,1)} custom-call(bf16[4,48,64]{2,1,0:T(8,128)(2,1)} %bitcast.7, bf16[4,48,64]{2,1,0:T(8,128)(2,1)} %copy-done.7), custom_call_target="tpu_custom_call" | custom-call | tf_op jit(solution)/shard_map/spread_window/pallas_call | solution.py:37
  6.6 5.0 %all-to-all-start = ((bf16[16,2,48,128]{3,2,1,0:T(8,128)(2,1)}), bf16[16,2,48,128]{3,2,1,0:T(8,128)(2,1)S(1)}, u32[]{:S(2)}, u32[]{:S(2)}) async-start(bf16[16,2,48,128]{3,2,1,0:T(8,128)(2,1)} %spread_window.1), calls=%async_computation | async-start | bytes 786432 | tf_op jit(solution)/shard_map/all_to_all | solution.py:175
  11.7 4.0 %regroup_amplitudes.1 = bf16[32,4,16,512]{3,2,1,0:T(8,128)(2,1)} custom-call(bf16[16,64,512]{2,1,0:T(8,128)(2,1)} %bitcast.5), custom_call_target="tpu_custom_call" | custom-call | tf_op jit(solution)/shard_map/regroup_amplitudes/pallas_call | solution.py:54
  15.7 5.5 %all-to-all-done.rest_0_ = bf16[16,2,48,128]{3,2,1,0:T(8,128)(2,1)S(1)} async-done(((bf16[16,2,48,128]{3,2,1,0:T(8,128)(2,1)}), bf16[16,2,48,128]{3,2,1,0:T(8,128)(2,1)S(1)}, u32[]{:S(2)}, u32[]{:S(2)}) %all-to-all-start) | async-done | bytes 393248 | tf_op jit(solution)/shard_map/all_to_all | solution.py:175
  21.2 3.7 %all-to-all-start.1 = ((bf16[16,4,16,1536]{3,2,1,0:T(8,128)(2,1)}), bf16[16,4,16,1536]{3,2,1,0:T(8,128)(2,1)S(1)}, u32[]{:S(2)}, u32[]{:S(2)}) async-start(bf16[16,4,16,1536]{3,2,1,0:T(8,128)(2,1)} %bitcast.4), calls=%async_computation.1 | async-start | bytes 6291456 | tf_op jit(solution)/shard_map/all_to_all | solution.py:175
  25.0 1.7 %collective-permute-start.1 = (bf16[16,2,48,128]{3,2,1,0:T(8,128)(2,1)S(1)}, bf16[16,2,48,128]{3,2,1,0:T(8,128)(2,1)S(1)}, u32[]{:S(2)}, u32[]{:S(2)}) collective-permute-start(bf16[16,2,48,128]{3,2,1,0:T(8,128)(2,1)S(1)} %all-to-all-done.rest_0_), channel_id=1, source_target_pairs={{0,32},{32,2},{2,34},{34,4},{4,36},{36,6},{6,38},{38,0},{1,33},{33... | collective-permute-start | bytes 1179656 | tf_op jit(solution)/shard_map/ppermute | solution.py:186
  26.7 0.0 copy-done.4
  26.7 4.0 %collective-permute-start.2 = (bf16[16,2,48,128]{3,2,1,0:T(8,128)(2,1)S(1)}, bf16[16,2,48,128]{3,2,1,0:T(8,128)(2,1)S(1)}, u32[]{:S(2)}, u32[]{:S(2)}) collective-permute-start(bf16[16,2,48,128]{3,2,1,0:T(8,128)(2,1)S(1)} %all-to-all-done.rest_0_), channel_id=1, source_target_pairs={{0,38},{32,0},{2,32},{34,2},{4,34},{36,4},{6,36},{38,6},{1,39},{33... | collective-permute-start | bytes 1179656 | tf_op jit(solution)/shard_map/ppermute | solution.py:186
  30.7 7.8 %collective-permute-done.1.rest_1_ = bf16[16,2,48,128]{3,2,1,0:T(8,128)(2,1)S(1)} collective-permute-done((bf16[16,2,48,128]{3,2,1,0:T(8,128)(2,1)S(1)}, bf16[16,2,48,128]{3,2,1,0:T(8,128)(2,1)S(1)}, u32[]{:S(2)}, u32[]{:S(2)}) %collective-permute-start.1) | collective-permute-done | bytes 393248 | tf_op jit(solution)/shard_map/ppermute | solution.py:186
  38.5 0.0 collective-permute-start.3
  38.6 0.0 collective-permute-done.2.rest_2_
  38.6 0.0 copy-start.9
  38.6 2.7 %collective-permute-start.4 = (bf16[16,2,48,128]{3,2,1,0:T(8,128)(2,1)S(1)}, bf16[16,2,48,128]{3,2,1,0:T(8,128)(2,1)S(1)}, u32[]{:S(2)}, u32[]{:S(2)}) collective-permute-start(bf16[16,2,48,128]{3,2,1,0:T(8,128)(2,1)S(1)} %collective-permute-done.2.rest_2_), channel_id=1, source_target_pairs={{0,38},{32,0},{2,32},{34,2},{4,34},{36,4},{6,36},{38,6},{1,39},{33... | collective-permute-start | bytes 1179656 | tf_op jit(solution)/shard_map/ppermute | solution.py:186
  41.2 7.0 %collective-permute-done.3.rest_3_ = bf16[16,2,48,128]{3,2,1,0:T(8,128)(2,1)S(1)} collective-permute-done((bf16[16,2,48,128]{3,2,1,0:T(8,128)(2,1)S(1)}, bf16[16,2,48,128]{3,2,1,0:T(8,128)(2,1)S(1)}, u32[]{:S(2)}, u32[]{:S(2)}) %collective-permute-start.3) | collective-permute-done | bytes 393248 | tf_op jit(solution)/shard_map/ppermute | solution.py:186
  48.2 0.0 collective-permute-start.5
  48.2 0.0 collective-permute-done.4.rest_4_
  48.2 0.0 copy-start.11
  48.2 2.7 %collective-permute-start.6 = (bf16[16,2,48,128]{3,2,1,0:T(8,128)(2,1)S(1)}, bf16[16,2,48,128]{3,2,1,0:T(8,128)(2,1)S(1)}, u32[]{:S(2)}, u32[]{:S(2)}) collective-permute-start(bf16[16,2,48,128]{3,2,1,0:T(8,128)(2,1)S(1)} %collective-permute-done.4.rest_4_), channel_id=1, source_target_pairs={{0,38},{32,0},{2,32},{34,2},{4,34},{36,4},{6,36},{38,6},{1,39},{33... | collective-permute-start | bytes 1179656 | tf_op jit(solution)/shard_map/ppermute | solution.py:186
  50.9 0.0 copy-done.8
  50.9 0.0 copy-done.9
  50.9 6.1 %collective-permute-done.5.rest_5_ = bf16[16,2,48,128]{3,2,1,0:T(8,128)(2,1)S(1)} collective-permute-done((bf16[16,2,48,128]{3,2,1,0:T(8,128)(2,1)S(1)}, bf16[16,2,48,128]{3,2,1,0:T(8,128)(2,1)S(1)}, u32[]{:S(2)}, u32[]{:S(2)}) %collective-permute-start.5) | collective-permute-done | bytes 393248 | tf_op jit(solution)/shard_map/ppermute | solution.py:186
  57.0 0.1 collective-permute-start.7
  57.1 0.0 collective-permute-done.6.rest_6_
  57.1 2.7 %collective-permute-start.8 = (bf16[8,2,48,128]{3,2,1,0:T(8,128)(2,1)S(1)}, bf16[8,2,48,128]{3,2,1,0:T(8,128)(2,1)}, u32[]{:S(2)}, u32[]{:S(2)}) collective-permute-start(bf16[8,2,48,128]{3,2,1,0:T(8,128)(2,1)S(1)} %slice.9), channel_id=1, source_target_pairs={{0,38},{32,0},{2,32},{34,2},{4,34},{36,4},{6,36},{38,6},{1,39},{33... | collective-permute-start | bytes 589832 | tf_op jit(solution)/shard_map/ppermute | solution.py:186
  59.9 3.2 %collective-permute-done.7.rest_7_ = bf16[8,2,48,128]{3,2,1,0:T(8,128)(2,1)S(1)} collective-permute-done((bf16[8,2,48,128]{3,2,1,0:T(8,128)(2,1)S(1)}, bf16[8,2,48,128]{3,2,1,0:T(8,128)(2,1)S(1)}, u32[]{:S(2)}, u32[]{:S(2)}) %collective-permute-start.7) | collective-permute-done | bytes 196640 | tf_op jit(solution)/shard_map/ppermute | solution.py:186
  63.1 0.7 copy-done.12
  63.8 0.0 collective-permute-done.8.rest_8_
  63.8 6.2 %all-to-all-done.1.own_f = bf16[16,4,16,1536]{3,2,1,0:T(8,128)(2,1)S(1)} async-done(((bf16[16,4,16,1536]{3,2,1,0:T(8,128)(2,1)}), bf16[16,4,16,1536]{3,2,1,0:T(8,128)(2,1)S(1)}, u32[]{:S(2)}, u32[]{:S(2)}) %all-to-all-start.1) | async-done | bytes 3145760 | tf_op jit(solution)/shard_map/all_to_all | solution.py:175
  70.0 0.0 copy-done.5
  70.0 4.9 %all-to-all-start.2 = ((bf16[32,4,16,512]{3,2,1,0:T(8,128)(2,1)}), bf16[32,4,16,512]{3,2,1,0:T(8,128)(2,1)}, u32[]{:S(2)}, u32[]{:S(2)}) async-start(bf16[32,4,16,512]{3,2,1,0:T(8,128)(2,1)} %regroup_amplitudes.1), calls=%async_computation.2 | async-start | bytes 4194304 | tf_op jit(solution)/shard_map/all_to_all | solution.py:175
  74.9 2.6 %collective-permute-start.10 = (bf16[16,4,16,1536]{3,2,1,0:T(8,128)(2,1)S(1)}, bf16[16,4,16,1536]{3,2,1,0:T(8,128)(2,1)S(1)}, u32[]{:S(2)}, u32[]{:S(2)}) collective-permute-start(bf16[16,4,16,1536]{3,2,1,0:T(8,128)(2,1)S(1)} %all-to-all-done.1.own_f), channel_id=1, source_target_pairs={{0,1},{1,0},{2,3},{3,2},{4,5},{5,4},{6,7},{7,6},{8,9},{9,8},{10,11... | collective-permute-start | bytes 9437192 | tf_op jit(solution)/shard_map/ppermute | solution.py:179
  77.5 5.3 %collective-permute-done.10.far_f = bf16[16,4,16,1536]{3,2,1,0:T(8,128)(2,1)S(1)} collective-permute-done((bf16[16,4,16,1536]{3,2,1,0:T(8,128)(2,1)S(1)}, bf16[16,4,16,1536]{3,2,1,0:T(8,128)(2,1)S(1)}, u32[]{:S(2)}, u32[]{:S(2)}) %collective-permute-start.10) | collective-permute-done | bytes 3145760 | tf_op jit(solution)/shard_map/ppermute | solution.py:179
  82.8 10.1 %build_integrals.1 = (bf16[4,2,256,512]{3,2,1,0:T(8,128)(2,1)S(1)}, bf16[4,2,256,512]{3,2,1,0:T(8,128)(2,1)S(1)}) custom-call(bf16[16,4,16,1536]{3,2,1,0:T(8,128)(2,1)S(1)} %all-to-all-done.1.own_f, bf16[16,4,16,1536]{3,2,1,0:T(8,128)(2,1)S(1)} %collective-permute-done.10.far_f, bf16[16,2,48,128]{3,2,1,0:T(8,128)(2,1)} %copy-done.4, ...), custom_call_target="tpu_custom_call" | custom-call | flops 6499999744 | bytes 14000000 | tf_op jit(solution)/shard_map/build_integrals/pallas_call | solution.py:98
  93.0 1.4 copy-done
  94.3 1.4 copy-done.2
  95.7 4.5 %all-to-all-done.2.t_ref = bf16[32,4,16,512]{3,2,1,0:T(8,128)(2,1)} async-done(((bf16[32,4,16,512]{3,2,1,0:T(8,128)(2,1)}), bf16[32,4,16,512]{3,2,1,0:T(8,128)(2,1)}, u32[]{:S(2)}, u32[]{:S(2)}) %all-to-all-start.2) | async-done | bytes 2097184 | tf_op jit(solution)/shard_map/all_to_all | solution.py:175
  100.2 4.8 %collective-permute-start.9 = (bf16[32,4,16,512]{3,2,1,0:T(8,128)(2,1)}, bf16[32,4,16,512]{3,2,1,0:T(8,128)(2,1)S(1)}, u32[]{:S(2)}, u32[]{:S(2)}) collective-permute-start(bf16[32,4,16,512]{3,2,1,0:T(8,128)(2,1)} %all-to-all-done.2.t_ref), channel_id=1, source_target_pairs={{0,1},{1,0},{2,3},{3,2},{4,5},{5,4},{6,7},{7,6},{8,9},{9,8},{10,11... | collective-permute-start | bytes 6291464 | tf_op jit(solution)/shard_map/ppermute | solution.py:179
  105.1 1.6 %copy-done.3 = bf16[4,2,256,512]{3,2,1,0:T(8,128)(2,1)S(1)} copy-done((bf16[4,2,256,512]{3,2,1,0:T(8,128)(2,1)S(1)}, bf16[4,2,256,512]{3,2,1,0:T(8,128)(2,1)}, u32[]{:S(2)}) %copy-start.3) | copy-done | bytes 2097176
  106.7 3.0 %ladder_part.2.rest_0_ = f32[512,512]{1,0:T(8,128)S(1)} custom-call(bf16[32,4,16,512]{3,2,1,0:T(8,128)(2,1)} %all-to-all-done.2.t_ref, bf16[4,2,256,512]{3,2,1,0:T(8,128)(2,1)S(1)} %copy-done.3), custom_call_target="tpu_custom_call" | custom-call | flops 99999997952 | bytes 5000000 | tf_op jit(solution)/shard_map/ladder_part/pallas_call | solution.py:133
  109.6 0.0 collective-permute-done.9.t_ref
  109.7 1.2 ladder_part.3
  110.9 15.3 %all_to_all.25.parts_ref = bf16[16,2,16,512]{3,2,1,0:T(8,128)(2,1)} all-to-all(bf16[16,2,16,512]{3,2,1,0:T(8,128)(2,1)S(1)} %ladder_part.3), channel_id=1, replica_groups=mesh['y'=4,'zl'=2,'x'=4,'zh'=4,'core'=2] {'y','x'}, dimensions={0} | all-to-all | bytes 1048576 | tf_op jit(solution)/shard_map/all_to_all | solution.py:175
  126.2 1.8 %sum_parts.1 = f32[8,16,128]{2,1,0:T(8,128)} custom-call(bf16[16,2,16,512]{3,2,1,0:T(8,128)(2,1)} %all_to_all.25.parts_ref), custom_call_target="tpu_custom_call" | custom-call | tf_op jit(solution)/shard_map/sum_parts/pallas_call | solution.py:152
  128.0 17.6 %all_to_all.26.parts_ref = f32[8,16,128]{2,1,0:T(8,128)} all-to-all(f32[8,16,128]{2,1,0:T(8,128)} %sum_parts.1), channel_id=1, replica_groups=mesh['y'=4,'zl'=2,'x'=4,'zh'=4,'core'=2] {'zh','core'}, dimensions={0} | all-to-all | bytes 131072 | tf_op jit(solution)/shard_map/all_to_all | solution.py:175
  145.7 1.5 %finish.1 = f32[4,16,64]{2,1,0:T(8,128)} custom-call(f32[8,16,128]{2,1,0:T(8,128)} %all_to_all.26.parts_ref), custom_call_target="tpu_custom_call" | custom-call | tf_op jit(solution)/shard_map/finish/pallas_call | solution.py:167
  (17 shorter events, 0.1 us)
Async XLA Ops:
  0.0 4.3 %collective-permute-start = (bf16[4,48,64]{2,1,0:T(8,128)(2,1)}, bf16[4,48,64]{2,1,0:T(8,128)(2,1)S(1)}, u32[]{:S(2)}, u32[]{:S(2)}) collective-permute-start(bf16[4,48,64]{2,1,0:T(8,128)(2,1)} %bitcast.6), channel_id=1, source_target_pairs={{0,1},{1,0},{2,3},{3,2},{4,5},{5,4},{6,7},{7,6},{8,9},{9,8},{10,11... | collective-permute-start | bytes 73736 | tf_op jit(solution)/shard_map/ppermute | solution.py:179
  4.3 0.6 copy-start.7
  6.6 14.6 %all-to-all-start = ((bf16[16,2,48,128]{3,2,1,0:T(8,128)(2,1)}), bf16[16,2,48,128]{3,2,1,0:T(8,128)(2,1)S(1)}, u32[]{:S(2)}, u32[]{:S(2)}) async-start(bf16[16,2,48,128]{3,2,1,0:T(8,128)(2,1)} %spread_window.1), calls=%async_computation | async-start | bytes 786432 | tf_op jit(solution)/shard_map/all_to_all | solution.py:175
  21.2 5.5 %copy-start.4 = (bf16[16,2,48,128]{3,2,1,0:T(8,128)(2,1)}, bf16[16,2,48,128]{3,2,1,0:T(8,128)(2,1)S(1)}, u32[]{:S(2)}) copy-start(bf16[16,2,48,128]{3,2,1,0:T(8,128)(2,1)S(1)} %all-to-all-done.rest_0_) | copy-start | bytes 1179652
  21.2 48.8 %all-to-all-start.1 = ((bf16[16,4,16,1536]{3,2,1,0:T(8,128)(2,1)}), bf16[16,4,16,1536]{3,2,1,0:T(8,128)(2,1)S(1)}, u32[]{:S(2)}, u32[]{:S(2)}) async-start(bf16[16,4,16,1536]{3,2,1,0:T(8,128)(2,1)} %bitcast.4), calls=%async_computation.1 | async-start | bytes 6291456 | tf_op jit(solution)/shard_map/all_to_all | solution.py:175
  25.0 13.6 %collective-permute-start.1 = (bf16[16,2,48,128]{3,2,1,0:T(8,128)(2,1)S(1)}, bf16[16,2,48,128]{3,2,1,0:T(8,128)(2,1)S(1)}, u32[]{:S(2)}, u32[]{:S(2)}) collective-permute-start(bf16[16,2,48,128]{3,2,1,0:T(8,128)(2,1)S(1)} %all-to-all-done.rest_0_), channel_id=1, source_target_pairs={{0,32},{32,2},{2,34},{34,4},{4,36},{36,6},{6,38},{38,0},{1,33},{33... | collective-permute-start | bytes 1179656 | tf_op jit(solution)/shard_map/ppermute | solution.py:186
  26.7 11.9 %collective-permute-start.2 = (bf16[16,2,48,128]{3,2,1,0:T(8,128)(2,1)S(1)}, bf16[16,2,48,128]{3,2,1,0:T(8,128)(2,1)S(1)}, u32[]{:S(2)}, u32[]{:S(2)}) collective-permute-start(bf16[16,2,48,128]{3,2,1,0:T(8,128)(2,1)S(1)} %all-to-all-done.rest_0_), channel_id=1, source_target_pairs={{0,38},{32,0},{2,32},{34,2},{4,34},{36,4},{6,36},{38,6},{1,39},{33... | collective-permute-start | bytes 1179656 | tf_op jit(solution)/shard_map/ppermute | solution.py:186
  38.5 12.4 %copy-start.8 = (bf16[16,2,48,128]{3,2,1,0:T(8,128)(2,1)}, bf16[16,2,48,128]{3,2,1,0:T(8,128)(2,1)S(1)}, u32[]{:S(2)}) copy-start(bf16[16,2,48,128]{3,2,1,0:T(8,128)(2,1)S(1)} %collective-permute-done.1.rest_1_) | copy-start | bytes 1179652
  38.5 9.7 %collective-permute-start.3 = (bf16[16,2,48,128]{3,2,1,0:T(8,128)(2,1)S(1)}, bf16[16,2,48,128]{3,2,1,0:T(8,128)(2,1)S(1)}, u32[]{:S(2)}, u32[]{:S(2)}) collective-permute-start(bf16[16,2,48,128]{3,2,1,0:T(8,128)(2,1)S(1)} %collective-permute-done.1.rest_1_), channel_id=1, source_target_pairs={{0,32},{32,2},{2,34},{34,4},{4,36},{36,6},{6,38},{38,0},{1,33},{33... | collective-permute-start | bytes 1179656 | tf_op jit(solution)/shard_map/ppermute | solution.py:186
  38.6 12.4 %copy-start.9 = (bf16[16,2,48,128]{3,2,1,0:T(8,128)(2,1)}, bf16[16,2,48,128]{3,2,1,0:T(8,128)(2,1)S(1)}, u32[]{:S(2)}) copy-start(bf16[16,2,48,128]{3,2,1,0:T(8,128)(2,1)S(1)} %collective-permute-done.2.rest_2_) | copy-start | bytes 1179652
  38.6 9.7 %collective-permute-start.4 = (bf16[16,2,48,128]{3,2,1,0:T(8,128)(2,1)S(1)}, bf16[16,2,48,128]{3,2,1,0:T(8,128)(2,1)S(1)}, u32[]{:S(2)}, u32[]{:S(2)}) collective-permute-start(bf16[16,2,48,128]{3,2,1,0:T(8,128)(2,1)S(1)} %collective-permute-done.2.rest_2_), channel_id=1, source_target_pairs={{0,38},{32,0},{2,32},{34,2},{4,34},{36,4},{6,36},{38,6},{1,39},{33... | collective-permute-start | bytes 1179656 | tf_op jit(solution)/shard_map/ppermute | solution.py:186
  48.2 2.7 %copy-start.10 = (bf16[16,2,48,128]{3,2,1,0:T(8,128)(2,1)}, bf16[16,2,48,128]{3,2,1,0:T(8,128)(2,1)S(1)}, u32[]{:S(2)}) copy-start(bf16[16,2,48,128]{3,2,1,0:T(8,128)(2,1)S(1)} %collective-permute-done.3.rest_3_) | copy-start | bytes 1179652
  48.2 8.8 %collective-permute-start.5 = (bf16[16,2,48,128]{3,2,1,0:T(8,128)(2,1)S(1)}, bf16[16,2,48,128]{3,2,1,0:T(8,128)(2,1)S(1)}, u32[]{:S(2)}, u32[]{:S(2)}) collective-permute-start(bf16[16,2,48,128]{3,2,1,0:T(8,128)(2,1)S(1)} %collective-permute-done.3.rest_3_), channel_id=1, source_target_pairs={{0,32},{32,2},{2,34},{34,4},{4,36},{36,6},{6,38},{38,0},{1,33},{33... | collective-permute-start | bytes 1179656 | tf_op jit(solution)/shard_map/ppermute | solution.py:186
  48.2 14.9 %copy-start.11 = (bf16[16,2,48,128]{3,2,1,0:T(8,128)(2,1)}, bf16[16,2,48,128]{3,2,1,0:T(8,128)(2,1)S(1)}, u32[]{:S(2)}) copy-start(bf16[16,2,48,128]{3,2,1,0:T(8,128)(2,1)S(1)} %collective-permute-done.4.rest_4_) | copy-start | bytes 1179652
  48.2 8.9 %collective-permute-start.6 = (bf16[16,2,48,128]{3,2,1,0:T(8,128)(2,1)S(1)}, bf16[16,2,48,128]{3,2,1,0:T(8,128)(2,1)S(1)}, u32[]{:S(2)}, u32[]{:S(2)}) collective-permute-start(bf16[16,2,48,128]{3,2,1,0:T(8,128)(2,1)S(1)} %collective-permute-done.4.rest_4_), channel_id=1, source_target_pairs={{0,38},{32,0},{2,32},{34,2},{4,34},{36,4},{6,36},{38,6},{1,39},{33... | collective-permute-start | bytes 1179656 | tf_op jit(solution)/shard_map/ppermute | solution.py:186
  57.0 13.1 %copy-start.5 = (bf16[16,2,48,128]{3,2,1,0:T(8,128)(2,1)}, bf16[16,2,48,128]{3,2,1,0:T(8,128)(2,1)S(1)}, u32[]{:S(2)}) copy-start(bf16[16,2,48,128]{3,2,1,0:T(8,128)(2,1)S(1)} %collective-permute-done.5.rest_5_) | copy-start | bytes 1179652
  57.0 6.1 %collective-permute-start.7 = (bf16[8,2,48,128]{3,2,1,0:T(8,128)(2,1)S(1)}, bf16[8,2,48,128]{3,2,1,0:T(8,128)(2,1)S(1)}, u32[]{:S(2)}, u32[]{:S(2)}) collective-permute-start(bf16[8,2,48,128]{3,2,1,0:T(8,128)(2,1)S(1)} %slice.8), channel_id=1, source_target_pairs={{0,32},{32,2},{2,34},{34,4},{4,36},{36,6},{6,38},{38,0},{1,33},{33... | collective-permute-start | bytes 589832 | tf_op jit(solution)/shard_map/ppermute | solution.py:186
  57.1 6.0 %copy-start.6 = (bf16[16,2,48,128]{3,2,1,0:T(8,128)(2,1)}, bf16[16,2,48,128]{3,2,1,0:T(8,128)(2,1)S(1)}, u32[]{:S(2)}) copy-start(bf16[16,2,48,128]{3,2,1,0:T(8,128)(2,1)S(1)} %collective-permute-done.6.rest_6_) | copy-start | bytes 1179652
  57.1 6.7 %collective-permute-start.8 = (bf16[8,2,48,128]{3,2,1,0:T(8,128)(2,1)S(1)}, bf16[8,2,48,128]{3,2,1,0:T(8,128)(2,1)}, u32[]{:S(2)}, u32[]{:S(2)}) collective-permute-start(bf16[8,2,48,128]{3,2,1,0:T(8,128)(2,1)S(1)} %slice.9), channel_id=1, source_target_pairs={{0,38},{32,0},{2,32},{34,2},{4,34},{36,4},{6,36},{38,6},{1,39},{33... | collective-permute-start | bytes 589832 | tf_op jit(solution)/shard_map/ppermute | solution.py:186
  63.1 0.7 copy-start.12
  70.0 30.2 %all-to-all-start.2 = ((bf16[32,4,16,512]{3,2,1,0:T(8,128)(2,1)}), bf16[32,4,16,512]{3,2,1,0:T(8,128)(2,1)}, u32[]{:S(2)}, u32[]{:S(2)}) async-start(bf16[32,4,16,512]{3,2,1,0:T(8,128)(2,1)} %regroup_amplitudes.1), calls=%async_computation.2 | async-start | bytes 4194304 | tf_op jit(solution)/shard_map/all_to_all | solution.py:175
  74.9 7.9 %collective-permute-start.10 = (bf16[16,4,16,1536]{3,2,1,0:T(8,128)(2,1)S(1)}, bf16[16,4,16,1536]{3,2,1,0:T(8,128)(2,1)S(1)}, u32[]{:S(2)}, u32[]{:S(2)}) collective-permute-start(bf16[16,4,16,1536]{3,2,1,0:T(8,128)(2,1)S(1)} %all-to-all-done.1.own_f), channel_id=1, source_target_pairs={{0,1},{1,0},{2,3},{3,2},{4,5},{5,4},{6,7},{7,6},{8,9},{9,8},{10,11... | collective-permute-start | bytes 9437192 | tf_op jit(solution)/shard_map/ppermute | solution.py:179
  93.0 1.4 copy-start
  94.3 1.4 copy-start.2
  100.2 9.4 %collective-permute-start.9 = (bf16[32,4,16,512]{3,2,1,0:T(8,128)(2,1)}, bf16[32,4,16,512]{3,2,1,0:T(8,128)(2,1)S(1)}, u32[]{:S(2)}, u32[]{:S(2)}) collective-permute-start(bf16[32,4,16,512]{3,2,1,0:T(8,128)(2,1)} %all-to-all-done.2.t_ref), channel_id=1, source_target_pairs={{0,1},{1,0},{2,3},{3,2},{4,5},{5,4},{6,7},{7,6},{8,9},{9,8},{10,11... | collective-permute-start | bytes 6291464 | tf_op jit(solution)/shard_map/ppermute | solution.py:179
  105.1 1.6 %copy-start.3 = (bf16[4,2,256,512]{3,2,1,0:T(8,128)(2,1)S(1)}, bf16[4,2,256,512]{3,2,1,0:T(8,128)(2,1)}, u32[]{:S(2)}) copy-start(bf16[4,2,256,512]{3,2,1,0:T(8,128)(2,1)} %copy-done.2) | copy-start | bytes 6291460
  106.7 3.0 %copy-start.1 = (bf16[4,2,256,512]{3,2,1,0:T(8,128)(2,1)S(1)}, bf16[4,2,256,512]{3,2,1,0:T(8,128)(2,1)}, u32[]{:S(2)}) copy-start(bf16[4,2,256,512]{3,2,1,0:T(8,128)(2,1)} %copy-done) | copy-start | bytes 6291460

commit v4 on v3

--- a/solution.py
+++ b/solution.py
@@ -8,7 +8,7 @@
 
 BF16 = jnp.bfloat16
 F32 = jnp.float32
-PLANE = ("y", "x")
+PLANE = ("x", "y")
 ROW = ("y", "zl", "x")
 RING = ("zl", "zh")
 MIB = 1024 * 1024
@@ -46,19 +46,19 @@
     src = lax.broadcasted_iota(jnp.int32, (256, 256), 1)
     select = jnp.where(src == (dest % 16) * 16 + dest // 16, 1.0, 0.0).astype(BF16)
     rows = dot(select, t_ref[...].reshape(256, 512)).astype(BF16).reshape(4, 4, 16, 512)
-    out_ref[0:4] = rows
-    out_ref[4:8] = rows
+    out_ref[:, 0, 0] = rows
+    out_ref[:, 1, 0] = rows
 
 
 def regroup(amps):
     return pl.pallas_call(
         regroup_kernel,
-        out_shape=jax.ShapeDtypeStruct((32, 4, 16, 512), BF16),
+        out_shape=jax.ShapeDtypeStruct((4, 2, 4, 4, 16, 512), BF16),
         grid=(4,),
         in_specs=[pl.BlockSpec((16, 16, 512), lambda g: (0, g, 0))],
-        out_specs=pl.BlockSpec((8, 4, 16, 512), lambda g: (g, 0, 0, 0)),
+        out_specs=pl.BlockSpec((4, 2, 1, 4, 16, 512), lambda g: (0, 0, g, 0, 0, 0)),
         name="regroup_amplitudes",
-    )(amps)
+    )(amps).reshape(32, 4, 16, 512)
 
 
 def integrals_kernel(own_f, far_f, *rest):
@@ -145,7 +145,7 @@
     total = jnp.sum(parts_ref[...].astype(F32), axis=0)
     for q in range(8):
         lanes = slice(64 * q, 64 * q + 64)
-        out_ref[q] = jnp.concatenate([total[0, :, lanes], total[1, :, lanes]], axis=-1)
+        out_ref[q % 2 * 4 + q // 2] = jnp.concatenate([total[0, :, lanes], total[1, :, lanes]], axis=-1)
 
 
 def sum_parts(parts):
@@ -158,7 +158,7 @@
 
 def finish_kernel(parts_ref, out_ref):
     for core in range(2):
-        both = parts_ref[core] + parts_ref[2 + core] + parts_ref[4 + core] + parts_ref[6 + core]
+        both = jnp.sum(parts_ref[4 * core : 4 * core + 4], axis=0)
         out_ref[2 * core] = both[:, :64]
         out_ref[2 * core + 1] = both[:, 64:]
 
@@ -188,7 +188,7 @@
 
 def per_device(window_factors, factors, amplitudes):
     window = jnp.transpose(window_factors, (0, 2, 1))
-    own_w = exchange(spread(window, other(window, "core")), PLANE)
+    own_w = exchange(spread(window, other(window, "core")), ("y", "x"))
     own_t = regroup(jnp.transpose(amplitudes, (1, 2, 0)))
     factors, own_w, own_t = lax.optimization_barrier((factors, own_w, own_t))
     own_f = exchange(factors.reshape(16, 4, 16, 1536), PLANE)
@@ -205,7 +205,7 @@
     part = ladder_part(other(amps, "core"), far_v, part)
 
     part = sum_parts(exchange(part, PLANE))
-    return jnp.transpose(finish(exchange(part, ("zh", "core"))), (2, 0, 1))
+    return jnp.transpose(finish(exchange(part, ("core", "zh"))), (2, 0, 1))
 
 
 def solution(mesh):

time: 148 us -> 142 us (0.959)
  waiting for transfers between devices: 46.8 us -> 38.5 us
  starting transfers between devices: 38.2 us -> 41 us
    all_to_all x3, waiting for transfers between devices: 16.3 us -> 8.27 us  [exchange(): return lax.all_to_all(x, axis, split_axis=0, concat_axis=0, tiled=True)]
    ppermute x3, starting transfers between devices: 10.7 us -> 13 us  [other(): return lax.ppermute(x, axis, [(0, 1), (1, 0)])]
where the time goes in v4:
time: 142 us; the launch traced here: 141 us
  starting transfers between devices  41 us (29%)
  waiting for transfers between devices  38.5 us (27%)
  blocking collectives  32.1 us (23%)
  Pallas kernels  23.5 us (17%)
  local copies, waits for them, and re-layouts  5.69 us (4%)
    all_to_all x2, blocking collectives, exchange(): return lax.all_to_all(x, axis, split_axis=0, concat_axis=0, tiled=True)  32.1 us
    ppermute x8, waiting for transfers between devices, shift(): lax.ppermute(x, RING, [(flat(z), flat((z + step) % 8)) for z in range(8)])  23.9 us
    all_to_all x3, starting transfers between devices, exchange(): return lax.all_to_all(x, axis, split_axis=0, concat_axis=0, tiled=True)  14 us
    ppermute x8, starting transfers between devices, shift(): lax.ppermute(x, RING, [(flat(z), flat((z + step) % 8)) for z in range(8)])  13.9 us
    ppermute x3, starting transfers between devices, other(): return lax.ppermute(x, axis, [(0, 1), (1, 0)])  13 us
    pallas_call x1, Pallas kernels, build_integrals(): pl.pallas_call(integrals_kernel, out_shape=[pltpu.VMEM((4, 2, 256, 512),...  10.1 us
    all_to_all x3, waiting for transfers between devices, exchange(): return lax.all_to_all(x, axis, split_axis=0, concat_axis=0, tiled=True)  8.27 us
    ppermute x3, waiting for transfers between devices, other(): return lax.ppermute(x, axis, [(0, 1), (1, 0)])  6.38 us
  transfers between devices with their start and end apart: 14, of which 9 were waited for; matrix products, arithmetic and copies ran while one was open for 0% of the time, Pallas kernels for 12%

profile of v4, /device:TPU:1, one launch (start us, length us, event | category | flops | bytes accessed | tf_op | source)
XLA Modules:
  0.0 141.0 jit_solution(2409248339556953326)
XLA Ops:
  0.0 3.2 %collective-permute-start = (bf16[4,48,64]{2,1,0:T(8,128)(2,1)}, bf16[4,48,64]{2,1,0:T(8,128)(2,1)S(1)}, u32[]{:S(2)}, u32[]{:S(2)}) collective-permute-start(bf16[4,48,64]{2,1,0:T(8,128)(2,1)} %bitcast.8), channel_id=1, source_target_pairs={{0,1},{1,0},{2,3},{3,2},{4,5},{5,4},{6,7},{7,6},{8,9},{9,8},{10,11... | collective-permute-start | bytes 73736 | tf_op jit(solution)/shard_map/ppermute | solution.py:179
  3.2 1.1 collective-permute-done.far_ref
  4.3 0.6 copy-done.7
  4.9 1.7 %spread_window.1 = bf16[16,2,48,128]{3,2,1,0:T(8,128)(2,1)} custom-call(bf16[4,48,64]{2,1,0:T(8,128)(2,1)} %bitcast.9, bf16[4,48,64]{2,1,0:T(8,128)(2,1)} %copy-done.7), custom_call_target="tpu_custom_call" | custom-call | tf_op jit(solution)/shard_map/spread_window/pallas_call | solution.py:37
  6.6 5.0 %all-to-all-start = ((bf16[16,2,48,128]{3,2,1,0:T(8,128)(2,1)}), bf16[16,2,48,128]{3,2,1,0:T(8,128)(2,1)S(1)}, u32[]{:S(2)}, u32[]{:S(2)}) async-start(bf16[16,2,48,128]{3,2,1,0:T(8,128)(2,1)} %spread_window.1), calls=%async_computation | async-start | bytes 786432 | tf_op jit(solution)/shard_map/all_to_all | solution.py:175
  11.7 4.1 %regroup_amplitudes.1 = bf16[4,2,4,4,16,512]{5,4,3,2,1,0:T(8,128)(2,1)} custom-call(bf16[16,64,512]{2,1,0:T(8,128)(2,1)} %bitcast.7), custom_call_target="tpu_custom_call" | custom-call | tf_op jit(solution)/shard_map/regroup_amplitudes/pallas_call | solution.py:54
  15.8 5.4 %all-to-all-done.rest_0_ = bf16[16,2,48,128]{3,2,1,0:T(8,128)(2,1)S(1)} async-done(((bf16[16,2,48,128]{3,2,1,0:T(8,128)(2,1)}), bf16[16,2,48,128]{3,2,1,0:T(8,128)(2,1)S(1)}, u32[]{:S(2)}, u32[]{:S(2)}) %all-to-all-start) | async-done | bytes 393248 | tf_op jit(solution)/shard_map/all_to_all | solution.py:175
  21.2 3.7 %all-to-all-start.1 = ((bf16[16,4,16,1536]{3,2,1,0:T(8,128)(2,1)}), bf16[16,4,16,1536]{3,2,1,0:T(8,128)(2,1)S(1)}, u32[]{:S(2)}, u32[]{:S(2)}) async-start(bf16[16,4,16,1536]{3,2,1,0:T(8,128)(2,1)} %bitcast.6), calls=%async_computation.1 | async-start | bytes 6291456 | tf_op jit(solution)/shard_map/all_to_all | solution.py:175
  25.0 1.7 %collective-permute-start.1 = (bf16[16,2,48,128]{3,2,1,0:T(8,128)(2,1)S(1)}, bf16[16,2,48,128]{3,2,1,0:T(8,128)(2,1)S(1)}, u32[]{:S(2)}, u32[]{:S(2)}) collective-permute-start(bf16[16,2,48,128]{3,2,1,0:T(8,128)(2,1)S(1)} %all-to-all-done.rest_0_), channel_id=1, source_target_pairs={{0,32},{32,2},{2,34},{34,4},{4,36},{36,6},{6,38},{38,0},{1,33},{33... | collective-permute-start | bytes 1179656 | tf_op jit(solution)/shard_map/ppermute | solution.py:186
  26.7 0.0 copy-done.4
  26.7 4.0 %collective-permute-start.2 = (bf16[16,2,48,128]{3,2,1,0:T(8,128)(2,1)S(1)}, bf16[16,2,48,128]{3,2,1,0:T(8,128)(2,1)S(1)}, u32[]{:S(2)}, u32[]{:S(2)}) collective-permute-start(bf16[16,2,48,128]{3,2,1,0:T(8,128)(2,1)S(1)} %all-to-all-done.rest_0_), channel_id=1, source_target_pairs={{0,38},{32,0},{2,32},{34,2},{4,34},{36,4},{6,36},{38,6},{1,39},{33... | collective-permute-start | bytes 1179656 | tf_op jit(solution)/shard_map/ppermute | solution.py:186
  30.7 7.8 %collective-permute-done.1.rest_1_ = bf16[16,2,48,128]{3,2,1,0:T(8,128)(2,1)S(1)} collective-permute-done((bf16[16,2,48,128]{3,2,1,0:T(8,128)(2,1)S(1)}, bf16[16,2,48,128]{3,2,1,0:T(8,128)(2,1)S(1)}, u32[]{:S(2)}, u32[]{:S(2)}) %collective-permute-start.1) | collective-permute-done | bytes 393248 | tf_op jit(solution)/shard_map/ppermute | solution.py:186
  38.5 0.0 collective-permute-start.3
  38.6 0.0 collective-permute-done.2.rest_2_
  38.6 0.0 copy-start.9
  38.6 2.7 %collective-permute-start.4 = (bf16[16,2,48,128]{3,2,1,0:T(8,128)(2,1)S(1)}, bf16[16,2,48,128]{3,2,1,0:T(8,128)(2,1)S(1)}, u32[]{:S(2)}, u32[]{:S(2)}) collective-permute-start(bf16[16,2,48,128]{3,2,1,0:T(8,128)(2,1)S(1)} %collective-permute-done.2.rest_2_), channel_id=1, source_target_pairs={{0,38},{32,0},{2,32},{34,2},{4,34},{36,4},{6,36},{38,6},{1,39},{33... | collective-permute-start | bytes 1179656 | tf_op jit(solution)/shard_map/ppermute | solution.py:186
  41.2 7.0 %collective-permute-done.3.rest_3_ = bf16[16,2,48,128]{3,2,1,0:T(8,128)(2,1)S(1)} collective-permute-done((bf16[16,2,48,128]{3,2,1,0:T(8,128)(2,1)S(1)}, bf16[16,2,48,128]{3,2,1,0:T(8,128)(2,1)S(1)}, u32[]{:S(2)}, u32[]{:S(2)}) %collective-permute-start.3) | collective-permute-done | bytes 393248 | tf_op jit(solution)/shard_map/ppermute | solution.py:186
  48.2 0.0 collective-permute-start.5
  48.2 0.0 collective-permute-done.4.rest_4_
  48.2 0.0 copy-start.11
  48.2 2.7 %collective-permute-start.6 = (bf16[16,2,48,128]{3,2,1,0:T(8,128)(2,1)S(1)}, bf16[16,2,48,128]{3,2,1,0:T(8,128)(2,1)S(1)}, u32[]{:S(2)}, u32[]{:S(2)}) collective-permute-start(bf16[16,2,48,128]{3,2,1,0:T(8,128)(2,1)S(1)} %collective-permute-done.4.rest_4_), channel_id=1, source_target_pairs={{0,38},{32,0},{2,32},{34,2},{4,34},{36,4},{6,36},{38,6},{1,39},{33... | collective-permute-start | bytes 1179656 | tf_op jit(solution)/shard_map/ppermute | solution.py:186
  50.9 0.0 copy-done.8
  50.9 0.0 copy-done.9
  50.9 6.1 %collective-permute-done.5.rest_5_ = bf16[16,2,48,128]{3,2,1,0:T(8,128)(2,1)S(1)} collective-permute-done((bf16[16,2,48,128]{3,2,1,0:T(8,128)(2,1)S(1)}, bf16[16,2,48,128]{3,2,1,0:T(8,128)(2,1)S(1)}, u32[]{:S(2)}, u32[]{:S(2)}) %collective-permute-start.5) | collective-permute-done | bytes 393248 | tf_op jit(solution)/shard_map/ppermute | solution.py:186
  57.0 0.1 collective-permute-start.7
  57.1 0.0 collective-permute-done.6.rest_6_
  57.1 2.7 %collective-permute-start.8 = (bf16[8,2,48,128]{3,2,1,0:T(8,128)(2,1)S(1)}, bf16[8,2,48,128]{3,2,1,0:T(8,128)(2,1)}, u32[]{:S(2)}, u32[]{:S(2)}) collective-permute-start(bf16[8,2,48,128]{3,2,1,0:T(8,128)(2,1)S(1)} %slice.9), channel_id=1, source_target_pairs={{0,38},{32,0},{2,32},{34,2},{4,34},{36,4},{6,36},{38,6},{1,39},{33... | collective-permute-start | bytes 589832 | tf_op jit(solution)/shard_map/ppermute | solution.py:186
  59.9 3.0 %collective-permute-done.7.rest_7_ = bf16[8,2,48,128]{3,2,1,0:T(8,128)(2,1)S(1)} collective-permute-done((bf16[8,2,48,128]{3,2,1,0:T(8,128)(2,1)S(1)}, bf16[8,2,48,128]{3,2,1,0:T(8,128)(2,1)S(1)}, u32[]{:S(2)}, u32[]{:S(2)}) %collective-permute-start.7) | collective-permute-done | bytes 196640 | tf_op jit(solution)/shard_map/ppermute | solution.py:186
  62.8 0.7 copy-done.12
  63.5 0.0 collective-permute-done.8.rest_8_
  63.5 1.5 %all-to-all-done.1.own_f = bf16[16,4,16,1536]{3,2,1,0:T(8,128)(2,1)S(1)} async-done(((bf16[16,4,16,1536]{3,2,1,0:T(8,128)(2,1)}), bf16[16,4,16,1536]{3,2,1,0:T(8,128)(2,1)S(1)}, u32[]{:S(2)}, u32[]{:S(2)}) %all-to-all-start.1) | async-done | bytes 3145760 | tf_op jit(solution)/shard_map/all_to_all | solution.py:175
  65.1 5.3 %all-to-all-start.2 = ((bf16[32,4,16,512]{3,2,1,0:T(8,128)(2,1)}), bf16[32,4,16,512]{3,2,1,0:T(8,128)(2,1)}, u32[]{:S(2)}, u32[]{:S(2)}) async-start(bf16[32,4,16,512]{3,2,1,0:T(8,128)(2,1)} %bitcast.5), calls=%async_computation.2 | async-start | bytes 4194304 | tf_op jit(solution)/shard_map/all_to_all | solution.py:175
  70.3 5.1 %collective-permute-start.10 = (bf16[16,4,16,1536]{3,2,1,0:T(8,128)(2,1)S(1)}, bf16[16,4,16,1536]{3,2,1,0:T(8,128)(2,1)S(1)}, u32[]{:S(2)}, u32[]{:S(2)}) collective-permute-start(bf16[16,4,16,1536]{3,2,1,0:T(8,128)(2,1)S(1)} %all-to-all-done.1.own_f), channel_id=1, source_target_pairs={{0,1},{1,0},{2,3},{3,2},{4,5},{5,4},{6,7},{7,6},{8,9},{9,8},{10,11... | collective-permute-start | bytes 9437192 | tf_op jit(solution)/shard_map/ppermute | solution.py:179
  75.4 5.3 %collective-permute-done.10.far_f = bf16[16,4,16,1536]{3,2,1,0:T(8,128)(2,1)S(1)} collective-permute-done((bf16[16,4,16,1536]{3,2,1,0:T(8,128)(2,1)S(1)}, bf16[16,4,16,1536]{3,2,1,0:T(8,128)(2,1)S(1)}, u32[]{:S(2)}, u32[]{:S(2)}) %collective-permute-start.10) | collective-permute-done | bytes 3145760 | tf_op jit(solution)/shard_map/ppermute | solution.py:179
  80.7 10.1 %build_integrals.1 = (bf16[4,2,256,512]{3,2,1,0:T(8,128)(2,1)S(1)}, bf16[4,2,256,512]{3,2,1,0:T(8,128)(2,1)S(1)}) custom-call(bf16[16,4,16,1536]{3,2,1,0:T(8,128)(2,1)S(1)} %all-to-all-done.1.own_f, bf16[16,4,16,1536]{3,2,1,0:T(8,128)(2,1)S(1)} %collective-permute-done.10.far_f, bf16[16,2,48,128]{3,2,1,0:T(8,128)(2,1)} %copy-done.4, ...), custom_call_target="tpu_custom_call" | custom-call | flops 6499999744 | bytes 14000000 | tf_op jit(solution)/shard_map/build_integrals/pallas_call | solution.py:98
  90.8 0.0 copy-start
  90.8 1.4 copy-done
  92.2 1.4 copy-done.2
  93.6 1.3 all-to-all-done.2.t_ref
  94.9 4.7 %collective-permute-start.9 = (bf16[32,4,16,512]{3,2,1,0:T(8,128)(2,1)}, bf16[32,4,16,512]{3,2,1,0:T(8,128)(2,1)S(1)}, u32[]{:S(2)}, u32[]{:S(2)}) collective-permute-start(bf16[32,4,16,512]{3,2,1,0:T(8,128)(2,1)} %all-to-all-done.2.t_ref), channel_id=1, source_target_pairs={{0,1},{1,0},{2,3},{3,2},{4,5},{5,4},{6,7},{7,6},{8,9},{9,8},{10,11... | collective-permute-start | bytes 6291464 | tf_op jit(solution)/shard_map/ppermute | solution.py:179
  99.7 1.6 %copy-done.3 = bf16[4,2,256,512]{3,2,1,0:T(8,128)(2,1)S(1)} copy-done((bf16[4,2,256,512]{3,2,1,0:T(8,128)(2,1)S(1)}, bf16[4,2,256,512]{3,2,1,0:T(8,128)(2,1)}, u32[]{:S(2)}) %copy-start.3) | copy-done | bytes 2097176
  101.2 3.0 %ladder_part.2.rest_0_ = f32[512,512]{1,0:T(8,128)S(1)} custom-call(bf16[32,4,16,512]{3,2,1,0:T(8,128)(2,1)} %all-to-all-done.2.t_ref, bf16[4,2,256,512]{3,2,1,0:T(8,128)(2,1)S(1)} %copy-done.3), custom_call_target="tpu_custom_call" | custom-call | flops 99999997952 | bytes 5000000 | tf_op jit(solution)/shard_map/ladder_part/pallas_call | solution.py:133
  104.2 0.0 collective-permute-done.9.t_ref
  104.2 1.2 ladder_part.3
  105.5 14.2 %all_to_all.25.parts_ref = bf16[16,2,16,512]{3,2,1,0:T(8,128)(2,1)} all-to-all(bf16[16,2,16,512]{3,2,1,0:T(8,128)(2,1)S(1)} %ladder_part.3), channel_id=1, replica_groups=mesh['y'=4,'zl'=2,'x'=4,'zh'=4,'core'=2] {'x','y'}, dimensions={0} | all-to-all | bytes 1048576 | tf_op jit(solution)/shard_map/all_to_all | solution.py:175
  119.7 1.8 %sum_parts.1 = f32[8,16,128]{2,1,0:T(8,128)} custom-call(bf16[16,2,16,512]{3,2,1,0:T(8,128)(2,1)} %all_to_all.25.parts_ref), custom_call_target="tpu_custom_call" | custom-call | tf_op jit(solution)/shard_map/sum_parts/pallas_call | solution.py:152
  121.5 17.9 %all_to_all.26.parts_ref = f32[8,16,128]{2,1,0:T(8,128)} all-to-all(f32[8,16,128]{2,1,0:T(8,128)} %sum_parts.1), channel_id=1, replica_groups=mesh['y'=4,'zl'=2,'x'=4,'zh'=4,'core'=2] {'core','zh'}, dimensions={0} | all-to-all | bytes 131072 | tf_op jit(solution)/shard_map/all_to_all | solution.py:175
  139.5 1.5 %finish.1 = f32[4,16,64]{2,1,0:T(8,128)} custom-call(f32[8,16,128]{2,1,0:T(8,128)} %all_to_all.26.parts_ref), custom_call_target="tpu_custom_call" | custom-call | tf_op jit(solution)/shard_map/finish/pallas_call | solution.py:167
  (17 shorter events, 0.1 us)
Async XLA Ops:
  0.0 4.3 %collective-permute-start = (bf16[4,48,64]{2,1,0:T(8,128)(2,1)}, bf16[4,48,64]{2,1,0:T(8,128)(2,1)S(1)}, u32[]{:S(2)}, u32[]{:S(2)}) collective-permute-start(bf16[4,48,64]{2,1,0:T(8,128)(2,1)} %bitcast.8), channel_id=1, source_target_pairs={{0,1},{1,0},{2,3},{3,2},{4,5},{5,4},{6,7},{7,6},{8,9},{9,8},{10,11... | collective-permute-start | bytes 73736 | tf_op jit(solution)/shard_map/ppermute | solution.py:179
  4.3 0.6 copy-start.7
  6.6 14.6 %all-to-all-start = ((bf16[16,2,48,128]{3,2,1,0:T(8,128)(2,1)}), bf16[16,2,48,128]{3,2,1,0:T(8,128)(2,1)S(1)}, u32[]{:S(2)}, u32[]{:S(2)}) async-start(bf16[16,2,48,128]{3,2,1,0:T(8,128)(2,1)} %spread_window.1), calls=%async_computation | async-start | bytes 786432 | tf_op jit(solution)/shard_map/all_to_all | solution.py:175
  21.2 5.5 %copy-start.4 = (bf16[16,2,48,128]{3,2,1,0:T(8,128)(2,1)}, bf16[16,2,48,128]{3,2,1,0:T(8,128)(2,1)S(1)}, u32[]{:S(2)}) copy-start(bf16[16,2,48,128]{3,2,1,0:T(8,128)(2,1)S(1)} %all-to-all-done.rest_0_) | copy-start | bytes 1179652
  21.2 43.8 %all-to-all-start.1 = ((bf16[16,4,16,1536]{3,2,1,0:T(8,128)(2,1)}), bf16[16,4,16,1536]{3,2,1,0:T(8,128)(2,1)S(1)}, u32[]{:S(2)}, u32[]{:S(2)}) async-start(bf16[16,4,16,1536]{3,2,1,0:T(8,128)(2,1)} %bitcast.6), calls=%async_computation.1 | async-start | bytes 6291456 | tf_op jit(solution)/shard_map/all_to_all | solution.py:175
  25.0 13.6 %collective-permute-start.1 = (bf16[16,2,48,128]{3,2,1,0:T(8,128)(2,1)S(1)}, bf16[16,2,48,128]{3,2,1,0:T(8,128)(2,1)S(1)}, u32[]{:S(2)}, u32[]{:S(2)}) collective-permute-start(bf16[16,2,48,128]{3,2,1,0:T(8,128)(2,1)S(1)} %all-to-all-done.rest_0_), channel_id=1, source_target_pairs={{0,32},{32,2},{2,34},{34,4},{4,36},{36,6},{6,38},{38,0},{1,33},{33... | collective-permute-start | bytes 1179656 | tf_op jit(solution)/shard_map/ppermute | solution.py:186
  26.7 11.9 %collective-permute-start.2 = (bf16[16,2,48,128]{3,2,1,0:T(8,128)(2,1)S(1)}, bf16[16,2,48,128]{3,2,1,0:T(8,128)(2,1)S(1)}, u32[]{:S(2)}, u32[]{:S(2)}) collective-permute-start(bf16[16,2,48,128]{3,2,1,0:T(8,128)(2,1)S(1)} %all-to-all-done.rest_0_), channel_id=1, source_target_pairs={{0,38},{32,0},{2,32},{34,2},{4,34},{36,4},{6,36},{38,6},{1,39},{33... | collective-permute-start | bytes 1179656 | tf_op jit(solution)/shard_map/ppermute | solution.py:186
  38.5 12.4 %copy-start.8 = (bf16[16,2,48,128]{3,2,1,0:T(8,128)(2,1)}, bf16[16,2,48,128]{3,2,1,0:T(8,128)(2,1)S(1)}, u32[]{:S(2)}) copy-start(bf16[16,2,48,128]{3,2,1,0:T(8,128)(2,1)S(1)} %collective-permute-done.1.rest_1_) | copy-start | bytes 1179652
  38.5 9.7 %collective-permute-start.3 = (bf16[16,2,48,128]{3,2,1,0:T(8,128)(2,1)S(1)}, bf16[16,2,48,128]{3,2,1,0:T(8,128)(2,1)S(1)}, u32[]{:S(2)}, u32[]{:S(2)}) collective-permute-start(bf16[16,2,48,128]{3,2,1,0:T(8,128)(2,1)S(1)} %collective-permute-done.1.rest_1_), channel_id=1, source_target_pairs={{0,32},{32,2},{2,34},{34,4},{4,36},{36,6},{6,38},{38,0},{1,33},{33... | collective-permute-start | bytes 1179656 | tf_op jit(solution)/shard_map/ppermute | solution.py:186
  38.6 12.4 %copy-start.9 = (bf16[16,2,48,128]{3,2,1,0:T(8,128)(2,1)}, bf16[16,2,48,128]{3,2,1,0:T(8,128)(2,1)S(1)}, u32[]{:S(2)}) copy-start(bf16[16,2,48,128]{3,2,1,0:T(8,128)(2,1)S(1)} %collective-permute-done.2.rest_2_) | copy-start | bytes 1179652
  38.6 9.7 %collective-permute-start.4 = (bf16[16,2,48,128]{3,2,1,0:T(8,128)(2,1)S(1)}, bf16[16,2,48,128]{3,2,1,0:T(8,128)(2,1)S(1)}, u32[]{:S(2)}, u32[]{:S(2)}) collective-permute-start(bf16[16,2,48,128]{3,2,1,0:T(8,128)(2,1)S(1)} %collective-permute-done.2.rest_2_), channel_id=1, source_target_pairs={{0,38},{32,0},{2,32},{34,2},{4,34},{36,4},{6,36},{38,6},{1,39},{33... | collective-permute-start | bytes 1179656 | tf_op jit(solution)/shard_map/ppermute | solution.py:186
  48.2 2.7 %copy-start.10 = (bf16[16,2,48,128]{3,2,1,0:T(8,128)(2,1)}, bf16[16,2,48,128]{3,2,1,0:T(8,128)(2,1)S(1)}, u32[]{:S(2)}) copy-start(bf16[16,2,48,128]{3,2,1,0:T(8,128)(2,1)S(1)} %collective-permute-done.3.rest_3_) | copy-start | bytes 1179652
  48.2 8.8 %collective-permute-start.5 = (bf16[16,2,48,128]{3,2,1,0:T(8,128)(2,1)S(1)}, bf16[16,2,48,128]{3,2,1,0:T(8,128)(2,1)S(1)}, u32[]{:S(2)}, u32[]{:S(2)}) collective-permute-start(bf16[16,2,48,128]{3,2,1,0:T(8,128)(2,1)S(1)} %collective-permute-done.3.rest_3_), channel_id=1, source_target_pairs={{0,32},{32,2},{2,34},{34,4},{4,36},{36,6},{6,38},{38,0},{1,33},{33... | collective-permute-start | bytes 1179656 | tf_op jit(solution)/shard_map/ppermute | solution.py:186
  48.2 14.6 %copy-start.11 = (bf16[16,2,48,128]{3,2,1,0:T(8,128)(2,1)}, bf16[16,2,48,128]{3,2,1,0:T(8,128)(2,1)S(1)}, u32[]{:S(2)}) copy-start(bf16[16,2,48,128]{3,2,1,0:T(8,128)(2,1)S(1)} %collective-permute-done.4.rest_4_) | copy-start | bytes 1179652
  48.2 8.9 %collective-permute-start.6 = (bf16[16,2,48,128]{3,2,1,0:T(8,128)(2,1)S(1)}, bf16[16,2,48,128]{3,2,1,0:T(8,128)(2,1)S(1)}, u32[]{:S(2)}, u32[]{:S(2)}) collective-permute-start(bf16[16,2,48,128]{3,2,1,0:T(8,128)(2,1)S(1)} %collective-permute-done.4.rest_4_), channel_id=1, source_target_pairs={{0,38},{32,0},{2,32},{34,2},{4,34},{36,4},{6,36},{38,6},{1,39},{33... | collective-permute-start | bytes 1179656 | tf_op jit(solution)/shard_map/ppermute | solution.py:186
  57.0 8.1 %copy-start.5 = (bf16[16,2,48,128]{3,2,1,0:T(8,128)(2,1)}, bf16[16,2,48,128]{3,2,1,0:T(8,128)(2,1)S(1)}, u32[]{:S(2)}) copy-start(bf16[16,2,48,128]{3,2,1,0:T(8,128)(2,1)S(1)} %collective-permute-done.5.rest_5_) | copy-start | bytes 1179652
  57.0 5.8 %collective-permute-start.7 = (bf16[8,2,48,128]{3,2,1,0:T(8,128)(2,1)S(1)}, bf16[8,2,48,128]{3,2,1,0:T(8,128)(2,1)S(1)}, u32[]{:S(2)}, u32[]{:S(2)}) collective-permute-start(bf16[8,2,48,128]{3,2,1,0:T(8,128)(2,1)S(1)} %slice.8), channel_id=1, source_target_pairs={{0,32},{32,2},{2,34},{34,4},{4,36},{36,6},{6,38},{38,0},{1,33},{33... | collective-permute-start | bytes 589832 | tf_op jit(solution)/shard_map/ppermute | solution.py:186
  57.1 5.7 %copy-start.6 = (bf16[16,2,48,128]{3,2,1,0:T(8,128)(2,1)}, bf16[16,2,48,128]{3,2,1,0:T(8,128)(2,1)S(1)}, u32[]{:S(2)}) copy-start(bf16[16,2,48,128]{3,2,1,0:T(8,128)(2,1)S(1)} %collective-permute-done.6.rest_6_) | copy-start | bytes 1179652
  57.1 6.4 %collective-permute-start.8 = (bf16[8,2,48,128]{3,2,1,0:T(8,128)(2,1)S(1)}, bf16[8,2,48,128]{3,2,1,0:T(8,128)(2,1)}, u32[]{:S(2)}, u32[]{:S(2)}) collective-permute-start(bf16[8,2,48,128]{3,2,1,0:T(8,128)(2,1)S(1)} %slice.9), channel_id=1, source_target_pairs={{0,38},{32,0},{2,32},{34,2},{4,34},{36,4},{6,36},{38,6},{1,39},{33... | collective-permute-start | bytes 589832 | tf_op jit(solution)/shard_map/ppermute | solution.py:186
  62.8 0.7 copy-start.12
  65.1 29.8 %all-to-all-start.2 = ((bf16[32,4,16,512]{3,2,1,0:T(8,128)(2,1)}), bf16[32,4,16,512]{3,2,1,0:T(8,128)(2,1)}, u32[]{:S(2)}, u32[]{:S(2)}) async-start(bf16[32,4,16,512]{3,2,1,0:T(8,128)(2,1)} %bitcast.5), calls=%async_computation.2 | async-start | bytes 4194304 | tf_op jit(solution)/shard_map/all_to_all | solution.py:175
  70.3 10.3 %collective-permute-start.10 = (bf16[16,4,16,1536]{3,2,1,0:T(8,128)(2,1)S(1)}, bf16[16,4,16,1536]{3,2,1,0:T(8,128)(2,1)S(1)}, u32[]{:S(2)}, u32[]{:S(2)}) collective-permute-start(bf16[16,4,16,1536]{3,2,1,0:T(8,128)(2,1)S(1)} %all-to-all-done.1.own_f), channel_id=1, source_target_pairs={{0,1},{1,0},{2,3},{3,2},{4,5},{5,4},{6,7},{7,6},{8,9},{9,8},{10,11... | collective-permute-start | bytes 9437192 | tf_op jit(solution)/shard_map/ppermute | solution.py:179
  90.8 1.4 copy-start
  92.2 1.4 copy-start.2
  94.9 9.3 %collective-permute-start.9 = (bf16[32,4,16,512]{3,2,1,0:T(8,128)(2,1)}, bf16[32,4,16,512]{3,2,1,0:T(8,128)(2,1)S(1)}, u32[]{:S(2)}, u32[]{:S(2)}) collective-permute-start(bf16[32,4,16,512]{3,2,1,0:T(8,128)(2,1)} %all-to-all-done.2.t_ref), channel_id=1, source_target_pairs={{0,1},{1,0},{2,3},{3,2},{4,5},{5,4},{6,7},{7,6},{8,9},{9,8},{10,11... | collective-permute-start | bytes 6291464 | tf_op jit(solution)/shard_map/ppermute | solution.py:179
  99.6 1.6 %copy-start.3 = (bf16[4,2,256,512]{3,2,1,0:T(8,128)(2,1)S(1)}, bf16[4,2,256,512]{3,2,1,0:T(8,128)(2,1)}, u32[]{:S(2)}) copy-start(bf16[4,2,256,512]{3,2,1,0:T(8,128)(2,1)} %copy-done.2) | copy-start | bytes 6291460
  101.2 3.0 %copy-start.1 = (bf16[4,2,256,512]{3,2,1,0:T(8,128)(2,1)S(1)}, bf16[4,2,256,512]{3,2,1,0:T(8,128)(2,1)}, u32[]{:S(2)}) copy-start(bf16[4,2,256,512]{3,2,1,0:T(8,128)(2,1)} %copy-done) | copy-start | bytes 6291460

commit v5 on v4

--- a/solution.py
+++ b/solution.py
@@ -37,8 +37,9 @@
     return pl.pallas_call(
         spread_kernel,
         out_shape=jax.ShapeDtypeStruct((16, 2, 48, 128), BF16),
+        in_specs=[pl.BlockSpec((4, 48, 64)), pl.BlockSpec(memory_space=pltpu.VMEM)],
         name="spread_window",
-    )(own, far)
+    )(*in_hbm(own), far)
 
 
 def regroup_kernel(t_ref, out_ref):
@@ -97,7 +98,7 @@
 def build_integrals(own_f, far_f, blocks):
     return pl.pallas_call(
         integrals_kernel,
-        out_shape=[pltpu.VMEM((4, 2, 256, 512), BF16)] * 2,
+        out_shape=[pltpu.HBM((4, 2, 256, 512), BF16)] * 2,
         grid=(4,),
         in_specs=[
             pl.BlockSpec((16, 2, 16, 1536), lambda g: (0, jnp.minimum(g, 1), 0, 0)),
@@ -128,6 +129,40 @@
             out_ref[rows] = total
 
 
+def first_kernel(t_ref, v_ref, out_ref, amps, integrals, sems):
+    copies = []
+    for d in range(4):
+        pair = (
+            pltpu.make_async_copy(t_ref.at[:, d], amps.at[d], sems.at[0, d]),
+            pltpu.make_async_copy(v_ref.at[d], integrals.at[d], sems.at[1, d]),
+        )
+        for copy in pair:
+            copy.start()
+        copies.append(pair)
+    for d, pair in enumerate(copies):
+        for copy in pair:
+            copy.wait()
+        product = dot(integrals[d].reshape(512, 512), amps[d].reshape(512, 512))
+        out_ref[...] = product + out_ref[...] if d else product
+
+
+def first_part(amps, integrals):
+    return pl.pallas_call(
+        first_kernel,
+        out_shape=jax.ShapeDtypeStruct((512, 512), F32),
+        in_specs=[pl.BlockSpec(memory_space=pl.ANY)] * 2,
+        out_specs=pl.BlockSpec(memory_space=pltpu.VMEM),
+        scratch_shapes=[
+            pltpu.VMEM((4, 32, 16, 512), BF16),
+            pltpu.VMEM((4, 2, 256, 512), BF16),
+            pltpu.SemaphoreType.DMA((2, 4)),
+        ],
+        compiler_params=pltpu.CompilerParams(vmem_limit_bytes=16 * MIB),
+        cost_estimate=pl.CostEstimate(flops=100_000_000_000, bytes_accessed=5_000_000, transcendentals=0),
+        name="first_part",
+    )(amps, *in_hbm(integrals))
+
+
 def ladder_part(*operands):
     out_shape = (16, 2, 16, 512) if len(operands) == 3 else (512, 512)
     return pl.pallas_call(
@@ -156,21 +191,6 @@
     )(parts)
 
 
-def finish_kernel(parts_ref, out_ref):
-    for core in range(2):
-        both = jnp.sum(parts_ref[4 * core : 4 * core + 4], axis=0)
-        out_ref[2 * core] = both[:, :64]
-        out_ref[2 * core + 1] = both[:, 64:]
-
-
-def finish(parts):
-    return pl.pallas_call(
-        finish_kernel,
-        out_shape=jax.ShapeDtypeStruct((4, 16, 64), F32),
-        name="finish",
-    )(parts)
-
-
 def exchange(x, axis):
     return lax.all_to_all(x, axis, split_axis=0, concat_axis=0, tiled=True)
 
@@ -191,7 +211,7 @@
     own_w = exchange(spread(window, other(window, "core")), ("y", "x"))
     own_t = regroup(jnp.transpose(amplitudes, (1, 2, 0)))
     factors, own_w, own_t = lax.optimization_barrier((factors, own_w, own_t))
-    own_f = exchange(factors.reshape(16, 4, 16, 1536), PLANE)
+    own_f = exchange(factors.reshape(16, 64, 1536), PLANE).reshape(16, 4, 16, 1536)
 
     blocks, up, down = [own_w], own_w, own_w
     for _ in range(3):
@@ -199,13 +219,14 @@
         blocks += [up, down]
     blocks += [shift(up[:8], 1), shift(down[8:], -1)]
     own_t, own_f, *blocks = lax.optimization_barrier((own_t, own_f, *blocks))
-    amps = exchange(own_t, ROW)
+    amps = exchange(own_t.reshape(32, 64, 512), ROW).reshape(32, 4, 16, 512)
     own_v, far_v = build_integrals(own_f, other(own_f, "core"), blocks)
-    part = ladder_part(amps, own_v)
+    part = first_part(amps, own_v)
     part = ladder_part(other(amps, "core"), far_v, part)
 
     part = sum_parts(exchange(part, PLANE))
-    return jnp.transpose(finish(exchange(part, ("core", "zh"))), (2, 0, 1))
+    part = exchange(part, ("core", "zh")).reshape(2, 4, 16, 2, 64)
+    return jnp.transpose(jnp.sum(part, axis=1), (3, 0, 2, 1)).reshape(64, 4, 16)
 
 
 def solution(mesh):

time: 142 us -> 140 us (0.986)
  local copies, waits for them, and re-layouts: 5.69 us -> 2.09 us
  waiting for transfers between devices: 38.5 us -> 41.1 us
    unnamed x26 -> x20, local copies, waits for them, and re-layouts: 5.66 us -> 1.32 us
    pallas_call x2 -> x1, Pallas kernels: 4.22 us -> 1.24 us  [ladder_part(): pl.pallas_call(ladder_kernel, out_shape=jax.ShapeDtypeStruct(out_shape, B...]
    pallas_call x2, Pallas kernels: 11.7 us -> 14.4 us  [the longest x1 11.6 us: build_integrals(): pl.pallas_call(integrals_kernel, out_shape=[pltpu.HBM((4, 2, 256, 512), B...]
    all_to_all x3, waiting for transfers between devices: 8.27 us -> 9.72 us  [exchange(): return lax.all_to_all(x, axis, split_axis=0, concat_axis=0, tiled=True)]
  transfers between devices with their start and end apart: 14 -> 14, of which waited for: 9 -> 10; matrix products, arithmetic and copies ran while one was open for 0% -> 0% of each run, Pallas kernels for 12% -> 13%
where the time goes in v5:
time: 140 us
  waiting for transfers between devices  41.1 us (29%)
  starting transfers between devices  41 us (29%)
  blocking collectives  32 us (23%)
  Pallas kernels  23.2 us (17%)
  local copies, waits for them, and re-layouts  2.09 us (1%)
    all_to_all x2, blocking collectives, exchange(): return lax.all_to_all(x, axis, split_axis=0, concat_axis=0, tiled=True)  32 us
    ppermute x8, waiting for transfers between devices, shift(): lax.ppermute(x, RING, [(flat(z), flat((z + step) % 8)) for z in range(8)])  23.9 us
    all_to_all x3, starting transfers between devices, exchange(): return lax.all_to_all(x, axis, split_axis=0, concat_axis=0, tiled=True)  14 us
    ppermute x8, starting transfers between devices, shift(): lax.ppermute(x, RING, [(flat(z), flat((z + step) % 8)) for z in range(8)])  13.9 us
    ppermute x3, starting transfers between devices, other(): return lax.ppermute(x, axis, [(0, 1), (1, 0)])  13 us
    pallas_call x1, Pallas kernels, build_integrals(): pl.pallas_call(integrals_kernel, out_shape=[pltpu.HBM((4, 2, 256, 512), B...  11.6 us
    all_to_all x3, waiting for transfers between devices, exchange(): return lax.all_to_all(x, axis, split_axis=0, concat_axis=0, tiled=True)  9.72 us
    ppermute x3, waiting for transfers between devices, other(): return lax.ppermute(x, axis, [(0, 1), (1, 0)])  7.54 us
  transfers between devices with their start and end apart: 14, of which 10 were waited for; matrix products, arithmetic and copies ran while one was open for 0% of the time, Pallas kernels for 13%

profile of v5, /device:TPU:1, one launch (start us, length us, event | category | flops | bytes accessed | tf_op | source)
XLA Modules:
  0.0 139.6 jit_solution(7779097167577235787)
XLA Ops:
  0.0 3.2 %collective-permute-start = (bf16[4,48,64]{2,1,0:T(8,128)(2,1)}, bf16[4,48,64]{2,1,0:T(8,128)(2,1)S(1)}, u32[]{:S(2)}, u32[]{:S(2)}) collective-permute-start(bf16[4,48,64]{2,1,0:T(8,128)(2,1)} %bitcast.15), channel_id=1, source_target_pairs={{0,1},{1,0},{2,3},{3,2},{4,5},{5,4},{6,7},{7,6},{8,9},{9,8},{10,11... | collective-permute-start | bytes 73736 | tf_op jit(solution)/shard_map/ppermute | solution.py:199
  3.2 1.1 collective-permute-done.far_ref
  4.3 0.6 copy-done.4
  5.0 1.7 %spread_window.1 = bf16[16,2,48,128]{3,2,1,0:T(8,128)(2,1)} custom-call(bf16[4,48,64]{2,1,0:T(8,128)(2,1)} %bitcast.16, bf16[4,48,64]{2,1,0:T(8,128)(2,1)} %copy-done.4), custom_call_target="tpu_custom_call" | custom-call | tf_op jit(solution)/shard_map/spread_window/pallas_call | solution.py:37
  6.6 5.0 %all-to-all-start = ((bf16[16,2,48,128]{3,2,1,0:T(8,128)(2,1)}), bf16[16,2,48,128]{3,2,1,0:T(8,128)(2,1)S(1)}, u32[]{:S(2)}, u32[]{:S(2)}) async-start(bf16[16,2,48,128]{3,2,1,0:T(8,128)(2,1)} %spread_window.1), calls=%async_computation | async-start | bytes 786432 | tf_op jit(solution)/shard_map/all_to_all | solution.py:195
  11.7 4.0 %regroup_amplitudes.1 = bf16[4,2,4,4,16,512]{5,4,3,2,1,0:T(8,128)(2,1)} custom-call(bf16[16,64,512]{2,1,0:T(8,128)(2,1)} %bitcast.13), custom_call_target="tpu_custom_call" | custom-call | tf_op jit(solution)/shard_map/regroup_amplitudes/pallas_call | solution.py:55
  15.7 5.5 %all-to-all-done.rest_0_ = bf16[16,2,48,128]{3,2,1,0:T(8,128)(2,1)S(1)} async-done(((bf16[16,2,48,128]{3,2,1,0:T(8,128)(2,1)}), bf16[16,2,48,128]{3,2,1,0:T(8,128)(2,1)S(1)}, u32[]{:S(2)}, u32[]{:S(2)}) %all-to-all-start) | async-done | bytes 393248 | tf_op jit(solution)/shard_map/all_to_all | solution.py:195
  21.2 3.7 %all-to-all-start.1 = ((bf16[16,64,1536]{2,1,0:T(8,128)(2,1)}), bf16[16,64,1536]{2,1,0:T(8,128)(2,1)S(1)}, u32[]{:S(2)}, u32[]{:S(2)}) async-start(bf16[16,64,1536]{2,1,0:T(8,128)(2,1)} %bitcast.12), calls=%async_computation.1 | async-start | bytes 6291456 | tf_op jit(solution)/shard_map/all_to_all | solution.py:195
  25.0 1.7 %collective-permute-start.1 = (bf16[16,2,48,128]{3,2,1,0:T(8,128)(2,1)S(1)}, bf16[16,2,48,128]{3,2,1,0:T(8,128)(2,1)S(1)}, u32[]{:S(2)}, u32[]{:S(2)}) collective-permute-start(bf16[16,2,48,128]{3,2,1,0:T(8,128)(2,1)S(1)} %all-to-all-done.rest_0_), channel_id=1, source_target_pairs={{0,32},{32,2},{2,34},{34,4},{4,36},{36,6},{6,38},{38,0},{1,33},{33... | collective-permute-start | bytes 1179656 | tf_op jit(solution)/shard_map/ppermute | solution.py:206
  26.7 0.0 copy-done.1
  26.7 4.0 %collective-permute-start.2 = (bf16[16,2,48,128]{3,2,1,0:T(8,128)(2,1)S(1)}, bf16[16,2,48,128]{3,2,1,0:T(8,128)(2,1)S(1)}, u32[]{:S(2)}, u32[]{:S(2)}) collective-permute-start(bf16[16,2,48,128]{3,2,1,0:T(8,128)(2,1)S(1)} %all-to-all-done.rest_0_), channel_id=1, source_target_pairs={{0,38},{32,0},{2,32},{34,2},{4,34},{36,4},{6,36},{38,6},{1,39},{33... | collective-permute-start | bytes 1179656 | tf_op jit(solution)/shard_map/ppermute | solution.py:206
  30.7 7.8 %collective-permute-done.1.rest_1_ = bf16[16,2,48,128]{3,2,1,0:T(8,128)(2,1)S(1)} collective-permute-done((bf16[16,2,48,128]{3,2,1,0:T(8,128)(2,1)S(1)}, bf16[16,2,48,128]{3,2,1,0:T(8,128)(2,1)S(1)}, u32[]{:S(2)}, u32[]{:S(2)}) %collective-permute-start.1) | collective-permute-done | bytes 393248 | tf_op jit(solution)/shard_map/ppermute | solution.py:206
  38.6 0.0 collective-permute-start.3
  38.6 0.0 collective-permute-done.2.rest_2_
  38.6 0.0 copy-start.6
  38.6 2.7 %collective-permute-start.4 = (bf16[16,2,48,128]{3,2,1,0:T(8,128)(2,1)S(1)}, bf16[16,2,48,128]{3,2,1,0:T(8,128)(2,1)S(1)}, u32[]{:S(2)}, u32[]{:S(2)}) collective-permute-start(bf16[16,2,48,128]{3,2,1,0:T(8,128)(2,1)S(1)} %collective-permute-done.2.rest_2_), channel_id=1, source_target_pairs={{0,38},{32,0},{2,32},{34,2},{4,34},{36,4},{6,36},{38,6},{1,39},{33... | collective-permute-start | bytes 1179656 | tf_op jit(solution)/shard_map/ppermute | solution.py:206
  41.2 7.0 %collective-permute-done.3.rest_3_ = bf16[16,2,48,128]{3,2,1,0:T(8,128)(2,1)S(1)} collective-permute-done((bf16[16,2,48,128]{3,2,1,0:T(8,128)(2,1)S(1)}, bf16[16,2,48,128]{3,2,1,0:T(8,128)(2,1)S(1)}, u32[]{:S(2)}, u32[]{:S(2)}) %collective-permute-start.3) | collective-permute-done | bytes 393248 | tf_op jit(solution)/shard_map/ppermute | solution.py:206
  48.2 0.0 collective-permute-start.5
  48.2 0.0 collective-permute-done.4.rest_4_
  48.2 0.0 copy-start.8
  48.3 2.7 %collective-permute-start.6 = (bf16[16,2,48,128]{3,2,1,0:T(8,128)(2,1)S(1)}, bf16[16,2,48,128]{3,2,1,0:T(8,128)(2,1)S(1)}, u32[]{:S(2)}, u32[]{:S(2)}) collective-permute-start(bf16[16,2,48,128]{3,2,1,0:T(8,128)(2,1)S(1)} %collective-permute-done.4.rest_4_), channel_id=1, source_target_pairs={{0,38},{32,0},{2,32},{34,2},{4,34},{36,4},{6,36},{38,6},{1,39},{33... | collective-permute-start | bytes 1179656 | tf_op jit(solution)/shard_map/ppermute | solution.py:206
  50.9 0.0 copy-done.7
  50.9 6.1 %collective-permute-done.5.rest_5_ = bf16[16,2,48,128]{3,2,1,0:T(8,128)(2,1)S(1)} collective-permute-done((bf16[16,2,48,128]{3,2,1,0:T(8,128)(2,1)S(1)}, bf16[16,2,48,128]{3,2,1,0:T(8,128)(2,1)S(1)}, u32[]{:S(2)}, u32[]{:S(2)}) %collective-permute-start.5) | collective-permute-done | bytes 393248 | tf_op jit(solution)/shard_map/ppermute | solution.py:206
  57.0 0.1 collective-permute-start.7
  57.1 0.0 collective-permute-done.6.rest_6_
  57.1 0.0 copy-start.3
  57.2 2.7 %collective-permute-start.8 = (bf16[8,2,48,128]{3,2,1,0:T(8,128)(2,1)S(1)}, bf16[8,2,48,128]{3,2,1,0:T(8,128)(2,1)}, u32[]{:S(2)}, u32[]{:S(2)}) collective-permute-start(bf16[8,2,48,128]{3,2,1,0:T(8,128)(2,1)S(1)} %slice.9), channel_id=1, source_target_pairs={{0,38},{32,0},{2,32},{34,2},{4,34},{36,4},{6,36},{38,6},{1,39},{33... | collective-permute-start | bytes 589832 | tf_op jit(solution)/shard_map/ppermute | solution.py:206
  59.9 3.0 %collective-permute-done.7.rest_7_ = bf16[8,2,48,128]{3,2,1,0:T(8,128)(2,1)S(1)} collective-permute-done((bf16[8,2,48,128]{3,2,1,0:T(8,128)(2,1)S(1)}, bf16[8,2,48,128]{3,2,1,0:T(8,128)(2,1)S(1)}, u32[]{:S(2)}, u32[]{:S(2)}) %collective-permute-start.7) | collective-permute-done | bytes 196640 | tf_op jit(solution)/shard_map/ppermute | solution.py:206
  62.8 0.0 copy-done.3
  62.8 0.7 copy-done.9
  63.5 0.0 collective-permute-done.8.rest_8_
  63.5 1.6 %all-to-all-done.1 = bf16[16,64,1536]{2,1,0:T(8,128)(2,1)S(1)} async-done(((bf16[16,64,1536]{2,1,0:T(8,128)(2,1)}), bf16[16,64,1536]{2,1,0:T(8,128)(2,1)S(1)}, u32[]{:S(2)}, u32[]{:S(2)}) %all-to-all-start.1) | async-done | bytes 3145760 | tf_op jit(solution)/shard_map/all_to_all | solution.py:195
  65.1 0.0 copy-done.2
  65.1 5.3 %all-to-all-start.2 = ((bf16[32,64,512]{2,1,0:T(8,128)(2,1)}), bf16[32,64,512]{2,1,0:T(8,128)(2,1)}, u32[]{:S(2)}, u32[]{:S(2)}) async-start(bf16[32,64,512]{2,1,0:T(8,128)(2,1)} %bitcast.11), calls=%async_computation.2 | async-start | bytes 4194304 | tf_op jit(solution)/shard_map/all_to_all | solution.py:195
  70.4 5.0 %collective-permute-start.10 = (bf16[16,4,16,1536]{3,2,1,0:T(8,128)(2,1)S(1)}, bf16[16,4,16,1536]{3,2,1,0:T(8,128)(2,1)S(1)}, u32[]{:S(2)}, u32[]{:S(2)}) collective-permute-start(bf16[16,4,16,1536]{3,2,1,0:T(8,128)(2,1)S(1)} %bitcast.9), channel_id=1, source_target_pairs={{0,1},{1,0},{2,3},{3,2},{4,5},{5,4},{6,7},{7,6},{8,9},{9,8},{10,11... | collective-permute-start | bytes 9437192 | tf_op jit(solution)/shard_map/ppermute | solution.py:199
  75.4 5.3 %collective-permute-done.10.far_f = bf16[16,4,16,1536]{3,2,1,0:T(8,128)(2,1)S(1)} collective-permute-done((bf16[16,4,16,1536]{3,2,1,0:T(8,128)(2,1)S(1)}, bf16[16,4,16,1536]{3,2,1,0:T(8,128)(2,1)S(1)}, u32[]{:S(2)}, u32[]{:S(2)}) %collective-permute-start.10) | collective-permute-done | bytes 3145760 | tf_op jit(solution)/shard_map/ppermute | solution.py:199
  80.7 11.6 %build_integrals.1 = (bf16[4,2,256,512]{3,2,1,0:T(8,128)(2,1)}, bf16[4,2,256,512]{3,2,1,0:T(8,128)(2,1)}) custom-call(bf16[16,4,16,1536]{3,2,1,0:T(8,128)(2,1)S(1)} %bitcast.10, bf16[16,4,16,1536]{3,2,1,0:T(8,128)(2,1)S(1)} %collective-permute-done.10.far_f, bf16[16,2,48,128]{3,2,1,0:T(8,128)(2,1)} %copy-done.1, bf16[16,2,48,128]{3,2,1,0:T(8,128)(2,1)} %copy-done.5, ...), custom_call_target="tpu_custom_call" | custom-call | flops 6499999744 | bytes 14000000 | tf_op jit(solution)/shard_map/build_integrals/pallas_call | solution.py:99
  92.3 2.7 %all-to-all-done.2 = bf16[32,64,512]{2,1,0:T(8,128)(2,1)} async-done(((bf16[32,64,512]{2,1,0:T(8,128)(2,1)}), bf16[32,64,512]{2,1,0:T(8,128)(2,1)}, u32[]{:S(2)}, u32[]{:S(2)}) %all-to-all-start.2) | async-done | bytes 2097184 | tf_op jit(solution)/shard_map/all_to_all | solution.py:195
  94.9 4.7 %collective-permute-start.9 = (bf16[32,4,16,512]{3,2,1,0:T(8,128)(2,1)}, bf16[32,4,16,512]{3,2,1,0:T(8,128)(2,1)S(1)}, u32[]{:S(2)}, u32[]{:S(2)}) collective-permute-start(bf16[32,4,16,512]{3,2,1,0:T(8,128)(2,1)} %bitcast.6.t_ref), channel_id=1, source_target_pairs={{0,1},{1,0},{2,3},{3,2},{4,5},{5,4},{6,7},{7,6},{8,9},{9,8},{10,11... | collective-permute-start | bytes 6291464 | tf_op jit(solution)/shard_map/ppermute | solution.py:199
  99.7 2.8 %first_part.1.rest_0_ = f32[512,512]{1,0:T(8,128)S(1)} custom-call(bf16[32,4,16,512]{3,2,1,0:T(8,128)(2,1)} %bitcast.6.t_ref, bf16[4,2,256,512]{3,2,1,0:T(8,128)(2,1)} %get-tuple-element.36.v_ref), custom_call_target="tpu_custom_call" | custom-call | flops 99999997952 | bytes 5000000 | tf_op jit(solution)/shard_map/first_part/pallas_call | solution.py:150
  102.5 1.2 collective-permute-done.9.t_ref
  103.7 1.2 ladder_part.1
  104.9 14.5 %all_to_all.25.parts_ref = bf16[16,2,16,512]{3,2,1,0:T(8,128)(2,1)} all-to-all(bf16[16,2,16,512]{3,2,1,0:T(8,128)(2,1)S(1)} %ladder_part.1), channel_id=1, replica_groups=mesh['y'=4,'zl'=2,'x'=4,'zh'=4,'core'=2] {'x','y'}, dimensions={0} | all-to-all | bytes 1048576 | tf_op jit(solution)/shard_map/all_to_all | solution.py:195
  119.4 1.8 %sum_parts.1 = f32[8,16,128]{2,1,0:T(8,128)} custom-call(bf16[16,2,16,512]{3,2,1,0:T(8,128)(2,1)} %all_to_all.25.parts_ref), custom_call_target="tpu_custom_call" | custom-call | tf_op jit(solution)/shard_map/sum_parts/pallas_call | solution.py:187
  121.2 17.6 %all_to_all.26 = f32[8,16,128]{2,1,0:T(8,128)S(1)} all-to-all(f32[8,16,128]{2,1,0:T(8,128)} %sum_parts.1), channel_id=1, replica_groups=mesh['y'=4,'zl'=2,'x'=4,'zh'=4,'core'=2] {'core','zh'}, dimensions={0} | all-to-all | bytes 131072 | tf_op jit(solution)/shard_map/all_to_all | solution.py:195
  138.8 0.1 reshape.26
  138.9 0.1 reduce_sum.9
  139.0 0.6 copy.4
  (13 shorter events, 0.0 us)
Async XLA Ops:
  0.0 4.3 %collective-permute-start = (bf16[4,48,64]{2,1,0:T(8,128)(2,1)}, bf16[4,48,64]{2,1,0:T(8,128)(2,1)S(1)}, u32[]{:S(2)}, u32[]{:S(2)}) collective-permute-start(bf16[4,48,64]{2,1,0:T(8,128)(2,1)} %bitcast.15), channel_id=1, source_target_pairs={{0,1},{1,0},{2,3},{3,2},{4,5},{5,4},{6,7},{7,6},{8,9},{9,8},{10,11... | collective-permute-start | bytes 73736 | tf_op jit(solution)/shard_map/ppermute | solution.py:199
  4.3 0.6 copy-start.4
  6.6 14.6 %all-to-all-start = ((bf16[16,2,48,128]{3,2,1,0:T(8,128)(2,1)}), bf16[16,2,48,128]{3,2,1,0:T(8,128)(2,1)S(1)}, u32[]{:S(2)}, u32[]{:S(2)}) async-start(bf16[16,2,48,128]{3,2,1,0:T(8,128)(2,1)} %spread_window.1), calls=%async_computation | async-start | bytes 786432 | tf_op jit(solution)/shard_map/all_to_all | solution.py:195
  21.2 5.5 %copy-start.1 = (bf16[16,2,48,128]{3,2,1,0:T(8,128)(2,1)}, bf16[16,2,48,128]{3,2,1,0:T(8,128)(2,1)S(1)}, u32[]{:S(2)}) copy-start(bf16[16,2,48,128]{3,2,1,0:T(8,128)(2,1)S(1)} %all-to-all-done.rest_0_) | copy-start | bytes 1179652
  21.2 43.8 %all-to-all-start.1 = ((bf16[16,64,1536]{2,1,0:T(8,128)(2,1)}), bf16[16,64,1536]{2,1,0:T(8,128)(2,1)S(1)}, u32[]{:S(2)}, u32[]{:S(2)}) async-start(bf16[16,64,1536]{2,1,0:T(8,128)(2,1)} %bitcast.12), calls=%async_computation.1 | async-start | bytes 6291456 | tf_op jit(solution)/shard_map/all_to_all | solution.py:195
  25.0 13.6 %collective-permute-start.1 = (bf16[16,2,48,128]{3,2,1,0:T(8,128)(2,1)S(1)}, bf16[16,2,48,128]{3,2,1,0:T(8,128)(2,1)S(1)}, u32[]{:S(2)}, u32[]{:S(2)}) collective-permute-start(bf16[16,2,48,128]{3,2,1,0:T(8,128)(2,1)S(1)} %all-to-all-done.rest_0_), channel_id=1, source_target_pairs={{0,32},{32,2},{2,34},{34,4},{4,36},{36,6},{6,38},{38,0},{1,33},{33... | collective-permute-start | bytes 1179656 | tf_op jit(solution)/shard_map/ppermute | solution.py:206
  26.7 11.9 %collective-permute-start.2 = (bf16[16,2,48,128]{3,2,1,0:T(8,128)(2,1)S(1)}, bf16[16,2,48,128]{3,2,1,0:T(8,128)(2,1)S(1)}, u32[]{:S(2)}, u32[]{:S(2)}) collective-permute-start(bf16[16,2,48,128]{3,2,1,0:T(8,128)(2,1)S(1)} %all-to-all-done.rest_0_), channel_id=1, source_target_pairs={{0,38},{32,0},{2,32},{34,2},{4,34},{36,4},{6,36},{38,6},{1,39},{33... | collective-permute-start | bytes 1179656 | tf_op jit(solution)/shard_map/ppermute | solution.py:206
  38.6 12.4 %copy-start.5 = (bf16[16,2,48,128]{3,2,1,0:T(8,128)(2,1)}, bf16[16,2,48,128]{3,2,1,0:T(8,128)(2,1)S(1)}, u32[]{:S(2)}) copy-start(bf16[16,2,48,128]{3,2,1,0:T(8,128)(2,1)S(1)} %collective-permute-done.1.rest_1_) | copy-start | bytes 1179652
  38.6 9.7 %collective-permute-start.3 = (bf16[16,2,48,128]{3,2,1,0:T(8,128)(2,1)S(1)}, bf16[16,2,48,128]{3,2,1,0:T(8,128)(2,1)S(1)}, u32[]{:S(2)}, u32[]{:S(2)}) collective-permute-start(bf16[16,2,48,128]{3,2,1,0:T(8,128)(2,1)S(1)} %collective-permute-done.1.rest_1_), channel_id=1, source_target_pairs={{0,32},{32,2},{2,34},{34,4},{4,36},{36,6},{6,38},{38,0},{1,33},{33... | collective-permute-start | bytes 1179656 | tf_op jit(solution)/shard_map/ppermute | solution.py:206
  38.6 12.4 %copy-start.6 = (bf16[16,2,48,128]{3,2,1,0:T(8,128)(2,1)}, bf16[16,2,48,128]{3,2,1,0:T(8,128)(2,1)S(1)}, u32[]{:S(2)}) copy-start(bf16[16,2,48,128]{3,2,1,0:T(8,128)(2,1)S(1)} %collective-permute-done.2.rest_2_) | copy-start | bytes 1179652
  38.6 9.7 %collective-permute-start.4 = (bf16[16,2,48,128]{3,2,1,0:T(8,128)(2,1)S(1)}, bf16[16,2,48,128]{3,2,1,0:T(8,128)(2,1)S(1)}, u32[]{:S(2)}, u32[]{:S(2)}) collective-permute-start(bf16[16,2,48,128]{3,2,1,0:T(8,128)(2,1)S(1)} %collective-permute-done.2.rest_2_), channel_id=1, source_target_pairs={{0,38},{32,0},{2,32},{34,2},{4,34},{36,4},{6,36},{38,6},{1,39},{33... | collective-permute-start | bytes 1179656 | tf_op jit(solution)/shard_map/ppermute | solution.py:206
  48.2 2.7 %copy-start.7 = (bf16[16,2,48,128]{3,2,1,0:T(8,128)(2,1)}, bf16[16,2,48,128]{3,2,1,0:T(8,128)(2,1)S(1)}, u32[]{:S(2)}) copy-start(bf16[16,2,48,128]{3,2,1,0:T(8,128)(2,1)S(1)} %collective-permute-done.3.rest_3_) | copy-start | bytes 1179652
  48.2 8.8 %collective-permute-start.5 = (bf16[16,2,48,128]{3,2,1,0:T(8,128)(2,1)S(1)}, bf16[16,2,48,128]{3,2,1,0:T(8,128)(2,1)S(1)}, u32[]{:S(2)}, u32[]{:S(2)}) collective-permute-start(bf16[16,2,48,128]{3,2,1,0:T(8,128)(2,1)S(1)} %collective-permute-done.3.rest_3_), channel_id=1, source_target_pairs={{0,32},{32,2},{2,34},{34,4},{4,36},{36,6},{6,38},{38,0},{1,33},{33... | collective-permute-start | bytes 1179656 | tf_op jit(solution)/shard_map/ppermute | solution.py:206
  48.2 14.6 %copy-start.8 = (bf16[16,2,48,128]{3,2,1,0:T(8,128)(2,1)}, bf16[16,2,48,128]{3,2,1,0:T(8,128)(2,1)S(1)}, u32[]{:S(2)}) copy-start(bf16[16,2,48,128]{3,2,1,0:T(8,128)(2,1)S(1)} %collective-permute-done.4.rest_4_) | copy-start | bytes 1179652
  48.3 8.9 %collective-permute-start.6 = (bf16[16,2,48,128]{3,2,1,0:T(8,128)(2,1)S(1)}, bf16[16,2,48,128]{3,2,1,0:T(8,128)(2,1)S(1)}, u32[]{:S(2)}, u32[]{:S(2)}) collective-permute-start(bf16[16,2,48,128]{3,2,1,0:T(8,128)(2,1)S(1)} %collective-permute-done.4.rest_4_), channel_id=1, source_target_pairs={{0,38},{32,0},{2,32},{34,2},{4,34},{36,4},{6,36},{38,6},{1,39},{33... | collective-permute-start | bytes 1179656 | tf_op jit(solution)/shard_map/ppermute | solution.py:206
  57.0 8.1 %copy-start.2 = (bf16[16,2,48,128]{3,2,1,0:T(8,128)(2,1)}, bf16[16,2,48,128]{3,2,1,0:T(8,128)(2,1)S(1)}, u32[]{:S(2)}) copy-start(bf16[16,2,48,128]{3,2,1,0:T(8,128)(2,1)S(1)} %collective-permute-done.5.rest_5_) | copy-start | bytes 1179652
  57.0 5.8 %collective-permute-start.7 = (bf16[8,2,48,128]{3,2,1,0:T(8,128)(2,1)S(1)}, bf16[8,2,48,128]{3,2,1,0:T(8,128)(2,1)S(1)}, u32[]{:S(2)}, u32[]{:S(2)}) collective-permute-start(bf16[8,2,48,128]{3,2,1,0:T(8,128)(2,1)S(1)} %slice.8), channel_id=1, source_target_pairs={{0,32},{32,2},{2,34},{34,4},{4,36},{36,6},{6,38},{38,0},{1,33},{33... | collective-permute-start | bytes 589832 | tf_op jit(solution)/shard_map/ppermute | solution.py:206
  57.1 5.7 %copy-start.3 = (bf16[16,2,48,128]{3,2,1,0:T(8,128)(2,1)}, bf16[16,2,48,128]{3,2,1,0:T(8,128)(2,1)S(1)}, u32[]{:S(2)}) copy-start(bf16[16,2,48,128]{3,2,1,0:T(8,128)(2,1)S(1)} %collective-permute-done.6.rest_6_) | copy-start | bytes 1179652
  57.2 6.4 %collective-permute-start.8 = (bf16[8,2,48,128]{3,2,1,0:T(8,128)(2,1)S(1)}, bf16[8,2,48,128]{3,2,1,0:T(8,128)(2,1)}, u32[]{:S(2)}, u32[]{:S(2)}) collective-permute-start(bf16[8,2,48,128]{3,2,1,0:T(8,128)(2,1)S(1)} %slice.9), channel_id=1, source_target_pairs={{0,38},{32,0},{2,32},{34,2},{4,34},{36,4},{6,36},{38,6},{1,39},{33... | collective-permute-start | bytes 589832 | tf_op jit(solution)/shard_map/ppermute | solution.py:206
  62.8 0.7 copy-start.9
  65.1 29.9 %all-to-all-start.2 = ((bf16[32,64,512]{2,1,0:T(8,128)(2,1)}), bf16[32,64,512]{2,1,0:T(8,128)(2,1)}, u32[]{:S(2)}, u32[]{:S(2)}) async-start(bf16[32,64,512]{2,1,0:T(8,128)(2,1)} %bitcast.11), calls=%async_computation.2 | async-start | bytes 4194304 | tf_op jit(solution)/shard_map/all_to_all | solution.py:195
  70.4 10.3 %collective-permute-start.10 = (bf16[16,4,16,1536]{3,2,1,0:T(8,128)(2,1)S(1)}, bf16[16,4,16,1536]{3,2,1,0:T(8,128)(2,1)S(1)}, u32[]{:S(2)}, u32[]{:S(2)}) collective-permute-start(bf16[16,4,16,1536]{3,2,1,0:T(8,128)(2,1)S(1)} %bitcast.9), channel_id=1, source_target_pairs={{0,1},{1,0},{2,3},{3,2},{4,5},{5,4},{6,7},{7,6},{8,9},{9,8},{10,11... | collective-permute-start | bytes 9437192 | tf_op jit(solution)/shard_map/ppermute | solution.py:199
  94.9 8.7 %collective-permute-start.9 = (bf16[32,4,16,512]{3,2,1,0:T(8,128)(2,1)}, bf16[32,4,16,512]{3,2,1,0:T(8,128)(2,1)S(1)}, u32[]{:S(2)}, u32[]{:S(2)}) collective-permute-start(bf16[32,4,16,512]{3,2,1,0:T(8,128)(2,1)} %bitcast.6.t_ref), channel_id=1, source_target_pairs={{0,1},{1,0},{2,3},{3,2},{4,5},{5,4},{6,7},{7,6},{8,9},{9,8},{10,11... | collective-permute-start | bytes 6291464 | tf_op jit(solution)/shard_map/ppermute | solution.py:199
  99.7 4.0 %copy-start = (bf16[4,2,256,512]{3,2,1,0:T(8,128)(2,1)S(1)}, bf16[4,2,256,512]{3,2,1,0:T(8,128)(2,1)}, u32[]{:S(2)}) copy-start(bf16[4,2,256,512]{3,2,1,0:T(8,128)(2,1)} %get-tuple-element.35.v_ref) | copy-start | bytes 6291460

commit v6 on v5

--- a/solution.py
+++ b/solution.py
@@ -22,24 +22,39 @@
     return lax.dot_general(left, right, (((1,), (0,)), ((), ())), preferred_element_type=F32)
 
 
-def spread_kernel(own_ref, far_ref, out_ref):
-    core = lax.axis_index("core")
-    for a in range(2):
-        mine, theirs = own_ref[2 * core + a], far_ref[2 * core + a]
-        first = jnp.where(core == 0, mine, theirs)
-        second = jnp.where(core == 0, theirs, mine)
-        block = jnp.concatenate([first, second], axis=-1)
+def spread_kernel(w_ref, out_ref):
+    for half in range(2):
+        block = jnp.concatenate([w_ref[2 * half], w_ref[2 * half + 1]], axis=-1)
         for s in range(16):
-            out_ref[s, a] = block
-
-
-def spread(own, far):
+            out_ref[s, half] = block
+
+
+def spread(window):
     return pl.pallas_call(
         spread_kernel,
         out_shape=jax.ShapeDtypeStruct((16, 2, 48, 128), BF16),
-        in_specs=[pl.BlockSpec((4, 48, 64)), pl.BlockSpec(memory_space=pltpu.VMEM)],
         name="spread_window",
-    )(*in_hbm(own), far)
+    )(*in_hbm(window))
+
+
+def join_kernel(own_ref, far_ref, *out_refs):
+    core = lax.axis_index("core")
+    mine, theirs = own_ref[:, core], far_ref[:, core]
+    first = jnp.where(core == 0, mine, theirs)
+    second = jnp.where(core == 0, theirs, mine)
+    for a in range(2):
+        lanes = slice(64 * a, 64 * a + 64)
+        block = jnp.concatenate([first[..., lanes], second[..., lanes]], axis=-1)
+        out_refs[0][:, a] = block[:8]
+        out_refs[1][:, a] = block[8:]
+
+
+def join_cores(own, far):
+    return pl.pallas_call(
+        join_kernel,
+        out_shape=[jax.ShapeDtypeStruct((8, 2, 48, 128), BF16)] * 2,
+        name="join_window",
+    )(own, far)
 
 
 def regroup_kernel(t_ref, out_ref):
@@ -69,13 +84,11 @@
     @pl.when(g == 0)
     def _():
         z = 2 * lax.axis_index("zh") + lax.axis_index("zl")
-        for step, ref in zip((0, -1, 1, -2, 2, -3, 3, 4, 4), blocks):
-            at = (z + step + 8) % 8
+        for n, ref in enumerate(blocks):
+            at = (z + (0, -1, 1, -2, 2, -3, 3, 4)[n // 2] + 8) % 8
             row, lane = (at % 2) * 192, pl.multiple_of((at // 2) * 128, 128)
-            count = ref.shape[0] // 4
-            first = 2 if ref is blocks[8] else 0
-            for y in range(count):
-                rows = pl.ds(pl.multiple_of((y + first) * 384 + row, 192), 192)
+            for y in range(2):
+                rows = pl.ds(pl.multiple_of((y + n % 2 * 2) * 384 + row, 192), 192)
                 for a in range(2):
                     window[a, rows, pl.ds(lane, 128)] = ref[4 * y : 4 * y + 4, a].reshape(192, 128)
 
@@ -208,16 +221,17 @@
 
 def per_device(window_factors, factors, amplitudes):
     window = jnp.transpose(window_factors, (0, 2, 1))
-    own_w = exchange(spread(window, other(window, "core")), ("y", "x"))
+    own_w = exchange(spread(window), ("y", "x"))
     own_t = regroup(jnp.transpose(amplitudes, (1, 2, 0)))
     factors, own_w, own_t = lax.optimization_barrier((factors, own_w, own_t))
     own_f = exchange(factors.reshape(16, 64, 1536), PLANE).reshape(16, 4, 16, 1536)
 
-    blocks, up, down = [own_w], own_w, own_w
+    up = down = join_cores(own_w, other(own_w, "core"))
+    blocks = list(up)
     for _ in range(3):
-        up, down = shift(up, 1), shift(down, -1)
-        blocks += [up, down]
-    blocks += [shift(up[:8], 1), shift(down[8:], -1)]
+        up, down = [shift(half, 1) for half in up], [shift(half, -1) for half in down]
+        blocks += up + down
+    blocks += [shift(up[0], 1), shift(down[1], -1)]
     own_t, own_f, *blocks = lax.optimization_barrier((own_t, own_f, *blocks))
     amps = exchange(own_t.reshape(32, 64, 512), ROW).reshape(32, 4, 16, 512)
     own_v, far_v = build_integrals(own_f, other(own_f, "core"), blocks)

time: 140 us -> 138 us (0.986)
  waiting for transfers between devices: 41.1 us -> 31.3 us
  starting transfers between devices: 41 us -> 49.9 us
  blocking collectives: 32 us -> 29 us
  Pallas kernels: 23.2 us -> 25.4 us
    ppermute x8 -> x14, waiting for transfers between devices: 23.9 us -> 12.9 us  [shift(): lax.ppermute(x, RING, [(flat(z), flat((z + step) % 8)) for z in range(8)])]
    ppermute x8 -> x14, starting transfers between devices: 13.9 us -> 21.6 us  [shift(): lax.ppermute(x, RING, [(flat(z), flat((z + step) % 8)) for z in range(8)])]
    all_to_all x3, starting transfers between devices: 14 us -> 18.6 us  [exchange(): return lax.all_to_all(x, axis, split_axis=0, concat_axis=0, tiled=True)]
    ppermute x3, starting transfers between devices: 13 us -> 9.72 us  [other(): return lax.ppermute(x, axis, [(0, 1), (1, 0)])]
    all_to_all x2, blocking collectives: 32 us -> 29 us  [exchange(): return lax.all_to_all(x, axis, split_axis=0, concat_axis=0, tiled=True)]
    pallas_call x0 -> x1, Pallas kernels: none -> 2.06 us  [join_cores(): pl.pallas_call(join_kernel, out_shape=[jax.ShapeDtypeStruct((8, 2, 48, 12...]
  transfers between devices with their start and end apart: 14 -> 20, of which waited for: 10 -> 12; matrix products, arithmetic and copies ran while one was open for 0% -> 0% of each run, Pallas kernels for 13% -> 15%
where the time goes in v6:
time: 138 us; the launch traced here: 137 us
  starting transfers between devices  49.9 us (36%)
  waiting for transfers between devices  31.3 us (23%)
  blocking collectives  29 us (21%)
  Pallas kernels  25.4 us (18%)
  local copies, waits for them, and re-layouts  1.46 us (1%)
    all_to_all x2, blocking collectives, exchange(): return lax.all_to_all(x, axis, split_axis=0, concat_axis=0, tiled=True)  29 us
    ppermute x14, starting transfers between devices, shift(): lax.ppermute(x, RING, [(flat(z), flat((z + step) % 8)) for z in range(8)])  21.6 us
    all_to_all x3, starting transfers between devices, exchange(): return lax.all_to_all(x, axis, split_axis=0, concat_axis=0, tiled=True)  18.6 us
    ppermute x14, waiting for transfers between devices, shift(): lax.ppermute(x, RING, [(flat(z), flat((z + step) % 8)) for z in range(8)])  12.9 us
    pallas_call x1, Pallas kernels, build_integrals(): pl.pallas_call(integrals_kernel, out_shape=[pltpu.HBM((4, 2, 256, 512), B...  11.7 us
    all_to_all x3, waiting for transfers between devices, exchange(): return lax.all_to_all(x, axis, split_axis=0, concat_axis=0, tiled=True)  10.5 us
    ppermute x3, starting transfers between devices, other(): return lax.ppermute(x, axis, [(0, 1), (1, 0)])  9.72 us
    ppermute x3, waiting for transfers between devices, other(): return lax.ppermute(x, axis, [(0, 1), (1, 0)])  7.93 us
  transfers between devices with their start and end apart: 20, of which 12 were waited for; matrix products, arithmetic and copies ran while one was open for 0% of the time, Pallas kernels for 15%

profile of v6, /device:TPU:1, one launch (start us, length us, event | category | flops | bytes accessed | tf_op | source)
XLA Modules:
  0.0 137.3 jit_solution(4585888337270377272)
XLA Ops:
  0.0 1.7 %spread_window.1 = bf16[16,2,48,128]{3,2,1,0:T(8,128)(2,1)} custom-call(bf16[4,48,64]{2,1,0:T(8,128)(2,1)} %bitcast.15), custom_call_target="tpu_custom_call" | custom-call | tf_op jit(solution)/shard_map/spread_window/pallas_call | solution.py:33
  1.7 7.6 %all-to-all-start = ((bf16[16,2,48,128]{3,2,1,0:T(8,128)(2,1)}), bf16[16,2,48,128]{3,2,1,0:T(8,128)(2,1)S(1)}, u32[]{:S(2)}, u32[]{:S(2)}) async-start(bf16[16,2,48,128]{3,2,1,0:T(8,128)(2,1)} %spread_window.1), calls=%async_computation | async-start | bytes 786432 | tf_op jit(solution)/shard_map/all_to_all | solution.py:208
  9.3 4.0 %regroup_amplitudes.1 = bf16[4,2,4,4,16,512]{5,4,3,2,1,0:T(8,128)(2,1)} custom-call(bf16[16,64,512]{2,1,0:T(8,128)(2,1)} %bitcast.13), custom_call_target="tpu_custom_call" | custom-call | tf_op jit(solution)/shard_map/regroup_amplitudes/pallas_call | solution.py:70
  13.3 5.2 %all-to-all-done.own_ref = bf16[16,2,48,128]{3,2,1,0:T(8,128)(2,1)S(1)} async-done(((bf16[16,2,48,128]{3,2,1,0:T(8,128)(2,1)}), bf16[16,2,48,128]{3,2,1,0:T(8,128)(2,1)S(1)}, u32[]{:S(2)}, u32[]{:S(2)}) %all-to-all-start) | async-done | bytes 393248 | tf_op jit(solution)/shard_map/all_to_all | solution.py:208
  18.4 3.7 %all-to-all-start.1 = ((bf16[16,64,1536]{2,1,0:T(8,128)(2,1)}), bf16[16,64,1536]{2,1,0:T(8,128)(2,1)S(1)}, u32[]{:S(2)}, u32[]{:S(2)}) async-start(bf16[16,64,1536]{2,1,0:T(8,128)(2,1)} %bitcast.12), calls=%async_computation.1 | async-start | bytes 6291456 | tf_op jit(solution)/shard_map/all_to_all | solution.py:208
  22.2 2.0 %collective-permute-start = (bf16[16,2,48,128]{3,2,1,0:T(8,128)(2,1)S(1)}, bf16[16,2,48,128]{3,2,1,0:T(8,128)(2,1)}, u32[]{:S(2)}, u32[]{:S(2)}) collective-permute-start(bf16[16,2,48,128]{3,2,1,0:T(8,128)(2,1)S(1)} %all-to-all-done.own_ref), channel_id=1, source_target_pairs={{0,1},{1,0},{2,3},{3,2},{4,5},{5,4},{6,7},{7,6},{8,9},{9,8},{10,11... | collective-permute-start | bytes 1179656 | tf_op jit(solution)/shard_map/ppermute | solution.py:212
  24.2 1.5 %collective-permute-done.far_ref = bf16[16,2,48,128]{3,2,1,0:T(8,128)(2,1)} collective-permute-done((bf16[16,2,48,128]{3,2,1,0:T(8,128)(2,1)S(1)}, bf16[16,2,48,128]{3,2,1,0:T(8,128)(2,1)}, u32[]{:S(2)}, u32[]{:S(2)}) %collective-permute-start) | collective-permute-done | bytes 393248 | tf_op jit(solution)/shard_map/ppermute | solution.py:212
  25.6 2.1 %join_window.1 = (bf16[8,2,48,128]{3,2,1,0:T(8,128)(2,1)}, bf16[8,2,48,128]{3,2,1,0:T(8,128)(2,1)}) custom-call(bf16[16,2,48,128]{3,2,1,0:T(8,128)(2,1)} %copy-done.1, bf16[16,2,48,128]{3,2,1,0:T(8,128)(2,1)} %collective-permute-done.far_ref), custom_call_target="tpu_custom_call" | custom-call | tf_op jit(solution)/shard_map/join_window/pallas_call | solution.py:53
  27.7 1.6 %collective-permute-start.1 = (bf16[8,2,48,128]{3,2,1,0:T(8,128)(2,1)}, bf16[8,2,48,128]{3,2,1,0:T(8,128)(2,1)S(1)}, u32[]{:S(2)}, u32[]{:S(2)}) collective-permute-start(bf16[8,2,48,128]{3,2,1,0:T(8,128)(2,1)} %get-tuple-element.37.rest_0_), channel_id=1, source_target_pairs={{0,32},{32,2},{2,34},{34,4},{4,36},{36,6},{6,38},{38,0},{1,33},{33... | collective-permute-start | bytes 589832 | tf_op jit(solution)/shard_map/ppermute | solution.py:219
  29.3 3.9 %collective-permute-start.4 = (bf16[8,2,48,128]{3,2,1,0:T(8,128)(2,1)}, bf16[8,2,48,128]{3,2,1,0:T(8,128)(2,1)S(1)}, u32[]{:S(2)}, u32[]{:S(2)}) collective-permute-start(bf16[8,2,48,128]{3,2,1,0:T(8,128)(2,1)} %get-tuple-element.38.rest_1_), channel_id=1, source_target_pairs={{0,38},{32,0},{2,32},{34,2},{4,34},{36,4},{6,36},{38,6},{1,39},{33... | collective-permute-start | bytes 589832 | tf_op jit(solution)/shard_map/ppermute | solution.py:219
  33.3 2.7 %collective-permute-start.3 = (bf16[8,2,48,128]{3,2,1,0:T(8,128)(2,1)}, bf16[8,2,48,128]{3,2,1,0:T(8,128)(2,1)S(1)}, u32[]{:S(2)}, u32[]{:S(2)}) collective-permute-start(bf16[8,2,48,128]{3,2,1,0:T(8,128)(2,1)} %get-tuple-element.37.rest_0_), channel_id=1, source_target_pairs={{0,38},{32,0},{2,32},{34,2},{4,34},{36,4},{6,36},{38,6},{1,39},{33... | collective-permute-start | bytes 589832 | tf_op jit(solution)/shard_map/ppermute | solution.py:219
  36.0 2.5 %collective-permute-done.1.rest_2_ = bf16[8,2,48,128]{3,2,1,0:T(8,128)(2,1)S(1)} collective-permute-done((bf16[8,2,48,128]{3,2,1,0:T(8,128)(2,1)}, bf16[8,2,48,128]{3,2,1,0:T(8,128)(2,1)S(1)}, u32[]{:S(2)}, u32[]{:S(2)}) %collective-permute-start.1) | collective-permute-done | bytes 196640 | tf_op jit(solution)/shard_map/ppermute | solution.py:219
  38.5 0.0 collective-permute-start.5
  38.5 0.0 collective-permute-done.4.rest_5_
  38.5 2.7 %collective-permute-start.8 = (bf16[8,2,48,128]{3,2,1,0:T(8,128)(2,1)S(1)}, bf16[8,2,48,128]{3,2,1,0:T(8,128)(2,1)S(1)}, u32[]{:S(2)}, u32[]{:S(2)}) collective-permute-start(bf16[8,2,48,128]{3,2,1,0:T(8,128)(2,1)S(1)} %collective-permute-done.4.rest_5_), channel_id=1, source_target_pairs={{0,38},{32,0},{2,32},{34,2},{4,34},{36,4},{6,36},{38,6},{1,39},{33... | collective-permute-start | bytes 589832 | tf_op jit(solution)/shard_map/ppermute | solution.py:219
  41.1 1.5 %collective-permute-done.2.rest_3_ = bf16[8,2,48,128]{3,2,1,0:T(8,128)(2,1)S(1)} collective-permute-done((bf16[8,2,48,128]{3,2,1,0:T(8,128)(2,1)}, bf16[8,2,48,128]{3,2,1,0:T(8,128)(2,1)S(1)}, u32[]{:S(2)}, u32[]{:S(2)}) %collective-permute-start.2) | collective-permute-done | bytes 196640 | tf_op jit(solution)/shard_map/ppermute | solution.py:219
  42.7 0.0 collective-permute-start.6
  42.7 0.0 collective-permute-done.3.rest_4_
  42.7 2.7 %collective-permute-start.7 = (bf16[8,2,48,128]{3,2,1,0:T(8,128)(2,1)S(1)}, bf16[8,2,48,128]{3,2,1,0:T(8,128)(2,1)S(1)}, u32[]{:S(2)}, u32[]{:S(2)}) collective-permute-start(bf16[8,2,48,128]{3,2,1,0:T(8,128)(2,1)S(1)} %collective-permute-done.3.rest_4_), channel_id=1, source_target_pairs={{0,38},{32,0},{2,32},{34,2},{4,34},{36,4},{6,36},{38,6},{1,39},{33... | collective-permute-start | bytes 589832 | tf_op jit(solution)/shard_map/ppermute | solution.py:219
  45.4 0.9 collective-permute-done.5.rest_6_
  46.3 0.0 collective-permute-start.9
  46.3 0.0 collective-permute-done.8.rest_9_
  46.3 2.7 %collective-permute-start.12 = (bf16[8,2,48,128]{3,2,1,0:T(8,128)(2,1)S(1)}, bf16[8,2,48,128]{3,2,1,0:T(8,128)(2,1)S(1)}, u32[]{:S(2)}, u32[]{:S(2)}) collective-permute-start(bf16[8,2,48,128]{3,2,1,0:T(8,128)(2,1)S(1)} %collective-permute-done.8.rest_9_), channel_id=1, source_target_pairs={{0,38},{32,0},{2,32},{34,2},{4,34},{36,4},{6,36},{38,6},{1,39},{33... | collective-permute-start | bytes 589832 | tf_op jit(solution)/shard_map/ppermute | solution.py:219
  48.9 1.5 %collective-permute-done.6.rest_7_ = bf16[8,2,48,128]{3,2,1,0:T(8,128)(2,1)S(1)} collective-permute-done((bf16[8,2,48,128]{3,2,1,0:T(8,128)(2,1)S(1)}, bf16[8,2,48,128]{3,2,1,0:T(8,128)(2,1)S(1)}, u32[]{:S(2)}, u32[]{:S(2)}) %collective-permute-start.6) | collective-permute-done | bytes 196640 | tf_op jit(solution)/shard_map/ppermute | solution.py:219
  50.5 0.0 collective-permute-start.10
  50.5 2.7 %collective-permute-start.11 = (bf16[8,2,48,128]{3,2,1,0:T(8,128)(2,1)S(1)}, bf16[8,2,48,128]{3,2,1,0:T(8,128)(2,1)S(1)}, u32[]{:S(2)}, u32[]{:S(2)}) collective-permute-start(bf16[8,2,48,128]{3,2,1,0:T(8,128)(2,1)S(1)} %collective-permute-done.7.rest_8_), channel_id=1, source_target_pairs={{0,38},{32,0},{2,32},{34,2},{4,34},{36,4},{6,36},{38,6},{1,39},{33... | collective-permute-start | bytes 589832 | tf_op jit(solution)/shard_map/ppermute | solution.py:219
  53.2 1.3 collective-permute-done.9.rest_10_
  54.5 0.0 collective-permute-done.12.rest_13_
  54.5 2.7 %collective-permute-start.14 = (bf16[8,2,48,128]{3,2,1,0:T(8,128)(2,1)S(1)}, bf16[8,2,48,128]{3,2,1,0:T(8,128)(2,1)}, u32[]{:S(2)}, u32[]{:S(2)}) collective-permute-start(bf16[8,2,48,128]{3,2,1,0:T(8,128)(2,1)S(1)} %collective-permute-done.12.rest_13_), channel_id=1, source_target_pairs={{0,38},{32,0},{2,32},{34,2},{4,34},{36,4},{6,36},{38,6},{1,39},{33... | collective-permute-start | bytes 589832 | tf_op jit(solution)/shard_map/ppermute | solution.py:219
  57.1 1.1 collective-permute-done.10.rest_11_
  58.3 4.0 %collective-permute-done.13.rest_14_ = bf16[8,2,48,128]{3,2,1,0:T(8,128)(2,1)S(1)} collective-permute-done((bf16[8,2,48,128]{3,2,1,0:T(8,128)(2,1)S(1)}, bf16[8,2,48,128]{3,2,1,0:T(8,128)(2,1)S(1)}, u32[]{:S(2)}, u32[]{:S(2)}) %collective-permute-start.13) | collective-permute-done | bytes 196640 | tf_op jit(solution)/shard_map/ppermute | solution.py:219
  62.3 0.7 copy-done.14
  63.0 0.0 collective-permute-done.14.rest_15_
  63.0 7.3 %all-to-all-start.2 = ((bf16[32,64,512]{2,1,0:T(8,128)(2,1)}), bf16[32,64,512]{2,1,0:T(8,128)(2,1)}, u32[]{:S(2)}, u32[]{:S(2)}) async-start(bf16[32,64,512]{2,1,0:T(8,128)(2,1)} %bitcast.11), calls=%async_computation.2 | async-start | bytes 4194304 | tf_op jit(solution)/shard_map/all_to_all | solution.py:208
  70.3 2.7 %collective-permute-start.16 = (bf16[16,4,16,1536]{3,2,1,0:T(8,128)(2,1)S(1)}, bf16[16,4,16,1536]{3,2,1,0:T(8,128)(2,1)S(1)}, u32[]{:S(2)}, u32[]{:S(2)}) collective-permute-start(bf16[16,4,16,1536]{3,2,1,0:T(8,128)(2,1)S(1)} %bitcast.9), channel_id=1, source_target_pairs={{0,1},{1,0},{2,3},{3,2},{4,5},{5,4},{6,7},{7,6},{8,9},{9,8},{10,11... | collective-permute-start | bytes 9437192 | tf_op jit(solution)/shard_map/ppermute | solution.py:212
  73.1 5.3 %collective-permute-done.16.far_f = bf16[16,4,16,1536]{3,2,1,0:T(8,128)(2,1)S(1)} collective-permute-done((bf16[16,4,16,1536]{3,2,1,0:T(8,128)(2,1)S(1)}, bf16[16,4,16,1536]{3,2,1,0:T(8,128)(2,1)S(1)}, u32[]{:S(2)}, u32[]{:S(2)}) %collective-permute-start.16) | collective-permute-done | bytes 3145760 | tf_op jit(solution)/shard_map/ppermute | solution.py:212
  78.4 11.7 %build_integrals.1 = (bf16[4,2,256,512]{3,2,1,0:T(8,128)(2,1)}, bf16[4,2,256,512]{3,2,1,0:T(8,128)(2,1)}) custom-call(bf16[16,4,16,1536]{3,2,1,0:T(8,128)(2,1)S(1)} %bitcast.10, bf16[16,4,16,1536]{3,2,1,0:T(8,128)(2,1)S(1)} %collective-permute-done.16.far_f, bf16[8,2,48,128]{3,2,1,0:T(8,128)(2,1)} %get-tuple-element.37.rest_0_, ...), custom_call_target="tpu_custom_call" | custom-call | flops 6499999744 | bytes 14000000 | tf_op jit(solution)/shard_map/build_integrals/pallas_call | solution.py:112
  90.1 5.3 %all-to-all-done.2 = bf16[32,64,512]{2,1,0:T(8,128)(2,1)} async-done(((bf16[32,64,512]{2,1,0:T(8,128)(2,1)}), bf16[32,64,512]{2,1,0:T(8,128)(2,1)}, u32[]{:S(2)}, u32[]{:S(2)}) %all-to-all-start.2) | async-done | bytes 2097184 | tf_op jit(solution)/shard_map/all_to_all | solution.py:208
  95.4 5.0 %collective-permute-start.15 = (bf16[32,4,16,512]{3,2,1,0:T(8,128)(2,1)}, bf16[32,4,16,512]{3,2,1,0:T(8,128)(2,1)S(1)}, u32[]{:S(2)}, u32[]{:S(2)}) collective-permute-start(bf16[32,4,16,512]{3,2,1,0:T(8,128)(2,1)} %bitcast.6.t_ref), channel_id=1, source_target_pairs={{0,1},{1,0},{2,3},{3,2},{4,5},{5,4},{6,7},{7,6},{8,9},{9,8},{10,11... | collective-permute-start | bytes 6291464 | tf_op jit(solution)/shard_map/ppermute | solution.py:212
  100.4 2.8 %first_part.1.rest_0_ = f32[512,512]{1,0:T(8,128)S(1)} custom-call(bf16[32,4,16,512]{3,2,1,0:T(8,128)(2,1)} %bitcast.6.t_ref, bf16[4,2,256,512]{3,2,1,0:T(8,128)(2,1)} %get-tuple-element.54.v_ref), custom_call_target="tpu_custom_call" | custom-call | flops 99999997952 | bytes 5000000 | tf_op jit(solution)/shard_map/first_part/pallas_call | solution.py:163
  103.3 1.2 collective-permute-done.15.t_ref
  104.4 1.2 ladder_part.1
  105.7 13.9 %all_to_all.25.parts_ref = bf16[16,2,16,512]{3,2,1,0:T(8,128)(2,1)} all-to-all(bf16[16,2,16,512]{3,2,1,0:T(8,128)(2,1)S(1)} %ladder_part.1), channel_id=1, replica_groups=mesh['y'=4,'zl'=2,'x'=4,'zh'=4,'core'=2] {'x','y'}, dimensions={0} | all-to-all | bytes 1048576 | tf_op jit(solution)/shard_map/all_to_all | solution.py:208
  119.6 1.8 %sum_parts.1 = f32[8,16,128]{2,1,0:T(8,128)} custom-call(bf16[16,2,16,512]{3,2,1,0:T(8,128)(2,1)} %all_to_all.25.parts_ref), custom_call_target="tpu_custom_call" | custom-call | tf_op jit(solution)/shard_map/sum_parts/pallas_call | solution.py:200
  121.4 15.1 %all_to_all.26 = f32[8,16,128]{2,1,0:T(8,128)S(1)} all-to-all(f32[8,16,128]{2,1,0:T(8,128)} %sum_parts.1), channel_id=1, replica_groups=mesh['y'=4,'zl'=2,'x'=4,'zh'=4,'core'=2] {'core','zh'}, dimensions={0} | all-to-all | bytes 131072 | tf_op jit(solution)/shard_map/all_to_all | solution.py:208
  136.5 0.1 reshape.26
  136.6 0.1 reduce_sum.9
  136.7 0.6 copy.4
  (34 shorter events, 0.1 us)
Async XLA Ops:
  1.7 16.8 %all-to-all-start = ((bf16[16,2,48,128]{3,2,1,0:T(8,128)(2,1)}), bf16[16,2,48,128]{3,2,1,0:T(8,128)(2,1)S(1)}, u32[]{:S(2)}, u32[]{:S(2)}) async-start(bf16[16,2,48,128]{3,2,1,0:T(8,128)(2,1)} %spread_window.1), calls=%async_computation | async-start | bytes 786432 | tf_op jit(solution)/shard_map/all_to_all | solution.py:208
  18.4 3.8 %copy-start.1 = (bf16[16,2,48,128]{3,2,1,0:T(8,128)(2,1)}, bf16[16,2,48,128]{3,2,1,0:T(8,128)(2,1)S(1)}, u32[]{:S(2)}) copy-start(bf16[16,2,48,128]{3,2,1,0:T(8,128)(2,1)S(1)} %all-to-all-done.own_ref) | copy-start | bytes 1179652
  18.4 44.6 %all-to-all-start.1 = ((bf16[16,64,1536]{2,1,0:T(8,128)(2,1)}), bf16[16,64,1536]{2,1,0:T(8,128)(2,1)S(1)}, u32[]{:S(2)}, u32[]{:S(2)}) async-start(bf16[16,64,1536]{2,1,0:T(8,128)(2,1)} %bitcast.12), calls=%async_computation.1 | async-start | bytes 6291456 | tf_op jit(solution)/shard_map/all_to_all | solution.py:208
  22.2 3.4 %collective-permute-start = (bf16[16,2,48,128]{3,2,1,0:T(8,128)(2,1)S(1)}, bf16[16,2,48,128]{3,2,1,0:T(8,128)(2,1)}, u32[]{:S(2)}, u32[]{:S(2)}) collective-permute-start(bf16[16,2,48,128]{3,2,1,0:T(8,128)(2,1)S(1)} %all-to-all-done.own_ref), channel_id=1, source_target_pairs={{0,1},{1,0},{2,3},{3,2},{4,5},{5,4},{6,7},{7,6},{8,9},{9,8},{10,11... | collective-permute-start | bytes 1179656 | tf_op jit(solution)/shard_map/ppermute | solution.py:212
  27.7 10.8 %collective-permute-start.1 = (bf16[8,2,48,128]{3,2,1,0:T(8,128)(2,1)}, bf16[8,2,48,128]{3,2,1,0:T(8,128)(2,1)S(1)}, u32[]{:S(2)}, u32[]{:S(2)}) collective-permute-start(bf16[8,2,48,128]{3,2,1,0:T(8,128)(2,1)} %get-tuple-element.37.rest_0_), channel_id=1, source_target_pairs={{0,32},{32,2},{2,34},{34,4},{4,36},{36,6},{6,38},{38,0},{1,33},{33... | collective-permute-start | bytes 589832 | tf_op jit(solution)/shard_map/ppermute | solution.py:219
  29.3 9.1 %collective-permute-start.4 = (bf16[8,2,48,128]{3,2,1,0:T(8,128)(2,1)}, bf16[8,2,48,128]{3,2,1,0:T(8,128)(2,1)S(1)}, u32[]{:S(2)}, u32[]{:S(2)}) collective-permute-start(bf16[8,2,48,128]{3,2,1,0:T(8,128)(2,1)} %get-tuple-element.38.rest_1_), channel_id=1, source_target_pairs={{0,38},{32,0},{2,32},{34,2},{4,34},{36,4},{6,36},{38,6},{1,39},{33... | collective-permute-start | bytes 589832 | tf_op jit(solution)/shard_map/ppermute | solution.py:219
  33.3 9.4 %collective-permute-start.2 = (bf16[8,2,48,128]{3,2,1,0:T(8,128)(2,1)}, bf16[8,2,48,128]{3,2,1,0:T(8,128)(2,1)S(1)}, u32[]{:S(2)}, u32[]{:S(2)}) collective-permute-start(bf16[8,2,48,128]{3,2,1,0:T(8,128)(2,1)} %get-tuple-element.38.rest_1_), channel_id=1, source_target_pairs={{0,32},{32,2},{2,34},{34,4},{4,36},{36,6},{6,38},{38,0},{1,33},{33... | collective-permute-start | bytes 589832 | tf_op jit(solution)/shard_map/ppermute | solution.py:219
  33.3 9.4 %collective-permute-start.3 = (bf16[8,2,48,128]{3,2,1,0:T(8,128)(2,1)}, bf16[8,2,48,128]{3,2,1,0:T(8,128)(2,1)S(1)}, u32[]{:S(2)}, u32[]{:S(2)}) collective-permute-start(bf16[8,2,48,128]{3,2,1,0:T(8,128)(2,1)} %get-tuple-element.37.rest_0_), channel_id=1, source_target_pairs={{0,38},{32,0},{2,32},{34,2},{4,34},{36,4},{6,36},{38,6},{1,39},{33... | collective-permute-start | bytes 589832 | tf_op jit(solution)/shard_map/ppermute | solution.py:219
  38.5 24.6 %copy-start.2 = (bf16[8,2,48,128]{3,2,1,0:T(8,128)(2,1)}, bf16[8,2,48,128]{3,2,1,0:T(8,128)(2,1)S(1)}, u32[]{:S(2)}) copy-start(bf16[8,2,48,128]{3,2,1,0:T(8,128)(2,1)S(1)} %collective-permute-done.1.rest_2_) | copy-start | bytes 589828
  38.5 7.8 %collective-permute-start.5 = (bf16[8,2,48,128]{3,2,1,0:T(8,128)(2,1)S(1)}, bf16[8,2,48,128]{3,2,1,0:T(8,128)(2,1)S(1)}, u32[]{:S(2)}, u32[]{:S(2)}) collective-permute-start(bf16[8,2,48,128]{3,2,1,0:T(8,128)(2,1)S(1)} %collective-permute-done.1.rest_2_), channel_id=1, source_target_pairs={{0,32},{32,2},{2,34},{34,4},{4,36},{36,6},{6,38},{38,0},{1,33},{33... | collective-permute-start | bytes 589832 | tf_op jit(solution)/shard_map/ppermute | solution.py:219
  38.5 24.6 %copy-start.3 = (bf16[8,2,48,128]{3,2,1,0:T(8,128)(2,1)}, bf16[8,2,48,128]{3,2,1,0:T(8,128)(2,1)S(1)}, u32[]{:S(2)}) copy-start(bf16[8,2,48,128]{3,2,1,0:T(8,128)(2,1)S(1)} %collective-permute-done.4.rest_5_) | copy-start | bytes 589828
  38.5 7.8 %collective-permute-start.8 = (bf16[8,2,48,128]{3,2,1,0:T(8,128)(2,1)S(1)}, bf16[8,2,48,128]{3,2,1,0:T(8,128)(2,1)S(1)}, u32[]{:S(2)}, u32[]{:S(2)}) collective-permute-start(bf16[8,2,48,128]{3,2,1,0:T(8,128)(2,1)S(1)} %collective-permute-done.4.rest_5_), channel_id=1, source_target_pairs={{0,38},{32,0},{2,32},{34,2},{4,34},{36,4},{6,36},{38,6},{1,39},{33... | collective-permute-start | bytes 589832 | tf_op jit(solution)/shard_map/ppermute | solution.py:219
  42.7 19.6 %copy-start.4 = (bf16[8,2,48,128]{3,2,1,0:T(8,128)(2,1)}, bf16[8,2,48,128]{3,2,1,0:T(8,128)(2,1)S(1)}, u32[]{:S(2)}) copy-start(bf16[8,2,48,128]{3,2,1,0:T(8,128)(2,1)S(1)} %collective-permute-done.2.rest_3_) | copy-start | bytes 589828
  42.7 7.8 %collective-permute-start.6 = (bf16[8,2,48,128]{3,2,1,0:T(8,128)(2,1)S(1)}, bf16[8,2,48,128]{3,2,1,0:T(8,128)(2,1)S(1)}, u32[]{:S(2)}, u32[]{:S(2)}) collective-permute-start(bf16[8,2,48,128]{3,2,1,0:T(8,128)(2,1)S(1)} %collective-permute-done.2.rest_3_), channel_id=1, source_target_pairs={{0,32},{32,2},{2,34},{34,4},{4,36},{36,6},{6,38},{38,0},{1,33},{33... | collective-permute-start | bytes 589832 | tf_op jit(solution)/shard_map/ppermute | solution.py:219
  42.7 19.6 %copy-start.5 = (bf16[8,2,48,128]{3,2,1,0:T(8,128)(2,1)}, bf16[8,2,48,128]{3,2,1,0:T(8,128)(2,1)S(1)}, u32[]{:S(2)}) copy-start(bf16[8,2,48,128]{3,2,1,0:T(8,128)(2,1)S(1)} %collective-permute-done.3.rest_4_) | copy-start | bytes 589828
  42.7 7.8 %collective-permute-start.7 = (bf16[8,2,48,128]{3,2,1,0:T(8,128)(2,1)S(1)}, bf16[8,2,48,128]{3,2,1,0:T(8,128)(2,1)S(1)}, u32[]{:S(2)}, u32[]{:S(2)}) collective-permute-start(bf16[8,2,48,128]{3,2,1,0:T(8,128)(2,1)S(1)} %collective-permute-done.3.rest_4_), channel_id=1, source_target_pairs={{0,38},{32,0},{2,32},{34,2},{4,34},{36,4},{6,36},{38,6},{1,39},{33... | collective-permute-start | bytes 589832 | tf_op jit(solution)/shard_map/ppermute | solution.py:219
  46.3 16.0 %copy-start.6 = (bf16[8,2,48,128]{3,2,1,0:T(8,128)(2,1)}, bf16[8,2,48,128]{3,2,1,0:T(8,128)(2,1)S(1)}, u32[]{:S(2)}) copy-start(bf16[8,2,48,128]{3,2,1,0:T(8,128)(2,1)S(1)} %collective-permute-done.5.rest_6_) | copy-start | bytes 589828
  46.3 8.2 %collective-permute-start.9 = (bf16[8,2,48,128]{3,2,1,0:T(8,128)(2,1)S(1)}, bf16[8,2,48,128]{3,2,1,0:T(8,128)(2,1)S(1)}, u32[]{:S(2)}, u32[]{:S(2)}) collective-permute-start(bf16[8,2,48,128]{3,2,1,0:T(8,128)(2,1)S(1)} %collective-permute-done.5.rest_6_), channel_id=1, source_target_pairs={{0,32},{32,2},{2,34},{34,4},{4,36},{36,6},{6,38},{38,0},{1,33},{33... | collective-permute-start | bytes 589832 | tf_op jit(solution)/shard_map/ppermute | solution.py:219
  46.3 16.0 %copy-start.7 = (bf16[8,2,48,128]{3,2,1,0:T(8,128)(2,1)}, bf16[8,2,48,128]{3,2,1,0:T(8,128)(2,1)S(1)}, u32[]{:S(2)}) copy-start(bf16[8,2,48,128]{3,2,1,0:T(8,128)(2,1)S(1)} %collective-permute-done.8.rest_9_) | copy-start | bytes 589828
  46.3 8.2 %collective-permute-start.12 = (bf16[8,2,48,128]{3,2,1,0:T(8,128)(2,1)S(1)}, bf16[8,2,48,128]{3,2,1,0:T(8,128)(2,1)S(1)}, u32[]{:S(2)}, u32[]{:S(2)}) collective-permute-start(bf16[8,2,48,128]{3,2,1,0:T(8,128)(2,1)S(1)} %collective-permute-done.8.rest_9_), channel_id=1, source_target_pairs={{0,38},{32,0},{2,32},{34,2},{4,34},{36,4},{6,36},{38,6},{1,39},{33... | collective-permute-start | bytes 589832 | tf_op jit(solution)/shard_map/ppermute | solution.py:219
  50.5 11.8 %copy-start.8 = (bf16[8,2,48,128]{3,2,1,0:T(8,128)(2,1)}, bf16[8,2,48,128]{3,2,1,0:T(8,128)(2,1)S(1)}, u32[]{:S(2)}) copy-start(bf16[8,2,48,128]{3,2,1,0:T(8,128)(2,1)S(1)} %collective-permute-done.6.rest_7_) | copy-start | bytes 589828
  50.5 7.8 %collective-permute-start.10 = (bf16[8,2,48,128]{3,2,1,0:T(8,128)(2,1)S(1)}, bf16[8,2,48,128]{3,2,1,0:T(8,128)(2,1)S(1)}, u32[]{:S(2)}, u32[]{:S(2)}) collective-permute-start(bf16[8,2,48,128]{3,2,1,0:T(8,128)(2,1)S(1)} %collective-permute-done.6.rest_7_), channel_id=1, source_target_pairs={{0,32},{32,2},{2,34},{34,4},{4,36},{36,6},{6,38},{38,0},{1,33},{33... | collective-permute-start | bytes 589832 | tf_op jit(solution)/shard_map/ppermute | solution.py:219
  50.5 11.8 %copy-start.9 = (bf16[8,2,48,128]{3,2,1,0:T(8,128)(2,1)}, bf16[8,2,48,128]{3,2,1,0:T(8,128)(2,1)S(1)}, u32[]{:S(2)}) copy-start(bf16[8,2,48,128]{3,2,1,0:T(8,128)(2,1)S(1)} %collective-permute-done.7.rest_8_) | copy-start | bytes 589828
  50.5 7.8 %collective-permute-start.11 = (bf16[8,2,48,128]{3,2,1,0:T(8,128)(2,1)S(1)}, bf16[8,2,48,128]{3,2,1,0:T(8,128)(2,1)S(1)}, u32[]{:S(2)}, u32[]{:S(2)}) collective-permute-start(bf16[8,2,48,128]{3,2,1,0:T(8,128)(2,1)S(1)} %collective-permute-done.7.rest_8_), channel_id=1, source_target_pairs={{0,38},{32,0},{2,32},{34,2},{4,34},{36,4},{6,36},{38,6},{1,39},{33... | collective-permute-start | bytes 589832 | tf_op jit(solution)/shard_map/ppermute | solution.py:219
  54.4 7.8 %copy-start.10 = (bf16[8,2,48,128]{3,2,1,0:T(8,128)(2,1)}, bf16[8,2,48,128]{3,2,1,0:T(8,128)(2,1)S(1)}, u32[]{:S(2)}) copy-start(bf16[8,2,48,128]{3,2,1,0:T(8,128)(2,1)S(1)} %collective-permute-done.9.rest_10_) | copy-start | bytes 589828
  54.5 7.8 %collective-permute-start.13 = (bf16[8,2,48,128]{3,2,1,0:T(8,128)(2,1)S(1)}, bf16[8,2,48,128]{3,2,1,0:T(8,128)(2,1)S(1)}, u32[]{:S(2)}, u32[]{:S(2)}) collective-permute-start(bf16[8,2,48,128]{3,2,1,0:T(8,128)(2,1)S(1)} %collective-permute-done.9.rest_10_), channel_id=1, source_target_pairs={{0,32},{32,2},{2,34},{34,4},{4,36},{36,6},{6,38},{38,0},{1,33},{33... | collective-permute-start | bytes 589832 | tf_op jit(solution)/shard_map/ppermute | solution.py:219
  54.5 7.8 %copy-start.11 = (bf16[8,2,48,128]{3,2,1,0:T(8,128)(2,1)}, bf16[8,2,48,128]{3,2,1,0:T(8,128)(2,1)S(1)}, u32[]{:S(2)}) copy-start(bf16[8,2,48,128]{3,2,1,0:T(8,128)(2,1)S(1)} %collective-permute-done.12.rest_13_) | copy-start | bytes 589828
  54.5 8.5 %collective-permute-start.14 = (bf16[8,2,48,128]{3,2,1,0:T(8,128)(2,1)S(1)}, bf16[8,2,48,128]{3,2,1,0:T(8,128)(2,1)}, u32[]{:S(2)}, u32[]{:S(2)}) collective-permute-start(bf16[8,2,48,128]{3,2,1,0:T(8,128)(2,1)S(1)} %collective-permute-done.12.rest_13_), channel_id=1, source_target_pairs={{0,38},{32,0},{2,32},{34,2},{4,34},{36,4},{6,36},{38,6},{1,39},{33... | collective-permute-start | bytes 589832 | tf_op jit(solution)/shard_map/ppermute | solution.py:219
  58.3 4.0 %copy-start.12 = (bf16[8,2,48,128]{3,2,1,0:T(8,128)(2,1)}, bf16[8,2,48,128]{3,2,1,0:T(8,128)(2,1)S(1)}, u32[]{:S(2)}) copy-start(bf16[8,2,48,128]{3,2,1,0:T(8,128)(2,1)S(1)} %collective-permute-done.10.rest_11_) | copy-start | bytes 589828
  58.3 4.1 %copy-start.13 = (bf16[8,2,48,128]{3,2,1,0:T(8,128)(2,1)}, bf16[8,2,48,128]{3,2,1,0:T(8,128)(2,1)S(1)}, u32[]{:S(2)}) copy-start(bf16[8,2,48,128]{3,2,1,0:T(8,128)(2,1)S(1)} %collective-permute-done.11.rest_12_) | copy-start | bytes 589828
  62.3 0.7 copy-start.14
  63.0 32.4 %all-to-all-start.2 = ((bf16[32,64,512]{2,1,0:T(8,128)(2,1)}), bf16[32,64,512]{2,1,0:T(8,128)(2,1)}, u32[]{:S(2)}, u32[]{:S(2)}) async-start(bf16[32,64,512]{2,1,0:T(8,128)(2,1)} %bitcast.11), calls=%async_computation.2 | async-start | bytes 4194304 | tf_op jit(solution)/shard_map/all_to_all | solution.py:208
  70.3 8.0 %collective-permute-start.16 = (bf16[16,4,16,1536]{3,2,1,0:T(8,128)(2,1)S(1)}, bf16[16,4,16,1536]{3,2,1,0:T(8,128)(2,1)S(1)}, u32[]{:S(2)}, u32[]{:S(2)}) collective-permute-start(bf16[16,4,16,1536]{3,2,1,0:T(8,128)(2,1)S(1)} %bitcast.9), channel_id=1, source_target_pairs={{0,1},{1,0},{2,3},{3,2},{4,5},{5,4},{6,7},{7,6},{8,9},{9,8},{10,11... | collective-permute-start | bytes 9437192 | tf_op jit(solution)/shard_map/ppermute | solution.py:212
  95.4 9.0 %collective-permute-start.15 = (bf16[32,4,16,512]{3,2,1,0:T(8,128)(2,1)}, bf16[32,4,16,512]{3,2,1,0:T(8,128)(2,1)S(1)}, u32[]{:S(2)}, u32[]{:S(2)}) collective-permute-start(bf16[32,4,16,512]{3,2,1,0:T(8,128)(2,1)} %bitcast.6.t_ref), channel_id=1, source_target_pairs={{0,1},{1,0},{2,3},{3,2},{4,5},{5,4},{6,7},{7,6},{8,9},{9,8},{10,11... | collective-permute-start | bytes 6291464 | tf_op jit(solution)/shard_map/ppermute | solution.py:212
  100.4 4.0 %copy-start = (bf16[4,2,256,512]{3,2,1,0:T(8,128)(2,1)S(1)}, bf16[4,2,256,512]{3,2,1,0:T(8,128)(2,1)}, u32[]{:S(2)}) copy-start(bf16[4,2,256,512]{3,2,1,0:T(8,128)(2,1)} %get-tuple-element.53.v_ref) | copy-start | bytes 6291460

commit v7 on v6

--- a/solution.py
+++ b/solution.py
@@ -14,6 +14,10 @@
 MIB = 1024 * 1024
 
 
+def in_vmem(*arrays):
+    return [pltpu.with_memory_space_constraint(a, pltpu.VMEM) for a in arrays]
+
+
 def in_hbm(*arrays):
     return [pltpu.with_memory_space_constraint(a, pltpu.HBM) for a in arrays]
 
@@ -32,7 +36,7 @@
 def spread(window):
     return pl.pallas_call(
         spread_kernel,
-        out_shape=jax.ShapeDtypeStruct((16, 2, 48, 128), BF16),
+        out_shape=pltpu.VMEM((16, 2, 48, 128), BF16),
         name="spread_window",
     )(*in_hbm(window))
 
@@ -52,9 +56,9 @@
 def join_cores(own, far):
     return pl.pallas_call(
         join_kernel,
-        out_shape=[jax.ShapeDtypeStruct((8, 2, 48, 128), BF16)] * 2,
+        out_shape=[pltpu.VMEM((8, 2, 48, 128), BF16)] * 2,
         name="join_window",
-    )(own, far)
+    )(*in_vmem(own, far))
 
 
 def regroup_kernel(t_ref, out_ref):
@@ -111,7 +115,7 @@
 def build_integrals(own_f, far_f, blocks):
     return pl.pallas_call(
         integrals_kernel,
-        out_shape=[pltpu.HBM((4, 2, 256, 512), BF16)] * 2,
+        out_shape=[pltpu.VMEM((4, 2, 256, 512), BF16)] * 2,
         grid=(4,),
         in_specs=[
             pl.BlockSpec((16, 2, 16, 1536), lambda g: (0, jnp.minimum(g, 1), 0, 0)),
@@ -142,40 +146,6 @@
             out_ref[rows] = total
 
 
-def first_kernel(t_ref, v_ref, out_ref, amps, integrals, sems):
-    copies = []
-    for d in range(4):
-        pair = (
-            pltpu.make_async_copy(t_ref.at[:, d], amps.at[d], sems.at[0, d]),
-            pltpu.make_async_copy(v_ref.at[d], integrals.at[d], sems.at[1, d]),
-        )
-        for copy in pair:
-            copy.start()
-        copies.append(pair)
-    for d, pair in enumerate(copies):
-        for copy in pair:
-            copy.wait()
-        product = dot(integrals[d].reshape(512, 512), amps[d].reshape(512, 512))
-        out_ref[...] = product + out_ref[...] if d else product
-
-
-def first_part(amps, integrals):
-    return pl.pallas_call(
-        first_kernel,
-        out_shape=jax.ShapeDtypeStruct((512, 512), F32),
-        in_specs=[pl.BlockSpec(memory_space=pl.ANY)] * 2,
-        out_specs=pl.BlockSpec(memory_space=pltpu.VMEM),
-        scratch_shapes=[
-            pltpu.VMEM((4, 32, 16, 512), BF16),
-            pltpu.VMEM((4, 2, 256, 512), BF16),
-            pltpu.SemaphoreType.DMA((2, 4)),
-        ],
-        compiler_params=pltpu.CompilerParams(vmem_limit_bytes=16 * MIB),
-        cost_estimate=pl.CostEstimate(flops=100_000_000_000, bytes_accessed=5_000_000, transcendentals=0),
-        name="first_part",
-    )(amps, *in_hbm(integrals))
-
-
 def ladder_part(*operands):
     out_shape = (16, 2, 16, 512) if len(operands) == 3 else (512, 512)
     return pl.pallas_call(
@@ -186,7 +156,7 @@
         compiler_params=pltpu.CompilerParams(vmem_limit_bytes=16 * MIB),
         cost_estimate=pl.CostEstimate(flops=100_000_000_000, bytes_accessed=5_000_000, transcendentals=0),
         name="ladder_part",
-    )(*operands)
+    )(*in_vmem(*operands))
 
 
 def sum_kernel(parts_ref, out_ref):
@@ -199,9 +169,9 @@
 def sum_parts(parts):
     return pl.pallas_call(
         sum_kernel,
-        out_shape=jax.ShapeDtypeStruct((8, 16, 128), F32),
+        out_shape=pltpu.VMEM((8, 16, 128), F32),
         name="sum_parts",
-    )(parts)
+    )(*in_vmem(parts))
 
 
 def exchange(x, axis):
@@ -235,7 +205,7 @@
     own_t, own_f, *blocks = lax.optimization_barrier((own_t, own_f, *blocks))
     amps = exchange(own_t.reshape(32, 64, 512), ROW).reshape(32, 4, 16, 512)
     own_v, far_v = build_integrals(own_f, other(own_f, "core"), blocks)
-    part = first_part(amps, own_v)
+    part = ladder_part(amps, own_v)
     part = ladder_part(other(amps, "core"), far_v, part)
 
     part = sum_parts(exchange(part, PLANE))

time: 138 us -> 136 us (0.986)
  Pallas kernels: 25.4 us -> 19 us
  local copies, waits for them, and re-layouts: 1.46 us -> 5.69 us
  waiting for transfers between devices: 31.3 us -> 27.8 us
  starting transfers between devices: 49.9 us -> 52.1 us
    pallas_call x5 -> x4, Pallas kernels: 20.1 us -> 12.5 us  [the longest x1 10.5 us: build_integrals(): pl.pallas_call(integrals_kernel, out_shape=[pltpu.VMEM((4, 2, 256, 512),...]
    unnamed x30 -> x40, local copies, waits for them, and re-layouts: 0.72 us -> 4.95 us
    all_to_all x3, waiting for transfers between devices: 10.5 us -> 7.29 us  [exchange(): return lax.all_to_all(x, axis, split_axis=0, concat_axis=0, tiled=True)]
    ppermute x3, starting transfers between devices: 9.72 us -> 11.2 us  [other(): return lax.ppermute(x, axis, [(0, 1), (1, 0)])]
  transfers between devices with their start and end apart: 20 -> 20, of which waited for: 12 -> 13; matrix products, arithmetic and copies ran while one was open for 0% -> 0% of each run, Pallas kernels for 15% -> 12%
where the time goes in v7:
time: 136 us; the launch traced here: 135 us
  starting transfers between devices  52.1 us (38%)
  blocking collectives  30.2 us (22%)
  waiting for transfers between devices  27.8 us (20%)
  Pallas kernels  19 us (14%)
  local copies, waits for them, and re-layouts  5.69 us (4%)
    all_to_all x2, blocking collectives, exchange(): return lax.all_to_all(x, axis, split_axis=0, concat_axis=0, tiled=True)  30.2 us
    ppermute x14, starting transfers between devices, shift(): lax.ppermute(x, RING, [(flat(z), flat((z + step) % 8)) for z in range(8)])  21.8 us
    all_to_all x3, starting transfers between devices, exchange(): return lax.all_to_all(x, axis, split_axis=0, concat_axis=0, tiled=True)  19.1 us
    ppermute x14, waiting for transfers between devices, shift(): lax.ppermute(x, RING, [(flat(z), flat((z + step) % 8)) for z in range(8)])  12.7 us
    ppermute x3, starting transfers between devices, other(): return lax.ppermute(x, axis, [(0, 1), (1, 0)])  11.2 us
    pallas_call x1, Pallas kernels, build_integrals(): pl.pallas_call(integrals_kernel, out_shape=[pltpu.VMEM((4, 2, 256, 512),...  10.5 us
    ppermute x3, waiting for transfers between devices, other(): return lax.ppermute(x, axis, [(0, 1), (1, 0)])  7.79 us
    all_to_all x3, waiting for transfers between devices, exchange(): return lax.all_to_all(x, axis, split_axis=0, concat_axis=0, tiled=True)  7.29 us
  transfers between devices with their start and end apart: 20, of which 13 were waited for; matrix products, arithmetic and copies ran while one was open for 0% of the time, Pallas kernels for 12%

profile of v7, /device:TPU:1, one launch (start us, length us, event | category | flops | bytes accessed | tf_op | source)
XLA Modules:
  0.0 135.1 jit_solution(18399656714466673350)
XLA Ops:
  0.0 1.7 %spread_window.1 = bf16[16,2,48,128]{3,2,1,0:T(8,128)(2,1)} custom-call(bf16[4,48,64]{2,1,0:T(8,128)(2,1)} %bitcast.15), custom_call_target="tpu_custom_call" | custom-call | tf_op jit(solution)/shard_map/spread_window/pallas_call | solution.py:37
  1.7 7.6 %all-to-all-start = ((bf16[16,2,48,128]{3,2,1,0:T(8,128)(2,1)}), bf16[16,2,48,128]{3,2,1,0:T(8,128)(2,1)S(1)}, u32[]{:S(2)}, u32[]{:S(2)}) async-start(bf16[16,2,48,128]{3,2,1,0:T(8,128)(2,1)} %spread_window.1), calls=%async_computation | async-start | bytes 786432 | tf_op jit(solution)/shard_map/all_to_all | solution.py:178
  9.3 4.1 %regroup_amplitudes.1 = bf16[4,2,4,4,16,512]{5,4,3,2,1,0:T(8,128)(2,1)} custom-call(bf16[16,64,512]{2,1,0:T(8,128)(2,1)} %bitcast.13), custom_call_target="tpu_custom_call" | custom-call | tf_op jit(solution)/shard_map/regroup_amplitudes/pallas_call | solution.py:74
  13.3 5.1 %all-to-all-done.own_ref = bf16[16,2,48,128]{3,2,1,0:T(8,128)(2,1)S(1)} async-done(((bf16[16,2,48,128]{3,2,1,0:T(8,128)(2,1)}), bf16[16,2,48,128]{3,2,1,0:T(8,128)(2,1)S(1)}, u32[]{:S(2)}, u32[]{:S(2)}) %all-to-all-start) | async-done | bytes 393248 | tf_op jit(solution)/shard_map/all_to_all | solution.py:178
  18.4 4.5 %all-to-all-start.1 = ((bf16[16,64,1536]{2,1,0:T(8,128)(2,1)}), bf16[16,64,1536]{2,1,0:T(8,128)(2,1)}, u32[]{:S(2)}, u32[]{:S(2)}) async-start(bf16[16,64,1536]{2,1,0:T(8,128)(2,1)} %bitcast.12), calls=%async_computation.1 | async-start | bytes 6291456 | tf_op jit(solution)/shard_map/all_to_all | solution.py:178
  22.9 2.0 %collective-permute-start = (bf16[16,2,48,128]{3,2,1,0:T(8,128)(2,1)S(1)}, bf16[16,2,48,128]{3,2,1,0:T(8,128)(2,1)S(1)}, u32[]{:S(2)}, u32[]{:S(2)}) collective-permute-start(bf16[16,2,48,128]{3,2,1,0:T(8,128)(2,1)S(1)} %all-to-all-done.own_ref), channel_id=1, source_target_pairs={{0,1},{1,0},{2,3},{3,2},{4,5},{5,4},{6,7},{7,6},{8,9},{9,8},{10,11... | collective-permute-start | bytes 1179656 | tf_op jit(solution)/shard_map/ppermute | solution.py:182
  24.9 1.3 collective-permute-done.far_ref
  26.2 0.2 join_window.1
  26.4 1.7 %collective-permute-start.1 = (bf16[8,2,48,128]{3,2,1,0:T(8,128)(2,1)S(1)}, bf16[8,2,48,128]{3,2,1,0:T(8,128)(2,1)S(1)}, u32[]{:S(2)}, u32[]{:S(2)}) collective-permute-start(bf16[8,2,48,128]{3,2,1,0:T(8,128)(2,1)S(1)} %get-tuple-element.37.rest_0_), channel_id=1, source_target_pairs={{0,32},{32,2},{2,34},{34,4},{4,36},{36,6},{6,38},{38,0},{1,33},{33... | collective-permute-start | bytes 589832 | tf_op jit(solution)/shard_map/ppermute | solution.py:189
  28.1 4.0 %collective-permute-start.4 = (bf16[8,2,48,128]{3,2,1,0:T(8,128)(2,1)S(1)}, bf16[8,2,48,128]{3,2,1,0:T(8,128)(2,1)S(1)}, u32[]{:S(2)}, u32[]{:S(2)}) collective-permute-start(bf16[8,2,48,128]{3,2,1,0:T(8,128)(2,1)S(1)} %get-tuple-element.38.rest_1_), channel_id=1, source_target_pairs={{0,38},{32,0},{2,32},{34,2},{4,34},{36,4},{6,36},{38,6},{1,39},{33... | collective-permute-start | bytes 589832 | tf_op jit(solution)/shard_map/ppermute | solution.py:189
  32.2 0.0 collective-permute-start.2
  32.2 2.7 %collective-permute-start.3 = (bf16[8,2,48,128]{3,2,1,0:T(8,128)(2,1)S(1)}, bf16[8,2,48,128]{3,2,1,0:T(8,128)(2,1)S(1)}, u32[]{:S(2)}, u32[]{:S(2)}) collective-permute-start(bf16[8,2,48,128]{3,2,1,0:T(8,128)(2,1)S(1)} %get-tuple-element.37.rest_0_), channel_id=1, source_target_pairs={{0,38},{32,0},{2,32},{34,2},{4,34},{36,4},{6,36},{38,6},{1,39},{33... | collective-permute-start | bytes 589832 | tf_op jit(solution)/shard_map/ppermute | solution.py:189
  34.8 2.3 %collective-permute-done.1.rest_2_ = bf16[8,2,48,128]{3,2,1,0:T(8,128)(2,1)S(1)} collective-permute-done((bf16[8,2,48,128]{3,2,1,0:T(8,128)(2,1)S(1)}, bf16[8,2,48,128]{3,2,1,0:T(8,128)(2,1)S(1)}, u32[]{:S(2)}, u32[]{:S(2)}) %collective-permute-start.1) | collective-permute-done | bytes 196640 | tf_op jit(solution)/shard_map/ppermute | solution.py:189
  37.2 2.7 %collective-permute-start.8 = (bf16[8,2,48,128]{3,2,1,0:T(8,128)(2,1)S(1)}, bf16[8,2,48,128]{3,2,1,0:T(8,128)(2,1)S(1)}, u32[]{:S(2)}, u32[]{:S(2)}) collective-permute-start(bf16[8,2,48,128]{3,2,1,0:T(8,128)(2,1)S(1)} %collective-permute-done.4.rest_5_), channel_id=1, source_target_pairs={{0,38},{32,0},{2,32},{34,2},{4,34},{36,4},{6,36},{38,6},{1,39},{33... | collective-permute-start | bytes 589832 | tf_op jit(solution)/shard_map/ppermute | solution.py:189
  39.8 1.5 %collective-permute-done.2.rest_3_ = bf16[8,2,48,128]{3,2,1,0:T(8,128)(2,1)S(1)} collective-permute-done((bf16[8,2,48,128]{3,2,1,0:T(8,128)(2,1)S(1)}, bf16[8,2,48,128]{3,2,1,0:T(8,128)(2,1)S(1)}, u32[]{:S(2)}, u32[]{:S(2)}) %collective-permute-start.2) | collective-permute-done | bytes 196640 | tf_op jit(solution)/shard_map/ppermute | solution.py:189
  41.4 0.0 collective-permute-done.3.rest_4_
  41.4 2.7 %collective-permute-start.7 = (bf16[8,2,48,128]{3,2,1,0:T(8,128)(2,1)S(1)}, bf16[8,2,48,128]{3,2,1,0:T(8,128)(2,1)S(1)}, u32[]{:S(2)}, u32[]{:S(2)}) collective-permute-start(bf16[8,2,48,128]{3,2,1,0:T(8,128)(2,1)S(1)} %collective-permute-done.3.rest_4_), channel_id=1, source_target_pairs={{0,38},{32,0},{2,32},{34,2},{4,34},{36,4},{6,36},{38,6},{1,39},{33... | collective-permute-start | bytes 589832 | tf_op jit(solution)/shard_map/ppermute | solution.py:189
  44.1 0.9 collective-permute-done.5.rest_6_
  45.0 0.0 collective-permute-start.9
  45.0 0.0 collective-permute-done.8.rest_9_
  45.0 2.7 %collective-permute-start.12 = (bf16[8,2,48,128]{3,2,1,0:T(8,128)(2,1)S(1)}, bf16[8,2,48,128]{3,2,1,0:T(8,128)(2,1)S(1)}, u32[]{:S(2)}, u32[]{:S(2)}) collective-permute-start(bf16[8,2,48,128]{3,2,1,0:T(8,128)(2,1)S(1)} %collective-permute-done.8.rest_9_), channel_id=1, source_target_pairs={{0,38},{32,0},{2,32},{34,2},{4,34},{36,4},{6,36},{38,6},{1,39},{33... | collective-permute-start | bytes 589832 | tf_op jit(solution)/shard_map/ppermute | solution.py:189
  47.6 1.5 %collective-permute-done.6.rest_7_ = bf16[8,2,48,128]{3,2,1,0:T(8,128)(2,1)S(1)} collective-permute-done((bf16[8,2,48,128]{3,2,1,0:T(8,128)(2,1)S(1)}, bf16[8,2,48,128]{3,2,1,0:T(8,128)(2,1)S(1)}, u32[]{:S(2)}, u32[]{:S(2)}) %collective-permute-start.6) | collective-permute-done | bytes 196640 | tf_op jit(solution)/shard_map/ppermute | solution.py:189
  49.2 2.7 %collective-permute-start.11 = (bf16[8,2,48,128]{3,2,1,0:T(8,128)(2,1)S(1)}, bf16[8,2,48,128]{3,2,1,0:T(8,128)(2,1)S(1)}, u32[]{:S(2)}, u32[]{:S(2)}) collective-permute-start(bf16[8,2,48,128]{3,2,1,0:T(8,128)(2,1)S(1)} %collective-permute-done.7.rest_8_), channel_id=1, source_target_pairs={{0,38},{32,0},{2,32},{34,2},{4,34},{36,4},{6,36},{38,6},{1,39},{33... | collective-permute-start | bytes 589832 | tf_op jit(solution)/shard_map/ppermute | solution.py:189
  51.9 1.4 %collective-permute-done.9.rest_10_ = bf16[8,2,48,128]{3,2,1,0:T(8,128)(2,1)S(1)} collective-permute-done((bf16[8,2,48,128]{3,2,1,0:T(8,128)(2,1)S(1)}, bf16[8,2,48,128]{3,2,1,0:T(8,128)(2,1)S(1)}, u32[]{:S(2)}, u32[]{:S(2)}) %collective-permute-start.9) | collective-permute-done | bytes 196640 | tf_op jit(solution)/shard_map/ppermute | solution.py:189
  53.3 2.7 %collective-permute-start.14 = (bf16[8,2,48,128]{3,2,1,0:T(8,128)(2,1)S(1)}, bf16[8,2,48,128]{3,2,1,0:T(8,128)(2,1)S(1)}, u32[]{:S(2)}, u32[]{:S(2)}) collective-permute-start(bf16[8,2,48,128]{3,2,1,0:T(8,128)(2,1)S(1)} %collective-permute-done.12.rest_13_), channel_id=1, source_target_pairs={{0,38},{32,0},{2,32},{34,2},{4,34},{36,4},{6,36},{38,6},{1,39},{33... | collective-permute-start | bytes 589832 | tf_op jit(solution)/shard_map/ppermute | solution.py:189
  55.9 1.0 collective-permute-done.10.rest_11_
  57.0 4.0 %collective-permute-done.13.rest_14_ = bf16[8,2,48,128]{3,2,1,0:T(8,128)(2,1)S(1)} collective-permute-done((bf16[8,2,48,128]{3,2,1,0:T(8,128)(2,1)S(1)}, bf16[8,2,48,128]{3,2,1,0:T(8,128)(2,1)S(1)}, u32[]{:S(2)}, u32[]{:S(2)}) %collective-permute-start.13) | collective-permute-done | bytes 196640 | tf_op jit(solution)/shard_map/ppermute | solution.py:189
  61.0 0.1 all-to-all-done.1
  61.1 0.5 copy-done.18
  61.6 0.1 copy-done.19
  61.8 7.0 %all-to-all-start.2 = ((bf16[32,64,512]{2,1,0:T(8,128)(2,1)}), bf16[32,64,512]{2,1,0:T(8,128)(2,1)S(1)}, u32[]{:S(2)}, u32[]{:S(2)}) async-start(bf16[32,64,512]{2,1,0:T(8,128)(2,1)} %bitcast.11), calls=%async_computation.2 | async-start | bytes 4194304 | tf_op jit(solution)/shard_map/all_to_all | solution.py:178
  68.8 3.6 %collective-permute-start.16 = (bf16[16,4,16,1536]{3,2,1,0:T(8,128)(2,1)}, bf16[16,4,16,1536]{3,2,1,0:T(8,128)(2,1)S(1)}, u32[]{:S(2)}, u32[]{:S(2)}) collective-permute-start(bf16[16,4,16,1536]{3,2,1,0:T(8,128)(2,1)} %bitcast.4.own_f), channel_id=1, source_target_pairs={{0,1},{1,0},{2,3},{3,2},{4,5},{5,4},{6,7},{7,6},{8,9},{9,8},{10,11... | collective-permute-start | bytes 9437192 | tf_op jit(solution)/shard_map/ppermute | solution.py:182
  72.4 5.5 %collective-permute-done.16.far_f = bf16[16,4,16,1536]{3,2,1,0:T(8,128)(2,1)S(1)} collective-permute-done((bf16[16,4,16,1536]{3,2,1,0:T(8,128)(2,1)}, bf16[16,4,16,1536]{3,2,1,0:T(8,128)(2,1)S(1)}, u32[]{:S(2)}, u32[]{:S(2)}) %collective-permute-start.16) | collective-permute-done | bytes 3145760 | tf_op jit(solution)/shard_map/ppermute | solution.py:182
  77.9 10.5 %build_integrals.1 = (bf16[4,2,256,512]{3,2,1,0:T(8,128)(2,1)S(1)}, bf16[4,2,256,512]{3,2,1,0:T(8,128)(2,1)S(1)}) custom-call(bf16[16,4,16,1536]{3,2,1,0:T(8,128)(2,1)} %bitcast.4.own_f, bf16[16,4,16,1536]{3,2,1,0:T(8,128)(2,1)S(1)} %collective-permute-done.16.far_f, bf16[8,2,48,128]{3,2,1,0:T(8,128)(2,1)} %copy-done, bf16[8,2,48,128]{3,2,1,0:T(8,128)(2,1)} %copy-done.1, ...), custom_call_target="tpu_custom_call" | custom-call | flops 6499999744 | bytes 14000000 | tf_op jit(solution)/shard_map/build_integrals/pallas_call | solution.py:116
  88.4 1.4 %copy-done.2 = bf16[4,2,256,512]{3,2,1,0:T(8,128)(2,1)} copy-done((bf16[4,2,256,512]{3,2,1,0:T(8,128)(2,1)}, bf16[4,2,256,512]{3,2,1,0:T(8,128)(2,1)S(1)}, u32[]{:S(2)}) %copy-start.2) | copy-done | bytes 2097176
  89.7 1.3 copy-done.4
  91.1 2.1 %all-to-all-done.2 = bf16[32,64,512]{2,1,0:T(8,128)(2,1)S(1)} async-done(((bf16[32,64,512]{2,1,0:T(8,128)(2,1)}), bf16[32,64,512]{2,1,0:T(8,128)(2,1)S(1)}, u32[]{:S(2)}, u32[]{:S(2)}) %all-to-all-start.2) | async-done | bytes 2097184 | tf_op jit(solution)/shard_map/all_to_all | solution.py:178
  93.1 5.7 %collective-permute-start.15 = (bf16[32,4,16,512]{3,2,1,0:T(8,128)(2,1)S(1)}, bf16[32,4,16,512]{3,2,1,0:T(8,128)(2,1)S(1)}, u32[]{:S(2)}, u32[]{:S(2)}) collective-permute-start(bf16[32,4,16,512]{3,2,1,0:T(8,128)(2,1)S(1)} %bitcast.9), channel_id=1, source_target_pairs={{0,1},{1,0},{2,3},{3,2},{4,5},{5,4},{6,7},{7,6},{8,9},{9,8},{10,11... | collective-permute-start | bytes 6291464 | tf_op jit(solution)/shard_map/ppermute | solution.py:182
  98.9 1.6 %copy-done.5 = bf16[4,2,256,512]{3,2,1,0:T(8,128)(2,1)S(1)} copy-done((bf16[4,2,256,512]{3,2,1,0:T(8,128)(2,1)S(1)}, bf16[4,2,256,512]{3,2,1,0:T(8,128)(2,1)}, u32[]{:S(2)}) %copy-start.5) | copy-done | bytes 2097176
  100.5 1.2 ladder_part.2.rest_0_
  101.7 0.9 collective-permute-done.15.t_ref
  102.7 1.2 ladder_part.3
  103.9 13.8 %all_to_all.25.parts_ref = bf16[16,2,16,512]{3,2,1,0:T(8,128)(2,1)S(1)} all-to-all(bf16[16,2,16,512]{3,2,1,0:T(8,128)(2,1)S(1)} %ladder_part.3), channel_id=1, replica_groups=mesh['y'=4,'zl'=2,'x'=4,'zh'=4,'core'=2] {'x','y'}, dimensions={0} | all-to-all | bytes 1048576 | tf_op jit(solution)/shard_map/all_to_all | solution.py:178
  117.7 0.2 sum_parts.1
  117.8 16.5 %all_to_all.26 = f32[8,16,128]{2,1,0:T(8,128)S(1)} all-to-all(f32[8,16,128]{2,1,0:T(8,128)S(1)} %sum_parts.1), channel_id=1, replica_groups=mesh['y'=4,'zl'=2,'x'=4,'zh'=4,'core'=2] {'core','zh'}, dimensions={0} | all-to-all | bytes 131072 | tf_op jit(solution)/shard_map/all_to_all | solution.py:178
  134.3 0.1 reshape.26
  134.4 0.1 reduce_sum.9
  134.5 0.6 copy.4
  (44 shorter events, 0.1 us)
Async XLA Ops:
  1.7 16.8 %all-to-all-start = ((bf16[16,2,48,128]{3,2,1,0:T(8,128)(2,1)}), bf16[16,2,48,128]{3,2,1,0:T(8,128)(2,1)S(1)}, u32[]{:S(2)}, u32[]{:S(2)}) async-start(bf16[16,2,48,128]{3,2,1,0:T(8,128)(2,1)} %spread_window.1), calls=%async_computation | async-start | bytes 786432 | tf_op jit(solution)/shard_map/all_to_all | solution.py:178
  18.4 42.6 %all-to-all-start.1 = ((bf16[16,64,1536]{2,1,0:T(8,128)(2,1)}), bf16[16,64,1536]{2,1,0:T(8,128)(2,1)}, u32[]{:S(2)}, u32[]{:S(2)}) async-start(bf16[16,64,1536]{2,1,0:T(8,128)(2,1)} %bitcast.12), calls=%async_computation.1 | async-start | bytes 6291456 | tf_op jit(solution)/shard_map/all_to_all | solution.py:178
  22.9 3.3 %collective-permute-start = (bf16[16,2,48,128]{3,2,1,0:T(8,128)(2,1)S(1)}, bf16[16,2,48,128]{3,2,1,0:T(8,128)(2,1)S(1)}, u32[]{:S(2)}, u32[]{:S(2)}) collective-permute-start(bf16[16,2,48,128]{3,2,1,0:T(8,128)(2,1)S(1)} %all-to-all-done.own_ref), channel_id=1, source_target_pairs={{0,1},{1,0},{2,3},{3,2},{4,5},{5,4},{6,7},{7,6},{8,9},{9,8},{10,11... | collective-permute-start | bytes 1179656 | tf_op jit(solution)/shard_map/ppermute | solution.py:182
  26.4 35.3 %copy-start = (bf16[8,2,48,128]{3,2,1,0:T(8,128)(2,1)}, bf16[8,2,48,128]{3,2,1,0:T(8,128)(2,1)S(1)}, u32[]{:S(2)}) copy-start(bf16[8,2,48,128]{3,2,1,0:T(8,128)(2,1)S(1)} %get-tuple-element.37.rest_0_) | copy-start | bytes 589828
  26.4 35.3 %copy-start.1 = (bf16[8,2,48,128]{3,2,1,0:T(8,128)(2,1)}, bf16[8,2,48,128]{3,2,1,0:T(8,128)(2,1)S(1)}, u32[]{:S(2)}) copy-start(bf16[8,2,48,128]{3,2,1,0:T(8,128)(2,1)S(1)} %get-tuple-element.38.rest_1_) | copy-start | bytes 589828
  26.4 10.7 %collective-permute-start.1 = (bf16[8,2,48,128]{3,2,1,0:T(8,128)(2,1)S(1)}, bf16[8,2,48,128]{3,2,1,0:T(8,128)(2,1)S(1)}, u32[]{:S(2)}, u32[]{:S(2)}) collective-permute-start(bf16[8,2,48,128]{3,2,1,0:T(8,128)(2,1)S(1)} %get-tuple-element.37.rest_0_), channel_id=1, source_target_pairs={{0,32},{32,2},{2,34},{34,4},{4,36},{36,6},{6,38},{38,0},{1,33},{33... | collective-permute-start | bytes 589832 | tf_op jit(solution)/shard_map/ppermute | solution.py:189
  28.1 9.0 %collective-permute-start.4 = (bf16[8,2,48,128]{3,2,1,0:T(8,128)(2,1)S(1)}, bf16[8,2,48,128]{3,2,1,0:T(8,128)(2,1)S(1)}, u32[]{:S(2)}, u32[]{:S(2)}) collective-permute-start(bf16[8,2,48,128]{3,2,1,0:T(8,128)(2,1)S(1)} %get-tuple-element.38.rest_1_), channel_id=1, source_target_pairs={{0,38},{32,0},{2,32},{34,2},{4,34},{36,4},{6,36},{38,6},{1,39},{33... | collective-permute-start | bytes 589832 | tf_op jit(solution)/shard_map/ppermute | solution.py:189
  32.2 9.2 %collective-permute-start.2 = (bf16[8,2,48,128]{3,2,1,0:T(8,128)(2,1)S(1)}, bf16[8,2,48,128]{3,2,1,0:T(8,128)(2,1)S(1)}, u32[]{:S(2)}, u32[]{:S(2)}) collective-permute-start(bf16[8,2,48,128]{3,2,1,0:T(8,128)(2,1)S(1)} %get-tuple-element.38.rest_1_), channel_id=1, source_target_pairs={{0,32},{32,2},{2,34},{34,4},{4,36},{36,6},{6,38},{38,0},{1,33},{33... | collective-permute-start | bytes 589832 | tf_op jit(solution)/shard_map/ppermute | solution.py:189
  32.2 9.2 %collective-permute-start.3 = (bf16[8,2,48,128]{3,2,1,0:T(8,128)(2,1)S(1)}, bf16[8,2,48,128]{3,2,1,0:T(8,128)(2,1)S(1)}, u32[]{:S(2)}, u32[]{:S(2)}) collective-permute-start(bf16[8,2,48,128]{3,2,1,0:T(8,128)(2,1)S(1)} %get-tuple-element.37.rest_0_), channel_id=1, source_target_pairs={{0,38},{32,0},{2,32},{34,2},{4,34},{36,4},{6,36},{38,6},{1,39},{33... | collective-permute-start | bytes 589832 | tf_op jit(solution)/shard_map/ppermute | solution.py:189
  37.2 24.6 %copy-start.6 = (bf16[8,2,48,128]{3,2,1,0:T(8,128)(2,1)}, bf16[8,2,48,128]{3,2,1,0:T(8,128)(2,1)S(1)}, u32[]{:S(2)}) copy-start(bf16[8,2,48,128]{3,2,1,0:T(8,128)(2,1)S(1)} %collective-permute-done.1.rest_2_) | copy-start | bytes 589828
  37.2 7.8 %collective-permute-start.5 = (bf16[8,2,48,128]{3,2,1,0:T(8,128)(2,1)S(1)}, bf16[8,2,48,128]{3,2,1,0:T(8,128)(2,1)S(1)}, u32[]{:S(2)}, u32[]{:S(2)}) collective-permute-start(bf16[8,2,48,128]{3,2,1,0:T(8,128)(2,1)S(1)} %collective-permute-done.1.rest_2_), channel_id=1, source_target_pairs={{0,32},{32,2},{2,34},{34,4},{4,36},{36,6},{6,38},{38,0},{1,33},{33... | collective-permute-start | bytes 589832 | tf_op jit(solution)/shard_map/ppermute | solution.py:189
  37.2 24.6 %copy-start.7 = (bf16[8,2,48,128]{3,2,1,0:T(8,128)(2,1)}, bf16[8,2,48,128]{3,2,1,0:T(8,128)(2,1)S(1)}, u32[]{:S(2)}) copy-start(bf16[8,2,48,128]{3,2,1,0:T(8,128)(2,1)S(1)} %collective-permute-done.4.rest_5_) | copy-start | bytes 589828
  37.2 7.8 %collective-permute-start.8 = (bf16[8,2,48,128]{3,2,1,0:T(8,128)(2,1)S(1)}, bf16[8,2,48,128]{3,2,1,0:T(8,128)(2,1)S(1)}, u32[]{:S(2)}, u32[]{:S(2)}) collective-permute-start(bf16[8,2,48,128]{3,2,1,0:T(8,128)(2,1)S(1)} %collective-permute-done.4.rest_5_), channel_id=1, source_target_pairs={{0,38},{32,0},{2,32},{34,2},{4,34},{36,4},{6,36},{38,6},{1,39},{33... | collective-permute-start | bytes 589832 | tf_op jit(solution)/shard_map/ppermute | solution.py:189
  41.4 20.4 %copy-start.8 = (bf16[8,2,48,128]{3,2,1,0:T(8,128)(2,1)}, bf16[8,2,48,128]{3,2,1,0:T(8,128)(2,1)S(1)}, u32[]{:S(2)}) copy-start(bf16[8,2,48,128]{3,2,1,0:T(8,128)(2,1)S(1)} %collective-permute-done.2.rest_3_) | copy-start | bytes 589828
  41.4 7.8 %collective-permute-start.6 = (bf16[8,2,48,128]{3,2,1,0:T(8,128)(2,1)S(1)}, bf16[8,2,48,128]{3,2,1,0:T(8,128)(2,1)S(1)}, u32[]{:S(2)}, u32[]{:S(2)}) collective-permute-start(bf16[8,2,48,128]{3,2,1,0:T(8,128)(2,1)S(1)} %collective-permute-done.2.rest_3_), channel_id=1, source_target_pairs={{0,32},{32,2},{2,34},{34,4},{4,36},{36,6},{6,38},{38,0},{1,33},{33... | collective-permute-start | bytes 589832 | tf_op jit(solution)/shard_map/ppermute | solution.py:189
  41.4 20.4 %copy-start.9 = (bf16[8,2,48,128]{3,2,1,0:T(8,128)(2,1)}, bf16[8,2,48,128]{3,2,1,0:T(8,128)(2,1)S(1)}, u32[]{:S(2)}) copy-start(bf16[8,2,48,128]{3,2,1,0:T(8,128)(2,1)S(1)} %collective-permute-done.3.rest_4_) | copy-start | bytes 589828
  41.4 7.8 %collective-permute-start.7 = (bf16[8,2,48,128]{3,2,1,0:T(8,128)(2,1)S(1)}, bf16[8,2,48,128]{3,2,1,0:T(8,128)(2,1)S(1)}, u32[]{:S(2)}, u32[]{:S(2)}) collective-permute-start(bf16[8,2,48,128]{3,2,1,0:T(8,128)(2,1)S(1)} %collective-permute-done.3.rest_4_), channel_id=1, source_target_pairs={{0,38},{32,0},{2,32},{34,2},{4,34},{36,4},{6,36},{38,6},{1,39},{33... | collective-permute-start | bytes 589832 | tf_op jit(solution)/shard_map/ppermute | solution.py:189
  45.0 16.8 %copy-start.10 = (bf16[8,2,48,128]{3,2,1,0:T(8,128)(2,1)}, bf16[8,2,48,128]{3,2,1,0:T(8,128)(2,1)S(1)}, u32[]{:S(2)}) copy-start(bf16[8,2,48,128]{3,2,1,0:T(8,128)(2,1)S(1)} %collective-permute-done.5.rest_6_) | copy-start | bytes 589828
  45.0 8.3 %collective-permute-start.9 = (bf16[8,2,48,128]{3,2,1,0:T(8,128)(2,1)S(1)}, bf16[8,2,48,128]{3,2,1,0:T(8,128)(2,1)S(1)}, u32[]{:S(2)}, u32[]{:S(2)}) collective-permute-start(bf16[8,2,48,128]{3,2,1,0:T(8,128)(2,1)S(1)} %collective-permute-done.5.rest_6_), channel_id=1, source_target_pairs={{0,32},{32,2},{2,34},{34,4},{4,36},{36,6},{6,38},{38,0},{1,33},{33... | collective-permute-start | bytes 589832 | tf_op jit(solution)/shard_map/ppermute | solution.py:189
  45.0 16.1 %copy-start.11 = (bf16[8,2,48,128]{3,2,1,0:T(8,128)(2,1)}, bf16[8,2,48,128]{3,2,1,0:T(8,128)(2,1)S(1)}, u32[]{:S(2)}) copy-start(bf16[8,2,48,128]{3,2,1,0:T(8,128)(2,1)S(1)} %collective-permute-done.8.rest_9_) | copy-start | bytes 589828
  45.0 8.3 %collective-permute-start.12 = (bf16[8,2,48,128]{3,2,1,0:T(8,128)(2,1)S(1)}, bf16[8,2,48,128]{3,2,1,0:T(8,128)(2,1)S(1)}, u32[]{:S(2)}, u32[]{:S(2)}) collective-permute-start(bf16[8,2,48,128]{3,2,1,0:T(8,128)(2,1)S(1)} %collective-permute-done.8.rest_9_), channel_id=1, source_target_pairs={{0,38},{32,0},{2,32},{34,2},{4,34},{36,4},{6,36},{38,6},{1,39},{33... | collective-permute-start | bytes 589832 | tf_op jit(solution)/shard_map/ppermute | solution.py:189
  49.2 11.9 %copy-start.12 = (bf16[8,2,48,128]{3,2,1,0:T(8,128)(2,1)}, bf16[8,2,48,128]{3,2,1,0:T(8,128)(2,1)S(1)}, u32[]{:S(2)}) copy-start(bf16[8,2,48,128]{3,2,1,0:T(8,128)(2,1)S(1)} %collective-permute-done.6.rest_7_) | copy-start | bytes 589828
  49.2 7.8 %collective-permute-start.10 = (bf16[8,2,48,128]{3,2,1,0:T(8,128)(2,1)S(1)}, bf16[8,2,48,128]{3,2,1,0:T(8,128)(2,1)S(1)}, u32[]{:S(2)}, u32[]{:S(2)}) collective-permute-start(bf16[8,2,48,128]{3,2,1,0:T(8,128)(2,1)S(1)} %collective-permute-done.6.rest_7_), channel_id=1, source_target_pairs={{0,32},{32,2},{2,34},{34,4},{4,36},{36,6},{6,38},{38,0},{1,33},{33... | collective-permute-start | bytes 589832 | tf_op jit(solution)/shard_map/ppermute | solution.py:189
  49.2 11.9 %copy-start.13 = (bf16[8,2,48,128]{3,2,1,0:T(8,128)(2,1)}, bf16[8,2,48,128]{3,2,1,0:T(8,128)(2,1)S(1)}, u32[]{:S(2)}) copy-start(bf16[8,2,48,128]{3,2,1,0:T(8,128)(2,1)S(1)} %collective-permute-done.7.rest_8_) | copy-start | bytes 589828
  49.2 7.8 %collective-permute-start.11 = (bf16[8,2,48,128]{3,2,1,0:T(8,128)(2,1)S(1)}, bf16[8,2,48,128]{3,2,1,0:T(8,128)(2,1)S(1)}, u32[]{:S(2)}, u32[]{:S(2)}) collective-permute-start(bf16[8,2,48,128]{3,2,1,0:T(8,128)(2,1)S(1)} %collective-permute-done.7.rest_8_), channel_id=1, source_target_pairs={{0,38},{32,0},{2,32},{34,2},{4,34},{36,4},{6,36},{38,6},{1,39},{33... | collective-permute-start | bytes 589832 | tf_op jit(solution)/shard_map/ppermute | solution.py:189
  53.3 7.8 %copy-start.14 = (bf16[8,2,48,128]{3,2,1,0:T(8,128)(2,1)}, bf16[8,2,48,128]{3,2,1,0:T(8,128)(2,1)S(1)}, u32[]{:S(2)}) copy-start(bf16[8,2,48,128]{3,2,1,0:T(8,128)(2,1)S(1)} %collective-permute-done.9.rest_10_) | copy-start | bytes 589828
  53.3 7.7 %collective-permute-start.13 = (bf16[8,2,48,128]{3,2,1,0:T(8,128)(2,1)S(1)}, bf16[8,2,48,128]{3,2,1,0:T(8,128)(2,1)S(1)}, u32[]{:S(2)}, u32[]{:S(2)}) collective-permute-start(bf16[8,2,48,128]{3,2,1,0:T(8,128)(2,1)S(1)} %collective-permute-done.9.rest_10_), channel_id=1, source_target_pairs={{0,32},{32,2},{2,34},{34,4},{4,36},{36,6},{6,38},{38,0},{1,33},{33... | collective-permute-start | bytes 589832 | tf_op jit(solution)/shard_map/ppermute | solution.py:189
  53.3 7.8 %copy-start.15 = (bf16[8,2,48,128]{3,2,1,0:T(8,128)(2,1)}, bf16[8,2,48,128]{3,2,1,0:T(8,128)(2,1)S(1)}, u32[]{:S(2)}) copy-start(bf16[8,2,48,128]{3,2,1,0:T(8,128)(2,1)S(1)} %collective-permute-done.12.rest_13_) | copy-start | bytes 589828
  53.3 7.7 %collective-permute-start.14 = (bf16[8,2,48,128]{3,2,1,0:T(8,128)(2,1)S(1)}, bf16[8,2,48,128]{3,2,1,0:T(8,128)(2,1)S(1)}, u32[]{:S(2)}, u32[]{:S(2)}) collective-permute-start(bf16[8,2,48,128]{3,2,1,0:T(8,128)(2,1)S(1)} %collective-permute-done.12.rest_13_), channel_id=1, source_target_pairs={{0,38},{32,0},{2,32},{34,2},{4,34},{36,4},{6,36},{38,6},{1,39},{33... | collective-permute-start | bytes 589832 | tf_op jit(solution)/shard_map/ppermute | solution.py:189
  57.0 4.1 %copy-start.16 = (bf16[8,2,48,128]{3,2,1,0:T(8,128)(2,1)}, bf16[8,2,48,128]{3,2,1,0:T(8,128)(2,1)S(1)}, u32[]{:S(2)}) copy-start(bf16[8,2,48,128]{3,2,1,0:T(8,128)(2,1)S(1)} %collective-permute-done.10.rest_11_) | copy-start | bytes 589828
  57.0 4.1 %copy-start.17 = (bf16[8,2,48,128]{3,2,1,0:T(8,128)(2,1)}, bf16[8,2,48,128]{3,2,1,0:T(8,128)(2,1)S(1)}, u32[]{:S(2)}) copy-start(bf16[8,2,48,128]{3,2,1,0:T(8,128)(2,1)S(1)} %collective-permute-done.11.rest_12_) | copy-start | bytes 589828
  61.0 0.7 copy-start.18
  61.0 0.8 copy-start.19
  61.8 31.4 %all-to-all-start.2 = ((bf16[32,64,512]{2,1,0:T(8,128)(2,1)}), bf16[32,64,512]{2,1,0:T(8,128)(2,1)S(1)}, u32[]{:S(2)}, u32[]{:S(2)}) async-start(bf16[32,64,512]{2,1,0:T(8,128)(2,1)} %bitcast.11), calls=%async_computation.2 | async-start | bytes 4194304 | tf_op jit(solution)/shard_map/all_to_all | solution.py:178
  68.8 9.1 %collective-permute-start.16 = (bf16[16,4,16,1536]{3,2,1,0:T(8,128)(2,1)}, bf16[16,4,16,1536]{3,2,1,0:T(8,128)(2,1)S(1)}, u32[]{:S(2)}, u32[]{:S(2)}) collective-permute-start(bf16[16,4,16,1536]{3,2,1,0:T(8,128)(2,1)} %bitcast.4.own_f), channel_id=1, source_target_pairs={{0,1},{1,0},{2,3},{3,2},{4,5},{5,4},{6,7},{7,6},{8,9},{9,8},{10,11... | collective-permute-start | bytes 9437192 | tf_op jit(solution)/shard_map/ppermute | solution.py:182
  88.4 1.4 %copy-start.2 = (bf16[4,2,256,512]{3,2,1,0:T(8,128)(2,1)}, bf16[4,2,256,512]{3,2,1,0:T(8,128)(2,1)S(1)}, u32[]{:S(2)}) copy-start(bf16[4,2,256,512]{3,2,1,0:T(8,128)(2,1)S(1)} %get-tuple-element.53.v_ref) | copy-start | bytes 6291460
  89.7 1.3 copy-start.4
  93.1 9.5 %collective-permute-start.15 = (bf16[32,4,16,512]{3,2,1,0:T(8,128)(2,1)S(1)}, bf16[32,4,16,512]{3,2,1,0:T(8,128)(2,1)S(1)}, u32[]{:S(2)}, u32[]{:S(2)}) collective-permute-start(bf16[32,4,16,512]{3,2,1,0:T(8,128)(2,1)S(1)} %bitcast.9), channel_id=1, source_target_pairs={{0,1},{1,0},{2,3},{3,2},{4,5},{5,4},{6,7},{7,6},{8,9},{9,8},{10,11... | collective-permute-start | bytes 6291464 | tf_op jit(solution)/shard_map/ppermute | solution.py:182
  98.9 1.6 %copy-start.5 = (bf16[4,2,256,512]{3,2,1,0:T(8,128)(2,1)S(1)}, bf16[4,2,256,512]{3,2,1,0:T(8,128)(2,1)}, u32[]{:S(2)}) copy-start(bf16[4,2,256,512]{3,2,1,0:T(8,128)(2,1)} %copy-done.4) | copy-start | bytes 6291460
  100.5 2.2 %copy-start.3 = (bf16[4,2,256,512]{3,2,1,0:T(8,128)(2,1)S(1)}, bf16[4,2,256,512]{3,2,1,0:T(8,128)(2,1)}, u32[]{:S(2)}) copy-start(bf16[4,2,256,512]{3,2,1,0:T(8,128)(2,1)} %copy-done.2) | copy-start | bytes 6291460

commit v8 on v7

--- a/solution.py
+++ b/solution.py
@@ -38,7 +38,7 @@
         spread_kernel,
         out_shape=pltpu.VMEM((16, 2, 48, 128), BF16),
         name="spread_window",
-    )(*in_hbm(window))
+    )(*in_vmem(window))
 
 
 def join_kernel(own_ref, far_ref, *out_refs):
@@ -174,6 +174,21 @@
     )(*in_vmem(parts))
 
 
+def finish_kernel(parts_ref, out_ref):
+    for core in range(2):
+        both = jnp.sum(parts_ref[4 * core : 4 * core + 4], axis=0)
+        out_ref[2 * core] = both[:, :64]
+        out_ref[2 * core + 1] = both[:, 64:]
+
+
+def finish(parts):
+    return pl.pallas_call(
+        finish_kernel,
+        out_shape=jax.ShapeDtypeStruct((4, 16, 64), F32),
+        name="finish",
+    )(*in_vmem(parts))
+
+
 def exchange(x, axis):
     return lax.all_to_all(x, axis, split_axis=0, concat_axis=0, tiled=True)
 
@@ -209,8 +224,7 @@
     part = ladder_part(other(amps, "core"), far_v, part)
 
     part = sum_parts(exchange(part, PLANE))
-    part = exchange(part, ("core", "zh")).reshape(2, 4, 16, 2, 64)
-    return jnp.transpose(jnp.sum(part, axis=1), (3, 0, 2, 1)).reshape(64, 4, 16)
+    return jnp.transpose(finish(exchange(part, ("core", "zh"))), (2, 0, 1))
 
 
 def solution(mesh):

time: 136 us -> 135 us (level)
  transfers between devices with their start and end apart: 20 -> 20, of which waited for: 13 -> 12; matrix products, arithmetic and copies ran while one was open for 0% -> 0% of each run, Pallas kernels for 12% -> 12%
where the time goes in v8:
time: 135 us
  starting transfers between devices  52.1 us (39%)
  blocking collectives  30.4 us (23%)
  waiting for transfers between devices  27.5 us (20%)
  Pallas kernels  18.9 us (14%)
  local copies, waits for them, and re-layouts  5.8 us (4%)
    all_to_all x2, blocking collectives, exchange(): return lax.all_to_all(x, axis, split_axis=0, concat_axis=0, tiled=True)  30.4 us
    ppermute x14, starting transfers between devices, shift(): lax.ppermute(x, RING, [(flat(z), flat((z + step) % 8)) for z in range(8)])  22 us
    all_to_all x3, starting transfers between devices, exchange(): return lax.all_to_all(x, axis, split_axis=0, concat_axis=0, tiled=True)  19.1 us
    ppermute x14, waiting for transfers between devices, shift(): lax.ppermute(x, RING, [(flat(z), flat((z + step) % 8)) for z in range(8)])  12.4 us
    ppermute x3, starting transfers between devices, other(): return lax.ppermute(x, axis, [(0, 1), (1, 0)])  11 us
    pallas_call x1, Pallas kernels, build_integrals(): pl.pallas_call(integrals_kernel, out_shape=[pltpu.VMEM((4, 2, 256, 512),...  10.5 us
    ppermute x3, waiting for transfers between devices, other(): return lax.ppermute(x, axis, [(0, 1), (1, 0)])  7.8 us
    all_to_all x3, waiting for transfers between devices, exchange(): return lax.all_to_all(x, axis, split_axis=0, concat_axis=0, tiled=True)  7.29 us
  transfers between devices with their start and end apart: 20, of which 12 were waited for; matrix products, arithmetic and copies ran while one was open for 0% of the time, Pallas kernels for 12%

profile of v8, /device:TPU:1, one launch (start us, length us, event | category | flops | bytes accessed | tf_op | source)
XLA Modules:
  0.0 134.9 jit_solution(4139733542374832124)
XLA Ops:
  0.0 0.8 copy-done
  0.8 0.9 spread_window.1
  1.7 7.6 %all-to-all-start = ((bf16[16,2,48,128]{3,2,1,0:T(8,128)(2,1)}), bf16[16,2,48,128]{3,2,1,0:T(8,128)(2,1)S(1)}, u32[]{:S(2)}, u32[]{:S(2)}) async-start(bf16[16,2,48,128]{3,2,1,0:T(8,128)(2,1)} %spread_window.1), calls=%async_computation | async-start | bytes 786432 | tf_op jit(solution)/shard_map/all_to_all | solution.py:193
  9.3 4.0 %regroup_amplitudes.1 = bf16[4,2,4,4,16,512]{5,4,3,2,1,0:T(8,128)(2,1)} custom-call(bf16[16,64,512]{2,1,0:T(8,128)(2,1)} %bitcast.13), custom_call_target="tpu_custom_call" | custom-call | tf_op jit(solution)/shard_map/regroup_amplitudes/pallas_call | solution.py:74
  13.3 5.1 %all-to-all-done.own_ref = bf16[16,2,48,128]{3,2,1,0:T(8,128)(2,1)S(1)} async-done(((bf16[16,2,48,128]{3,2,1,0:T(8,128)(2,1)}), bf16[16,2,48,128]{3,2,1,0:T(8,128)(2,1)S(1)}, u32[]{:S(2)}, u32[]{:S(2)}) %all-to-all-start) | async-done | bytes 393248 | tf_op jit(solution)/shard_map/all_to_all | solution.py:193
  18.4 4.5 %all-to-all-start.1 = ((bf16[16,64,1536]{2,1,0:T(8,128)(2,1)}), bf16[16,64,1536]{2,1,0:T(8,128)(2,1)}, u32[]{:S(2)}, u32[]{:S(2)}) async-start(bf16[16,64,1536]{2,1,0:T(8,128)(2,1)} %bitcast.12), calls=%async_computation.1 | async-start | bytes 6291456 | tf_op jit(solution)/shard_map/all_to_all | solution.py:193
  22.9 2.0 %collective-permute-start = (bf16[16,2,48,128]{3,2,1,0:T(8,128)(2,1)S(1)}, bf16[16,2,48,128]{3,2,1,0:T(8,128)(2,1)S(1)}, u32[]{:S(2)}, u32[]{:S(2)}) collective-permute-start(bf16[16,2,48,128]{3,2,1,0:T(8,128)(2,1)S(1)} %all-to-all-done.own_ref), channel_id=1, source_target_pairs={{0,1},{1,0},{2,3},{3,2},{4,5},{5,4},{6,7},{7,6},{8,9},{9,8},{10,11... | collective-permute-start | bytes 1179656 | tf_op jit(solution)/shard_map/ppermute | solution.py:197
  24.9 1.3 %collective-permute-done.far_ref = bf16[16,2,48,128]{3,2,1,0:T(8,128)(2,1)S(1)} collective-permute-done((bf16[16,2,48,128]{3,2,1,0:T(8,128)(2,1)S(1)}, bf16[16,2,48,128]{3,2,1,0:T(8,128)(2,1)S(1)}, u32[]{:S(2)}, u32[]{:S(2)}) %collective-permute-start) | collective-permute-done | bytes 393248 | tf_op jit(solution)/shard_map/ppermute | solution.py:197
  26.2 0.2 join_window.1
  26.4 1.7 %collective-permute-start.1 = (bf16[8,2,48,128]{3,2,1,0:T(8,128)(2,1)S(1)}, bf16[8,2,48,128]{3,2,1,0:T(8,128)(2,1)S(1)}, u32[]{:S(2)}, u32[]{:S(2)}) collective-permute-start(bf16[8,2,48,128]{3,2,1,0:T(8,128)(2,1)S(1)} %get-tuple-element.37.rest_0_), channel_id=1, source_target_pairs={{0,32},{32,2},{2,34},{34,4},{4,36},{36,6},{6,38},{38,0},{1,33},{33... | collective-permute-start | bytes 589832 | tf_op jit(solution)/shard_map/ppermute | solution.py:204
  28.1 4.0 %collective-permute-start.4 = (bf16[8,2,48,128]{3,2,1,0:T(8,128)(2,1)S(1)}, bf16[8,2,48,128]{3,2,1,0:T(8,128)(2,1)S(1)}, u32[]{:S(2)}, u32[]{:S(2)}) collective-permute-start(bf16[8,2,48,128]{3,2,1,0:T(8,128)(2,1)S(1)} %get-tuple-element.38.rest_1_), channel_id=1, source_target_pairs={{0,38},{32,0},{2,32},{34,2},{4,34},{36,4},{6,36},{38,6},{1,39},{33... | collective-permute-start | bytes 589832 | tf_op jit(solution)/shard_map/ppermute | solution.py:204
  32.2 2.7 %collective-permute-start.3 = (bf16[8,2,48,128]{3,2,1,0:T(8,128)(2,1)S(1)}, bf16[8,2,48,128]{3,2,1,0:T(8,128)(2,1)S(1)}, u32[]{:S(2)}, u32[]{:S(2)}) collective-permute-start(bf16[8,2,48,128]{3,2,1,0:T(8,128)(2,1)S(1)} %get-tuple-element.37.rest_0_), channel_id=1, source_target_pairs={{0,38},{32,0},{2,32},{34,2},{4,34},{36,4},{6,36},{38,6},{1,39},{33... | collective-permute-start | bytes 589832 | tf_op jit(solution)/shard_map/ppermute | solution.py:204
  34.8 2.3 %collective-permute-done.1.rest_2_ = bf16[8,2,48,128]{3,2,1,0:T(8,128)(2,1)S(1)} collective-permute-done((bf16[8,2,48,128]{3,2,1,0:T(8,128)(2,1)S(1)}, bf16[8,2,48,128]{3,2,1,0:T(8,128)(2,1)S(1)}, u32[]{:S(2)}, u32[]{:S(2)}) %collective-permute-start.1) | collective-permute-done | bytes 196640 | tf_op jit(solution)/shard_map/ppermute | solution.py:204
  37.2 0.0 collective-permute-start.5
  37.2 0.0 collective-permute-done.4.rest_5_
  37.2 2.7 %collective-permute-start.8 = (bf16[8,2,48,128]{3,2,1,0:T(8,128)(2,1)S(1)}, bf16[8,2,48,128]{3,2,1,0:T(8,128)(2,1)S(1)}, u32[]{:S(2)}, u32[]{:S(2)}) collective-permute-start(bf16[8,2,48,128]{3,2,1,0:T(8,128)(2,1)S(1)} %collective-permute-done.4.rest_5_), channel_id=1, source_target_pairs={{0,38},{32,0},{2,32},{34,2},{4,34},{36,4},{6,36},{38,6},{1,39},{33... | collective-permute-start | bytes 589832 | tf_op jit(solution)/shard_map/ppermute | solution.py:204
  39.8 1.5 %collective-permute-done.2.rest_3_ = bf16[8,2,48,128]{3,2,1,0:T(8,128)(2,1)S(1)} collective-permute-done((bf16[8,2,48,128]{3,2,1,0:T(8,128)(2,1)S(1)}, bf16[8,2,48,128]{3,2,1,0:T(8,128)(2,1)S(1)}, u32[]{:S(2)}, u32[]{:S(2)}) %collective-permute-start.2) | collective-permute-done | bytes 196640 | tf_op jit(solution)/shard_map/ppermute | solution.py:204
  41.4 0.0 collective-permute-start.6
  41.4 0.0 collective-permute-done.3.rest_4_
  41.4 2.7 %collective-permute-start.7 = (bf16[8,2,48,128]{3,2,1,0:T(8,128)(2,1)S(1)}, bf16[8,2,48,128]{3,2,1,0:T(8,128)(2,1)S(1)}, u32[]{:S(2)}, u32[]{:S(2)}) collective-permute-start(bf16[8,2,48,128]{3,2,1,0:T(8,128)(2,1)S(1)} %collective-permute-done.3.rest_4_), channel_id=1, source_target_pairs={{0,38},{32,0},{2,32},{34,2},{4,34},{36,4},{6,36},{38,6},{1,39},{33... | collective-permute-start | bytes 589832 | tf_op jit(solution)/shard_map/ppermute | solution.py:204
  44.1 0.9 collective-permute-done.5.rest_6_
  45.0 2.7 %collective-permute-start.12 = (bf16[8,2,48,128]{3,2,1,0:T(8,128)(2,1)S(1)}, bf16[8,2,48,128]{3,2,1,0:T(8,128)(2,1)S(1)}, u32[]{:S(2)}, u32[]{:S(2)}) collective-permute-start(bf16[8,2,48,128]{3,2,1,0:T(8,128)(2,1)S(1)} %collective-permute-done.8.rest_9_), channel_id=1, source_target_pairs={{0,38},{32,0},{2,32},{34,2},{4,34},{36,4},{6,36},{38,6},{1,39},{33... | collective-permute-start | bytes 589832 | tf_op jit(solution)/shard_map/ppermute | solution.py:204
  47.6 1.5 %collective-permute-done.6.rest_7_ = bf16[8,2,48,128]{3,2,1,0:T(8,128)(2,1)S(1)} collective-permute-done((bf16[8,2,48,128]{3,2,1,0:T(8,128)(2,1)S(1)}, bf16[8,2,48,128]{3,2,1,0:T(8,128)(2,1)S(1)}, u32[]{:S(2)}, u32[]{:S(2)}) %collective-permute-start.6) | collective-permute-done | bytes 196640 | tf_op jit(solution)/shard_map/ppermute | solution.py:204
  49.2 2.7 %collective-permute-start.11 = (bf16[8,2,48,128]{3,2,1,0:T(8,128)(2,1)S(1)}, bf16[8,2,48,128]{3,2,1,0:T(8,128)(2,1)S(1)}, u32[]{:S(2)}, u32[]{:S(2)}) collective-permute-start(bf16[8,2,48,128]{3,2,1,0:T(8,128)(2,1)S(1)} %collective-permute-done.7.rest_8_), channel_id=1, source_target_pairs={{0,38},{32,0},{2,32},{34,2},{4,34},{36,4},{6,36},{38,6},{1,39},{33... | collective-permute-start | bytes 589832 | tf_op jit(solution)/shard_map/ppermute | solution.py:204
  51.9 1.4 %collective-permute-done.9.rest_10_ = bf16[8,2,48,128]{3,2,1,0:T(8,128)(2,1)S(1)} collective-permute-done((bf16[8,2,48,128]{3,2,1,0:T(8,128)(2,1)S(1)}, bf16[8,2,48,128]{3,2,1,0:T(8,128)(2,1)S(1)}, u32[]{:S(2)}, u32[]{:S(2)}) %collective-permute-start.9) | collective-permute-done | bytes 196640 | tf_op jit(solution)/shard_map/ppermute | solution.py:204
  53.3 0.0 collective-permute-done.12.rest_13_
  53.3 2.9 %collective-permute-start.14 = (bf16[8,2,48,128]{3,2,1,0:T(8,128)(2,1)S(1)}, bf16[8,2,48,128]{3,2,1,0:T(8,128)(2,1)}, u32[]{:S(2)}, u32[]{:S(2)}) collective-permute-start(bf16[8,2,48,128]{3,2,1,0:T(8,128)(2,1)S(1)} %collective-permute-done.12.rest_13_), channel_id=1, source_target_pairs={{0,38},{32,0},{2,32},{34,2},{4,34},{36,4},{6,36},{38,6},{1,39},{33... | collective-permute-start | bytes 589832 | tf_op jit(solution)/shard_map/ppermute | solution.py:204
  56.2 0.8 collective-permute-done.10.rest_11_
  57.0 0.0 collective-permute-done.11.rest_12_
  57.0 4.0 %collective-permute-done.13.rest_14_ = bf16[8,2,48,128]{3,2,1,0:T(8,128)(2,1)S(1)} collective-permute-done((bf16[8,2,48,128]{3,2,1,0:T(8,128)(2,1)S(1)}, bf16[8,2,48,128]{3,2,1,0:T(8,128)(2,1)S(1)}, u32[]{:S(2)}, u32[]{:S(2)}) %collective-permute-start.13) | collective-permute-done | bytes 196640 | tf_op jit(solution)/shard_map/ppermute | solution.py:204
  61.0 0.7 copy-done.19
  61.7 0.0 collective-permute-done.14.rest_15_
  61.7 7.0 %all-to-all-start.2 = ((bf16[32,64,512]{2,1,0:T(8,128)(2,1)}), bf16[32,64,512]{2,1,0:T(8,128)(2,1)S(1)}, u32[]{:S(2)}, u32[]{:S(2)}) async-start(bf16[32,64,512]{2,1,0:T(8,128)(2,1)} %bitcast.11), calls=%async_computation.2 | async-start | bytes 4194304 | tf_op jit(solution)/shard_map/all_to_all | solution.py:193
  68.8 3.5 %collective-permute-start.16 = (bf16[16,4,16,1536]{3,2,1,0:T(8,128)(2,1)}, bf16[16,4,16,1536]{3,2,1,0:T(8,128)(2,1)S(1)}, u32[]{:S(2)}, u32[]{:S(2)}) collective-permute-start(bf16[16,4,16,1536]{3,2,1,0:T(8,128)(2,1)} %bitcast.4.own_f), channel_id=1, source_target_pairs={{0,1},{1,0},{2,3},{3,2},{4,5},{5,4},{6,7},{7,6},{8,9},{9,8},{10,11... | collective-permute-start | bytes 9437192 | tf_op jit(solution)/shard_map/ppermute | solution.py:197
  72.3 5.5 %collective-permute-done.16.far_f = bf16[16,4,16,1536]{3,2,1,0:T(8,128)(2,1)S(1)} collective-permute-done((bf16[16,4,16,1536]{3,2,1,0:T(8,128)(2,1)}, bf16[16,4,16,1536]{3,2,1,0:T(8,128)(2,1)S(1)}, u32[]{:S(2)}, u32[]{:S(2)}) %collective-permute-start.16) | collective-permute-done | bytes 3145760 | tf_op jit(solution)/shard_map/ppermute | solution.py:197
  77.8 10.5 %build_integrals.1 = (bf16[4,2,256,512]{3,2,1,0:T(8,128)(2,1)S(1)}, bf16[4,2,256,512]{3,2,1,0:T(8,128)(2,1)S(1)}) custom-call(bf16[16,4,16,1536]{3,2,1,0:T(8,128)(2,1)} %bitcast.4.own_f, bf16[16,4,16,1536]{3,2,1,0:T(8,128)(2,1)S(1)} %collective-permute-done.16.far_f, bf16[8,2,48,128]{3,2,1,0:T(8,128)(2,1)} %copy-done.1, bf16[8,2,48,128]{3,2,1,0:T(8,128)(2,1)} %copy-done.2, ...), custom_call_target="tpu_custom_call" | custom-call | flops 6499999744 | bytes 14000000 | tf_op jit(solution)/shard_map/build_integrals/pallas_call | solution.py:116
  88.3 1.3 copy-done.3
  89.6 1.3 copy-done.5
  91.0 2.2 %all-to-all-done.2 = bf16[32,64,512]{2,1,0:T(8,128)(2,1)S(1)} async-done(((bf16[32,64,512]{2,1,0:T(8,128)(2,1)}), bf16[32,64,512]{2,1,0:T(8,128)(2,1)S(1)}, u32[]{:S(2)}, u32[]{:S(2)}) %all-to-all-start.2) | async-done | bytes 2097184 | tf_op jit(solution)/shard_map/all_to_all | solution.py:193
  93.1 5.5 %collective-permute-start.15 = (bf16[32,4,16,512]{3,2,1,0:T(8,128)(2,1)S(1)}, bf16[32,4,16,512]{3,2,1,0:T(8,128)(2,1)S(1)}, u32[]{:S(2)}, u32[]{:S(2)}) collective-permute-start(bf16[32,4,16,512]{3,2,1,0:T(8,128)(2,1)S(1)} %bitcast.8), channel_id=1, source_target_pairs={{0,1},{1,0},{2,3},{3,2},{4,5},{5,4},{6,7},{7,6},{8,9},{9,8},{10,11... | collective-permute-start | bytes 6291464 | tf_op jit(solution)/shard_map/ppermute | solution.py:197
  98.6 1.6 %copy-done.6 = bf16[4,2,256,512]{3,2,1,0:T(8,128)(2,1)S(1)} copy-done((bf16[4,2,256,512]{3,2,1,0:T(8,128)(2,1)S(1)}, bf16[4,2,256,512]{3,2,1,0:T(8,128)(2,1)}, u32[]{:S(2)}) %copy-start.6) | copy-done | bytes 2097176
  100.2 1.2 ladder_part.2.rest_0_
  101.5 0.9 collective-permute-done.15.t_ref
  102.4 1.2 ladder_part.3
  103.7 14.0 %all_to_all.25.parts_ref = bf16[16,2,16,512]{3,2,1,0:T(8,128)(2,1)S(1)} all-to-all(bf16[16,2,16,512]{3,2,1,0:T(8,128)(2,1)S(1)} %ladder_part.3), channel_id=1, replica_groups=mesh['y'=4,'zl'=2,'x'=4,'zh'=4,'core'=2] {'x','y'}, dimensions={0} | all-to-all | bytes 1048576 | tf_op jit(solution)/shard_map/all_to_all | solution.py:193
  117.7 0.2 sum_parts.1
  117.8 16.4 %all_to_all.26.parts_ref = f32[8,16,128]{2,1,0:T(8,128)S(1)} all-to-all(f32[8,16,128]{2,1,0:T(8,128)S(1)} %sum_parts.1), channel_id=1, replica_groups=mesh['y'=4,'zl'=2,'x'=4,'zh'=4,'core'=2] {'core','zh'}, dimensions={0} | all-to-all | bytes 131072 | tf_op jit(solution)/shard_map/all_to_all | solution.py:193
  134.2 0.7 finish.1
  (42 shorter events, 0.1 us)
Async XLA Ops:
  0.0 0.8 copy-start
  1.7 16.8 %all-to-all-start = ((bf16[16,2,48,128]{3,2,1,0:T(8,128)(2,1)}), bf16[16,2,48,128]{3,2,1,0:T(8,128)(2,1)S(1)}, u32[]{:S(2)}, u32[]{:S(2)}) async-start(bf16[16,2,48,128]{3,2,1,0:T(8,128)(2,1)} %spread_window.1), calls=%async_computation | async-start | bytes 786432 | tf_op jit(solution)/shard_map/all_to_all | solution.py:193
  18.4 43.2 %all-to-all-start.1 = ((bf16[16,64,1536]{2,1,0:T(8,128)(2,1)}), bf16[16,64,1536]{2,1,0:T(8,128)(2,1)}, u32[]{:S(2)}, u32[]{:S(2)}) async-start(bf16[16,64,1536]{2,1,0:T(8,128)(2,1)} %bitcast.12), calls=%async_computation.1 | async-start | bytes 6291456 | tf_op jit(solution)/shard_map/all_to_all | solution.py:193
  22.9 3.3 %collective-permute-start = (bf16[16,2,48,128]{3,2,1,0:T(8,128)(2,1)S(1)}, bf16[16,2,48,128]{3,2,1,0:T(8,128)(2,1)S(1)}, u32[]{:S(2)}, u32[]{:S(2)}) collective-permute-start(bf16[16,2,48,128]{3,2,1,0:T(8,128)(2,1)S(1)} %all-to-all-done.own_ref), channel_id=1, source_target_pairs={{0,1},{1,0},{2,3},{3,2},{4,5},{5,4},{6,7},{7,6},{8,9},{9,8},{10,11... | collective-permute-start | bytes 1179656 | tf_op jit(solution)/shard_map/ppermute | solution.py:197
  26.4 35.3 %copy-start.1 = (bf16[8,2,48,128]{3,2,1,0:T(8,128)(2,1)}, bf16[8,2,48,128]{3,2,1,0:T(8,128)(2,1)S(1)}, u32[]{:S(2)}) copy-start(bf16[8,2,48,128]{3,2,1,0:T(8,128)(2,1)S(1)} %get-tuple-element.37.rest_0_) | copy-start | bytes 589828
  26.4 35.2 %copy-start.2 = (bf16[8,2,48,128]{3,2,1,0:T(8,128)(2,1)}, bf16[8,2,48,128]{3,2,1,0:T(8,128)(2,1)S(1)}, u32[]{:S(2)}) copy-start(bf16[8,2,48,128]{3,2,1,0:T(8,128)(2,1)S(1)} %get-tuple-element.38.rest_1_) | copy-start | bytes 589828
  26.4 10.7 %collective-permute-start.1 = (bf16[8,2,48,128]{3,2,1,0:T(8,128)(2,1)S(1)}, bf16[8,2,48,128]{3,2,1,0:T(8,128)(2,1)S(1)}, u32[]{:S(2)}, u32[]{:S(2)}) collective-permute-start(bf16[8,2,48,128]{3,2,1,0:T(8,128)(2,1)S(1)} %get-tuple-element.37.rest_0_), channel_id=1, source_target_pairs={{0,32},{32,2},{2,34},{34,4},{4,36},{36,6},{6,38},{38,0},{1,33},{33... | collective-permute-start | bytes 589832 | tf_op jit(solution)/shard_map/ppermute | solution.py:204
  28.1 9.0 %collective-permute-start.4 = (bf16[8,2,48,128]{3,2,1,0:T(8,128)(2,1)S(1)}, bf16[8,2,48,128]{3,2,1,0:T(8,128)(2,1)S(1)}, u32[]{:S(2)}, u32[]{:S(2)}) collective-permute-start(bf16[8,2,48,128]{3,2,1,0:T(8,128)(2,1)S(1)} %get-tuple-element.38.rest_1_), channel_id=1, source_target_pairs={{0,38},{32,0},{2,32},{34,2},{4,34},{36,4},{6,36},{38,6},{1,39},{33... | collective-permute-start | bytes 589832 | tf_op jit(solution)/shard_map/ppermute | solution.py:204
  32.2 9.2 %collective-permute-start.2 = (bf16[8,2,48,128]{3,2,1,0:T(8,128)(2,1)S(1)}, bf16[8,2,48,128]{3,2,1,0:T(8,128)(2,1)S(1)}, u32[]{:S(2)}, u32[]{:S(2)}) collective-permute-start(bf16[8,2,48,128]{3,2,1,0:T(8,128)(2,1)S(1)} %get-tuple-element.38.rest_1_), channel_id=1, source_target_pairs={{0,32},{32,2},{2,34},{34,4},{4,36},{36,6},{6,38},{38,0},{1,33},{33... | collective-permute-start | bytes 589832 | tf_op jit(solution)/shard_map/ppermute | solution.py:204
  32.2 9.2 %collective-permute-start.3 = (bf16[8,2,48,128]{3,2,1,0:T(8,128)(2,1)S(1)}, bf16[8,2,48,128]{3,2,1,0:T(8,128)(2,1)S(1)}, u32[]{:S(2)}, u32[]{:S(2)}) collective-permute-start(bf16[8,2,48,128]{3,2,1,0:T(8,128)(2,1)S(1)} %get-tuple-element.37.rest_0_), channel_id=1, source_target_pairs={{0,38},{32,0},{2,32},{34,2},{4,34},{36,4},{6,36},{38,6},{1,39},{33... | collective-permute-start | bytes 589832 | tf_op jit(solution)/shard_map/ppermute | solution.py:204
  37.2 24.5 %copy-start.7 = (bf16[8,2,48,128]{3,2,1,0:T(8,128)(2,1)}, bf16[8,2,48,128]{3,2,1,0:T(8,128)(2,1)S(1)}, u32[]{:S(2)}) copy-start(bf16[8,2,48,128]{3,2,1,0:T(8,128)(2,1)S(1)} %collective-permute-done.1.rest_2_) | copy-start | bytes 589828
  37.2 7.8 %collective-permute-start.5 = (bf16[8,2,48,128]{3,2,1,0:T(8,128)(2,1)S(1)}, bf16[8,2,48,128]{3,2,1,0:T(8,128)(2,1)S(1)}, u32[]{:S(2)}, u32[]{:S(2)}) collective-permute-start(bf16[8,2,48,128]{3,2,1,0:T(8,128)(2,1)S(1)} %collective-permute-done.1.rest_2_), channel_id=1, source_target_pairs={{0,32},{32,2},{2,34},{34,4},{4,36},{36,6},{6,38},{38,0},{1,33},{33... | collective-permute-start | bytes 589832 | tf_op jit(solution)/shard_map/ppermute | solution.py:204
  37.2 24.5 %copy-start.8 = (bf16[8,2,48,128]{3,2,1,0:T(8,128)(2,1)}, bf16[8,2,48,128]{3,2,1,0:T(8,128)(2,1)S(1)}, u32[]{:S(2)}) copy-start(bf16[8,2,48,128]{3,2,1,0:T(8,128)(2,1)S(1)} %collective-permute-done.4.rest_5_) | copy-start | bytes 589828
  37.2 7.8 %collective-permute-start.8 = (bf16[8,2,48,128]{3,2,1,0:T(8,128)(2,1)S(1)}, bf16[8,2,48,128]{3,2,1,0:T(8,128)(2,1)S(1)}, u32[]{:S(2)}, u32[]{:S(2)}) collective-permute-start(bf16[8,2,48,128]{3,2,1,0:T(8,128)(2,1)S(1)} %collective-permute-done.4.rest_5_), channel_id=1, source_target_pairs={{0,38},{32,0},{2,32},{34,2},{4,34},{36,4},{6,36},{38,6},{1,39},{33... | collective-permute-start | bytes 589832 | tf_op jit(solution)/shard_map/ppermute | solution.py:204
  41.4 20.3 %copy-start.9 = (bf16[8,2,48,128]{3,2,1,0:T(8,128)(2,1)}, bf16[8,2,48,128]{3,2,1,0:T(8,128)(2,1)S(1)}, u32[]{:S(2)}) copy-start(bf16[8,2,48,128]{3,2,1,0:T(8,128)(2,1)S(1)} %collective-permute-done.2.rest_3_) | copy-start | bytes 589828
  41.4 7.8 %collective-permute-start.6 = (bf16[8,2,48,128]{3,2,1,0:T(8,128)(2,1)S(1)}, bf16[8,2,48,128]{3,2,1,0:T(8,128)(2,1)S(1)}, u32[]{:S(2)}, u32[]{:S(2)}) collective-permute-start(bf16[8,2,48,128]{3,2,1,0:T(8,128)(2,1)S(1)} %collective-permute-done.2.rest_3_), channel_id=1, source_target_pairs={{0,32},{32,2},{2,34},{34,4},{4,36},{36,6},{6,38},{38,0},{1,33},{33... | collective-permute-start | bytes 589832 | tf_op jit(solution)/shard_map/ppermute | solution.py:204
  41.4 20.3 %copy-start.10 = (bf16[8,2,48,128]{3,2,1,0:T(8,128)(2,1)}, bf16[8,2,48,128]{3,2,1,0:T(8,128)(2,1)S(1)}, u32[]{:S(2)}) copy-start(bf16[8,2,48,128]{3,2,1,0:T(8,128)(2,1)S(1)} %collective-permute-done.3.rest_4_) | copy-start | bytes 589828
  41.4 7.8 %collective-permute-start.7 = (bf16[8,2,48,128]{3,2,1,0:T(8,128)(2,1)S(1)}, bf16[8,2,48,128]{3,2,1,0:T(8,128)(2,1)S(1)}, u32[]{:S(2)}, u32[]{:S(2)}) collective-permute-start(bf16[8,2,48,128]{3,2,1,0:T(8,128)(2,1)S(1)} %collective-permute-done.3.rest_4_), channel_id=1, source_target_pairs={{0,38},{32,0},{2,32},{34,2},{4,34},{36,4},{6,36},{38,6},{1,39},{33... | collective-permute-start | bytes 589832 | tf_op jit(solution)/shard_map/ppermute | solution.py:204
  45.0 16.8 %copy-start.11 = (bf16[8,2,48,128]{3,2,1,0:T(8,128)(2,1)}, bf16[8,2,48,128]{3,2,1,0:T(8,128)(2,1)S(1)}, u32[]{:S(2)}) copy-start(bf16[8,2,48,128]{3,2,1,0:T(8,128)(2,1)S(1)} %collective-permute-done.5.rest_6_) | copy-start | bytes 589828
  45.0 8.3 %collective-permute-start.9 = (bf16[8,2,48,128]{3,2,1,0:T(8,128)(2,1)S(1)}, bf16[8,2,48,128]{3,2,1,0:T(8,128)(2,1)S(1)}, u32[]{:S(2)}, u32[]{:S(2)}) collective-permute-start(bf16[8,2,48,128]{3,2,1,0:T(8,128)(2,1)S(1)} %collective-permute-done.5.rest_6_), channel_id=1, source_target_pairs={{0,32},{32,2},{2,34},{34,4},{4,36},{36,6},{6,38},{38,0},{1,33},{33... | collective-permute-start | bytes 589832 | tf_op jit(solution)/shard_map/ppermute | solution.py:204
  45.0 8.3 %copy-start.12 = (bf16[8,2,48,128]{3,2,1,0:T(8,128)(2,1)}, bf16[8,2,48,128]{3,2,1,0:T(8,128)(2,1)S(1)}, u32[]{:S(2)}) copy-start(bf16[8,2,48,128]{3,2,1,0:T(8,128)(2,1)S(1)} %collective-permute-done.8.rest_9_) | copy-start | bytes 589828
  45.0 8.3 %collective-permute-start.12 = (bf16[8,2,48,128]{3,2,1,0:T(8,128)(2,1)S(1)}, bf16[8,2,48,128]{3,2,1,0:T(8,128)(2,1)S(1)}, u32[]{:S(2)}, u32[]{:S(2)}) collective-permute-start(bf16[8,2,48,128]{3,2,1,0:T(8,128)(2,1)S(1)} %collective-permute-done.8.rest_9_), channel_id=1, source_target_pairs={{0,38},{32,0},{2,32},{34,2},{4,34},{36,4},{6,36},{38,6},{1,39},{33... | collective-permute-start | bytes 589832 | tf_op jit(solution)/shard_map/ppermute | solution.py:204
  49.2 4.1 %copy-start.13 = (bf16[8,2,48,128]{3,2,1,0:T(8,128)(2,1)}, bf16[8,2,48,128]{3,2,1,0:T(8,128)(2,1)S(1)}, u32[]{:S(2)}) copy-start(bf16[8,2,48,128]{3,2,1,0:T(8,128)(2,1)S(1)} %collective-permute-done.6.rest_7_) | copy-start | bytes 589828
  49.2 7.8 %collective-permute-start.10 = (bf16[8,2,48,128]{3,2,1,0:T(8,128)(2,1)S(1)}, bf16[8,2,48,128]{3,2,1,0:T(8,128)(2,1)S(1)}, u32[]{:S(2)}, u32[]{:S(2)}) collective-permute-start(bf16[8,2,48,128]{3,2,1,0:T(8,128)(2,1)S(1)} %collective-permute-done.6.rest_7_), channel_id=1, source_target_pairs={{0,32},{32,2},{2,34},{34,4},{4,36},{36,6},{6,38},{38,0},{1,33},{33... | collective-permute-start | bytes 589832 | tf_op jit(solution)/shard_map/ppermute | solution.py:204
  49.2 7.8 %copy-start.14 = (bf16[8,2,48,128]{3,2,1,0:T(8,128)(2,1)}, bf16[8,2,48,128]{3,2,1,0:T(8,128)(2,1)S(1)}, u32[]{:S(2)}) copy-start(bf16[8,2,48,128]{3,2,1,0:T(8,128)(2,1)S(1)} %collective-permute-done.7.rest_8_) | copy-start | bytes 589828
  49.2 7.8 %collective-permute-start.11 = (bf16[8,2,48,128]{3,2,1,0:T(8,128)(2,1)S(1)}, bf16[8,2,48,128]{3,2,1,0:T(8,128)(2,1)S(1)}, u32[]{:S(2)}, u32[]{:S(2)}) collective-permute-start(bf16[8,2,48,128]{3,2,1,0:T(8,128)(2,1)S(1)} %collective-permute-done.7.rest_8_), channel_id=1, source_target_pairs={{0,38},{32,0},{2,32},{34,2},{4,34},{36,4},{6,36},{38,6},{1,39},{33... | collective-permute-start | bytes 589832 | tf_op jit(solution)/shard_map/ppermute | solution.py:204
  53.3 3.7 %copy-start.15 = (bf16[8,2,48,128]{3,2,1,0:T(8,128)(2,1)}, bf16[8,2,48,128]{3,2,1,0:T(8,128)(2,1)S(1)}, u32[]{:S(2)}) copy-start(bf16[8,2,48,128]{3,2,1,0:T(8,128)(2,1)S(1)} %collective-permute-done.9.rest_10_) | copy-start | bytes 589828
  53.3 7.7 %collective-permute-start.13 = (bf16[8,2,48,128]{3,2,1,0:T(8,128)(2,1)S(1)}, bf16[8,2,48,128]{3,2,1,0:T(8,128)(2,1)S(1)}, u32[]{:S(2)}, u32[]{:S(2)}) collective-permute-start(bf16[8,2,48,128]{3,2,1,0:T(8,128)(2,1)S(1)} %collective-permute-done.9.rest_10_), channel_id=1, source_target_pairs={{0,32},{32,2},{2,34},{34,4},{4,36},{36,6},{6,38},{38,0},{1,33},{33... | collective-permute-start | bytes 589832 | tf_op jit(solution)/shard_map/ppermute | solution.py:204
  53.3 7.7 %copy-start.16 = (bf16[8,2,48,128]{3,2,1,0:T(8,128)(2,1)}, bf16[8,2,48,128]{3,2,1,0:T(8,128)(2,1)S(1)}, u32[]{:S(2)}) copy-start(bf16[8,2,48,128]{3,2,1,0:T(8,128)(2,1)S(1)} %collective-permute-done.12.rest_13_) | copy-start | bytes 589828
  53.3 8.3 %collective-permute-start.14 = (bf16[8,2,48,128]{3,2,1,0:T(8,128)(2,1)S(1)}, bf16[8,2,48,128]{3,2,1,0:T(8,128)(2,1)}, u32[]{:S(2)}, u32[]{:S(2)}) collective-permute-start(bf16[8,2,48,128]{3,2,1,0:T(8,128)(2,1)S(1)} %collective-permute-done.12.rest_13_), channel_id=1, source_target_pairs={{0,38},{32,0},{2,32},{34,2},{4,34},{36,4},{6,36},{38,6},{1,39},{33... | collective-permute-start | bytes 589832 | tf_op jit(solution)/shard_map/ppermute | solution.py:204
  57.0 4.0 %copy-start.17 = (bf16[8,2,48,128]{3,2,1,0:T(8,128)(2,1)}, bf16[8,2,48,128]{3,2,1,0:T(8,128)(2,1)S(1)}, u32[]{:S(2)}) copy-start(bf16[8,2,48,128]{3,2,1,0:T(8,128)(2,1)S(1)} %collective-permute-done.10.rest_11_) | copy-start | bytes 589828
  57.0 4.0 %copy-start.18 = (bf16[8,2,48,128]{3,2,1,0:T(8,128)(2,1)}, bf16[8,2,48,128]{3,2,1,0:T(8,128)(2,1)S(1)}, u32[]{:S(2)}) copy-start(bf16[8,2,48,128]{3,2,1,0:T(8,128)(2,1)S(1)} %collective-permute-done.11.rest_12_) | copy-start | bytes 589828
  61.0 0.7 copy-start.19
  61.7 31.4 %all-to-all-start.2 = ((bf16[32,64,512]{2,1,0:T(8,128)(2,1)}), bf16[32,64,512]{2,1,0:T(8,128)(2,1)S(1)}, u32[]{:S(2)}, u32[]{:S(2)}) async-start(bf16[32,64,512]{2,1,0:T(8,128)(2,1)} %bitcast.11), calls=%async_computation.2 | async-start | bytes 4194304 | tf_op jit(solution)/shard_map/all_to_all | solution.py:193
  68.8 9.0 %collective-permute-start.16 = (bf16[16,4,16,1536]{3,2,1,0:T(8,128)(2,1)}, bf16[16,4,16,1536]{3,2,1,0:T(8,128)(2,1)S(1)}, u32[]{:S(2)}, u32[]{:S(2)}) collective-permute-start(bf16[16,4,16,1536]{3,2,1,0:T(8,128)(2,1)} %bitcast.4.own_f), channel_id=1, source_target_pairs={{0,1},{1,0},{2,3},{3,2},{4,5},{5,4},{6,7},{7,6},{8,9},{9,8},{10,11... | collective-permute-start | bytes 9437192 | tf_op jit(solution)/shard_map/ppermute | solution.py:197
  88.3 1.4 %copy-start.3 = (bf16[4,2,256,512]{3,2,1,0:T(8,128)(2,1)}, bf16[4,2,256,512]{3,2,1,0:T(8,128)(2,1)S(1)}, u32[]{:S(2)}) copy-start(bf16[4,2,256,512]{3,2,1,0:T(8,128)(2,1)S(1)} %get-tuple-element.53.v_ref) | copy-start | bytes 6291460
  89.6 1.3 copy-start.5
  93.1 9.3 %collective-permute-start.15 = (bf16[32,4,16,512]{3,2,1,0:T(8,128)(2,1)S(1)}, bf16[32,4,16,512]{3,2,1,0:T(8,128)(2,1)S(1)}, u32[]{:S(2)}, u32[]{:S(2)}) collective-permute-start(bf16[32,4,16,512]{3,2,1,0:T(8,128)(2,1)S(1)} %bitcast.8), channel_id=1, source_target_pairs={{0,1},{1,0},{2,3},{3,2},{4,5},{5,4},{6,7},{7,6},{8,9},{9,8},{10,11... | collective-permute-start | bytes 6291464 | tf_op jit(solution)/shard_map/ppermute | solution.py:197
  98.6 1.6 %copy-start.6 = (bf16[4,2,256,512]{3,2,1,0:T(8,128)(2,1)S(1)}, bf16[4,2,256,512]{3,2,1,0:T(8,128)(2,1)}, u32[]{:S(2)}) copy-start(bf16[4,2,256,512]{3,2,1,0:T(8,128)(2,1)} %copy-done.5) | copy-start | bytes 6291460
  100.2 2.2 %copy-start.4 = (bf16[4,2,256,512]{3,2,1,0:T(8,128)(2,1)S(1)}, bf16[4,2,256,512]{3,2,1,0:T(8,128)(2,1)}, u32[]{:S(2)}) copy-start(bf16[4,2,256,512]{3,2,1,0:T(8,128)(2,1)} %copy-done.3) | copy-start | bytes 6291460

commit v9 on v8

--- a/solution.py
+++ b/solution.py
@@ -207,8 +207,8 @@
 def per_device(window_factors, factors, amplitudes):
     window = jnp.transpose(window_factors, (0, 2, 1))
     own_w = exchange(spread(window), ("y", "x"))
+    factors, own_w, amplitudes = lax.optimization_barrier((factors, own_w, amplitudes))
     own_t = regroup(jnp.transpose(amplitudes, (1, 2, 0)))
-    factors, own_w, own_t = lax.optimization_barrier((factors, own_w, own_t))
     own_f = exchange(factors.reshape(16, 64, 1536), PLANE).reshape(16, 4, 16, 1536)
 
     up = down = join_cores(own_w, other(own_w, "core"))

time: 135 us -> 134 us (level)
  blocking collectives: 30.4 us -> 46.9 us
  waiting for transfers between devices: 27.5 us -> 18.7 us
  starting transfers between devices: 52.1 us -> 44.4 us
    all_to_all x2 -> x3, blocking collectives: 30.4 us -> 46.9 us  [exchange(): return lax.all_to_all(x, axis, split_axis=0, concat_axis=0, tiled=True)]
    all_to_all x3 -> x2, starting transfers between devices: 19.1 us -> 11.5 us  [exchange(): return lax.all_to_all(x, axis, split_axis=0, concat_axis=0, tiled=True)]
    all_to_all x3 -> x2, waiting for transfers between devices: 7.29 us -> 2.22 us  [exchange(): return lax.all_to_all(x, axis, split_axis=0, concat_axis=0, tiled=True)]
    ppermute x14, waiting for transfers between devices: 12.4 us -> 8.69 us  [shift(): lax.ppermute(x, RING, [(flat(z), flat((z + step) % 8)) for z in range(8)])]
    unnamed x40 -> x42, local copies, waits for them, and re-layouts: 5.8 us -> 5.75 us
  transfers between devices with their start and end apart: 20 -> 19, of which waited for: 12 -> 11; matrix products, arithmetic and copies ran while one was open for 0% -> 0% of each run, Pallas kernels for 12% -> 12%
where the time goes in v9:
time: 134 us
  blocking collectives  46.9 us (35%)
  starting transfers between devices  44.4 us (33%)
  waiting for transfers between devices  18.7 us (14%)
  Pallas kernels  18.1 us (14%)
  local copies, waits for them, and re-layouts  5.75 us (4%)
    all_to_all x3, blocking collectives, exchange(): return lax.all_to_all(x, axis, split_axis=0, concat_axis=0, tiled=True)  46.9 us
    ppermute x14, starting transfers between devices, shift(): lax.ppermute(x, RING, [(flat(z), flat((z + step) % 8)) for z in range(8)])  21.7 us
    all_to_all x2, starting transfers between devices, exchange(): return lax.all_to_all(x, axis, split_axis=0, concat_axis=0, tiled=True)  11.5 us
    ppermute x3, starting transfers between devices, other(): return lax.ppermute(x, axis, [(0, 1), (1, 0)])  11.1 us
    pallas_call x1, Pallas kernels, build_integrals(): pl.pallas_call(integrals_kernel, out_shape=[pltpu.VMEM((4, 2, 256, 512),...  10.5 us
    ppermute x14, waiting for transfers between devices, shift(): lax.ppermute(x, RING, [(flat(z), flat((z + step) % 8)) for z in range(8)])  8.69 us
    ppermute x3, waiting for transfers between devices, other(): return lax.ppermute(x, axis, [(0, 1), (1, 0)])  7.79 us
    unnamed x42, local copies, waits for them, and re-layouts  5.75 us
  transfers between devices with their start and end apart: 19, of which 11 were waited for; matrix products, arithmetic and copies ran while one was open for 0% of the time, Pallas kernels for 12%

profile of v9, /device:TPU:1, one launch (start us, length us, event | category | flops | bytes accessed | tf_op | source)
XLA Modules:
  0.0 134.0 jit_solution(13591137090513215104)
XLA Ops:
  0.0 0.8 copy-done
  0.8 0.1 spread_window.1
  0.9 16.6 %all_to_all.25.own_ref = bf16[16,2,48,128]{3,2,1,0:T(8,128)(2,1)S(1)} all-to-all(bf16[16,2,48,128]{3,2,1,0:T(8,128)(2,1)S(1)} %spread_window.1), channel_id=1, replica_groups=mesh['y'=4,'zl'=2,'x'=4,'zh'=4,'core'=2] {'y','x'}, dimensions={0} | all-to-all | bytes 786432 | tf_op jit(solution)/shard_map/all_to_all | solution.py:193
  17.5 4.5 %all-to-all-start.1 = ((bf16[16,64,1536]{2,1,0:T(8,128)(2,1)}), bf16[16,64,1536]{2,1,0:T(8,128)(2,1)}, u32[]{:S(2)}, u32[]{:S(2)}) async-start(bf16[16,64,1536]{2,1,0:T(8,128)(2,1)} %bitcast.12), calls=%async_computation.1 | async-start | bytes 6291456 | tf_op jit(solution)/shard_map/all_to_all | solution.py:193
  22.0 2.0 %collective-permute-start = (bf16[16,2,48,128]{3,2,1,0:T(8,128)(2,1)S(1)}, bf16[16,2,48,128]{3,2,1,0:T(8,128)(2,1)S(1)}, u32[]{:S(2)}, u32[]{:S(2)}) collective-permute-start(bf16[16,2,48,128]{3,2,1,0:T(8,128)(2,1)S(1)} %all_to_all.25.own_ref), channel_id=1, source_target_pairs={{0,1},{1,0},{2,3},{3,2},{4,5},{5,4},{6,7},{7,6},{8,9},{9,8},{10,11... | collective-permute-start | bytes 1179656 | tf_op jit(solution)/shard_map/ppermute | solution.py:197
  23.9 1.3 %collective-permute-done.far_ref = bf16[16,2,48,128]{3,2,1,0:T(8,128)(2,1)S(1)} collective-permute-done((bf16[16,2,48,128]{3,2,1,0:T(8,128)(2,1)S(1)}, bf16[16,2,48,128]{3,2,1,0:T(8,128)(2,1)S(1)}, u32[]{:S(2)}, u32[]{:S(2)}) %collective-permute-start) | collective-permute-done | bytes 393248 | tf_op jit(solution)/shard_map/ppermute | solution.py:197
  25.3 0.2 join_window.1
  25.5 1.7 %collective-permute-start.1 = (bf16[8,2,48,128]{3,2,1,0:T(8,128)(2,1)S(1)}, bf16[8,2,48,128]{3,2,1,0:T(8,128)(2,1)S(1)}, u32[]{:S(2)}, u32[]{:S(2)}) collective-permute-start(bf16[8,2,48,128]{3,2,1,0:T(8,128)(2,1)S(1)} %get-tuple-element.37.rest_0_), channel_id=1, source_target_pairs={{0,32},{32,2},{2,34},{34,4},{4,36},{36,6},{6,38},{38,0},{1,33},{33... | collective-permute-start | bytes 589832 | tf_op jit(solution)/shard_map/ppermute | solution.py:204
  27.2 4.0 %collective-permute-start.4 = (bf16[8,2,48,128]{3,2,1,0:T(8,128)(2,1)S(1)}, bf16[8,2,48,128]{3,2,1,0:T(8,128)(2,1)S(1)}, u32[]{:S(2)}, u32[]{:S(2)}) collective-permute-start(bf16[8,2,48,128]{3,2,1,0:T(8,128)(2,1)S(1)} %get-tuple-element.38.rest_1_), channel_id=1, source_target_pairs={{0,38},{32,0},{2,32},{34,2},{4,34},{36,4},{6,36},{38,6},{1,39},{33... | collective-permute-start | bytes 589832 | tf_op jit(solution)/shard_map/ppermute | solution.py:204
  31.2 0.0 collective-permute-start.2
  31.2 2.7 %collective-permute-start.3 = (bf16[8,2,48,128]{3,2,1,0:T(8,128)(2,1)S(1)}, bf16[8,2,48,128]{3,2,1,0:T(8,128)(2,1)S(1)}, u32[]{:S(2)}, u32[]{:S(2)}) collective-permute-start(bf16[8,2,48,128]{3,2,1,0:T(8,128)(2,1)S(1)} %get-tuple-element.37.rest_0_), channel_id=1, source_target_pairs={{0,38},{32,0},{2,32},{34,2},{4,34},{36,4},{6,36},{38,6},{1,39},{33... | collective-permute-start | bytes 589832 | tf_op jit(solution)/shard_map/ppermute | solution.py:204
  33.9 2.3 %collective-permute-done.1.rest_2_ = bf16[8,2,48,128]{3,2,1,0:T(8,128)(2,1)S(1)} collective-permute-done((bf16[8,2,48,128]{3,2,1,0:T(8,128)(2,1)S(1)}, bf16[8,2,48,128]{3,2,1,0:T(8,128)(2,1)S(1)}, u32[]{:S(2)}, u32[]{:S(2)}) %collective-permute-start.1) | collective-permute-done | bytes 196640 | tf_op jit(solution)/shard_map/ppermute | solution.py:204
  36.2 0.0 collective-permute-start.5
  36.2 2.7 %collective-permute-start.8 = (bf16[8,2,48,128]{3,2,1,0:T(8,128)(2,1)S(1)}, bf16[8,2,48,128]{3,2,1,0:T(8,128)(2,1)S(1)}, u32[]{:S(2)}, u32[]{:S(2)}) collective-permute-start(bf16[8,2,48,128]{3,2,1,0:T(8,128)(2,1)S(1)} %collective-permute-done.4.rest_5_), channel_id=1, source_target_pairs={{0,38},{32,0},{2,32},{34,2},{4,34},{36,4},{6,36},{38,6},{1,39},{33... | collective-permute-start | bytes 589832 | tf_op jit(solution)/shard_map/ppermute | solution.py:204
  38.9 1.5 %collective-permute-done.2.rest_3_ = bf16[8,2,48,128]{3,2,1,0:T(8,128)(2,1)S(1)} collective-permute-done((bf16[8,2,48,128]{3,2,1,0:T(8,128)(2,1)S(1)}, bf16[8,2,48,128]{3,2,1,0:T(8,128)(2,1)S(1)}, u32[]{:S(2)}, u32[]{:S(2)}) %collective-permute-start.2) | collective-permute-done | bytes 196640 | tf_op jit(solution)/shard_map/ppermute | solution.py:204
  40.4 2.7 %collective-permute-start.7 = (bf16[8,2,48,128]{3,2,1,0:T(8,128)(2,1)S(1)}, bf16[8,2,48,128]{3,2,1,0:T(8,128)(2,1)S(1)}, u32[]{:S(2)}, u32[]{:S(2)}) collective-permute-start(bf16[8,2,48,128]{3,2,1,0:T(8,128)(2,1)S(1)} %collective-permute-done.3.rest_4_), channel_id=1, source_target_pairs={{0,38},{32,0},{2,32},{34,2},{4,34},{36,4},{6,36},{38,6},{1,39},{33... | collective-permute-start | bytes 589832 | tf_op jit(solution)/shard_map/ppermute | solution.py:204
  43.1 0.9 collective-permute-done.5.rest_6_
  44.0 2.7 %collective-permute-start.12 = (bf16[8,2,48,128]{3,2,1,0:T(8,128)(2,1)S(1)}, bf16[8,2,48,128]{3,2,1,0:T(8,128)(2,1)S(1)}, u32[]{:S(2)}, u32[]{:S(2)}) collective-permute-start(bf16[8,2,48,128]{3,2,1,0:T(8,128)(2,1)S(1)} %collective-permute-done.8.rest_9_), channel_id=1, source_target_pairs={{0,38},{32,0},{2,32},{34,2},{4,34},{36,4},{6,36},{38,6},{1,39},{33... | collective-permute-start | bytes 589832 | tf_op jit(solution)/shard_map/ppermute | solution.py:204
  46.7 1.5 %collective-permute-done.6.rest_7_ = bf16[8,2,48,128]{3,2,1,0:T(8,128)(2,1)S(1)} collective-permute-done((bf16[8,2,48,128]{3,2,1,0:T(8,128)(2,1)S(1)}, bf16[8,2,48,128]{3,2,1,0:T(8,128)(2,1)S(1)}, u32[]{:S(2)}, u32[]{:S(2)}) %collective-permute-start.6) | collective-permute-done | bytes 196640 | tf_op jit(solution)/shard_map/ppermute | solution.py:204
  48.2 0.0 collective-permute-done.7.rest_8_
  48.2 2.7 %collective-permute-start.11 = (bf16[8,2,48,128]{3,2,1,0:T(8,128)(2,1)S(1)}, bf16[8,2,48,128]{3,2,1,0:T(8,128)(2,1)S(1)}, u32[]{:S(2)}, u32[]{:S(2)}) collective-permute-start(bf16[8,2,48,128]{3,2,1,0:T(8,128)(2,1)S(1)} %collective-permute-done.7.rest_8_), channel_id=1, source_target_pairs={{0,38},{32,0},{2,32},{34,2},{4,34},{36,4},{6,36},{38,6},{1,39},{33... | collective-permute-start | bytes 589832 | tf_op jit(solution)/shard_map/ppermute | solution.py:204
  50.9 1.4 %collective-permute-done.9.rest_10_ = bf16[8,2,48,128]{3,2,1,0:T(8,128)(2,1)S(1)} collective-permute-done((bf16[8,2,48,128]{3,2,1,0:T(8,128)(2,1)S(1)}, bf16[8,2,48,128]{3,2,1,0:T(8,128)(2,1)S(1)}, u32[]{:S(2)}, u32[]{:S(2)}) %collective-permute-start.9) | collective-permute-done | bytes 196640 | tf_op jit(solution)/shard_map/ppermute | solution.py:204
  52.3 0.0 collective-permute-done.12.rest_13_
  52.3 2.7 %collective-permute-start.14 = (bf16[8,2,48,128]{3,2,1,0:T(8,128)(2,1)S(1)}, bf16[8,2,48,128]{3,2,1,0:T(8,128)(2,1)S(1)}, u32[]{:S(2)}, u32[]{:S(2)}) collective-permute-start(bf16[8,2,48,128]{3,2,1,0:T(8,128)(2,1)S(1)} %collective-permute-done.12.rest_13_), channel_id=1, source_target_pairs={{0,38},{32,0},{2,32},{34,2},{4,34},{36,4},{6,36},{38,6},{1,39},{33... | collective-permute-start | bytes 589832 | tf_op jit(solution)/shard_map/ppermute | solution.py:204
  55.0 4.0 %regroup_amplitudes.1 = bf16[4,2,4,4,16,512]{5,4,3,2,1,0:T(8,128)(2,1)} custom-call(bf16[16,64,512]{2,1,0:T(8,128)(2,1)} %bitcast.13), custom_call_target="tpu_custom_call" | custom-call | tf_op jit(solution)/shard_map/regroup_amplitudes/pallas_call | solution.py:74
  59.0 0.0 collective-permute-done.10.rest_11_
  59.0 0.0 collective-permute-done.11.rest_12_
  59.0 1.0 collective-permute-done.13.rest_14_
  60.0 0.0 collective-permute-done.14.rest_15_
  60.0 0.1 all-to-all-done.1
  60.2 0.5 copy-done.19
  60.7 0.1 copy-done.20
  60.8 7.0 %all-to-all-start.2 = ((bf16[32,64,512]{2,1,0:T(8,128)(2,1)}), bf16[32,64,512]{2,1,0:T(8,128)(2,1)S(1)}, u32[]{:S(2)}, u32[]{:S(2)}) async-start(bf16[32,64,512]{2,1,0:T(8,128)(2,1)} %bitcast.11), calls=%async_computation.2 | async-start | bytes 4194304 | tf_op jit(solution)/shard_map/all_to_all | solution.py:193
  67.9 3.5 %collective-permute-start.16 = (bf16[16,4,16,1536]{3,2,1,0:T(8,128)(2,1)}, bf16[16,4,16,1536]{3,2,1,0:T(8,128)(2,1)S(1)}, u32[]{:S(2)}, u32[]{:S(2)}) collective-permute-start(bf16[16,4,16,1536]{3,2,1,0:T(8,128)(2,1)} %bitcast.4.own_f), channel_id=1, source_target_pairs={{0,1},{1,0},{2,3},{3,2},{4,5},{5,4},{6,7},{7,6},{8,9},{9,8},{10,11... | collective-permute-start | bytes 9437192 | tf_op jit(solution)/shard_map/ppermute | solution.py:197
  71.4 5.5 %collective-permute-done.16.far_f = bf16[16,4,16,1536]{3,2,1,0:T(8,128)(2,1)S(1)} collective-permute-done((bf16[16,4,16,1536]{3,2,1,0:T(8,128)(2,1)}, bf16[16,4,16,1536]{3,2,1,0:T(8,128)(2,1)S(1)}, u32[]{:S(2)}, u32[]{:S(2)}) %collective-permute-start.16) | collective-permute-done | bytes 3145760 | tf_op jit(solution)/shard_map/ppermute | solution.py:197
  76.9 10.5 %build_integrals.1 = (bf16[4,2,256,512]{3,2,1,0:T(8,128)(2,1)S(1)}, bf16[4,2,256,512]{3,2,1,0:T(8,128)(2,1)S(1)}) custom-call(bf16[16,4,16,1536]{3,2,1,0:T(8,128)(2,1)} %bitcast.4.own_f, bf16[16,4,16,1536]{3,2,1,0:T(8,128)(2,1)S(1)} %collective-permute-done.16.far_f, bf16[8,2,48,128]{3,2,1,0:T(8,128)(2,1)} %copy-done.1, bf16[8,2,48,128]{3,2,1,0:T(8,128)(2,1)} %copy-done.2, ...), custom_call_target="tpu_custom_call" | custom-call | flops 6499999744 | bytes 14000000 | tf_op jit(solution)/shard_map/build_integrals/pallas_call | solution.py:116
  87.4 1.4 %copy-done.3 = bf16[4,2,256,512]{3,2,1,0:T(8,128)(2,1)} copy-done((bf16[4,2,256,512]{3,2,1,0:T(8,128)(2,1)}, bf16[4,2,256,512]{3,2,1,0:T(8,128)(2,1)S(1)}, u32[]{:S(2)}) %copy-start.3) | copy-done | bytes 2097176
  88.8 1.3 copy-done.5
  90.1 2.1 %all-to-all-done.2 = bf16[32,64,512]{2,1,0:T(8,128)(2,1)S(1)} async-done(((bf16[32,64,512]{2,1,0:T(8,128)(2,1)}), bf16[32,64,512]{2,1,0:T(8,128)(2,1)S(1)}, u32[]{:S(2)}, u32[]{:S(2)}) %all-to-all-start.2) | async-done | bytes 2097184 | tf_op jit(solution)/shard_map/all_to_all | solution.py:193
  92.2 5.6 %collective-permute-start.15 = (bf16[32,4,16,512]{3,2,1,0:T(8,128)(2,1)S(1)}, bf16[32,4,16,512]{3,2,1,0:T(8,128)(2,1)S(1)}, u32[]{:S(2)}, u32[]{:S(2)}) collective-permute-start(bf16[32,4,16,512]{3,2,1,0:T(8,128)(2,1)S(1)} %bitcast.8), channel_id=1, source_target_pairs={{0,1},{1,0},{2,3},{3,2},{4,5},{5,4},{6,7},{7,6},{8,9},{9,8},{10,11... | collective-permute-start | bytes 6291464 | tf_op jit(solution)/shard_map/ppermute | solution.py:197
  97.8 1.6 %copy-done.6 = bf16[4,2,256,512]{3,2,1,0:T(8,128)(2,1)S(1)} copy-done((bf16[4,2,256,512]{3,2,1,0:T(8,128)(2,1)S(1)}, bf16[4,2,256,512]{3,2,1,0:T(8,128)(2,1)}, u32[]{:S(2)}) %copy-start.6) | copy-done | bytes 2097176
  99.4 1.2 ladder_part.2.rest_0_
  100.7 0.9 collective-permute-done.15.t_ref
  101.6 1.2 ladder_part.3
  102.9 13.8 %all_to_all.26.parts_ref = bf16[16,2,16,512]{3,2,1,0:T(8,128)(2,1)S(1)} all-to-all(bf16[16,2,16,512]{3,2,1,0:T(8,128)(2,1)S(1)} %ladder_part.3), channel_id=1, replica_groups=mesh['y'=4,'zl'=2,'x'=4,'zh'=4,'core'=2] {'x','y'}, dimensions={0} | all-to-all | bytes 1048576 | tf_op jit(solution)/shard_map/all_to_all | solution.py:193
  116.7 0.2 sum_parts.1
  116.9 16.5 %all_to_all.27.parts_ref = f32[8,16,128]{2,1,0:T(8,128)S(1)} all-to-all(f32[8,16,128]{2,1,0:T(8,128)S(1)} %sum_parts.1), channel_id=1, replica_groups=mesh['y'=4,'zl'=2,'x'=4,'zh'=4,'core'=2] {'core','zh'}, dimensions={0} | all-to-all | bytes 131072 | tf_op jit(solution)/shard_map/all_to_all | solution.py:193
  133.3 0.7 finish.1
  (43 shorter events, 0.1 us)
Async XLA Ops:
  0.0 0.8 copy-start
  17.5 42.6 %all-to-all-start.1 = ((bf16[16,64,1536]{2,1,0:T(8,128)(2,1)}), bf16[16,64,1536]{2,1,0:T(8,128)(2,1)}, u32[]{:S(2)}, u32[]{:S(2)}) async-start(bf16[16,64,1536]{2,1,0:T(8,128)(2,1)} %bitcast.12), calls=%async_computation.1 | async-start | bytes 6291456 | tf_op jit(solution)/shard_map/all_to_all | solution.py:193
  22.0 3.3 %collective-permute-start = (bf16[16,2,48,128]{3,2,1,0:T(8,128)(2,1)S(1)}, bf16[16,2,48,128]{3,2,1,0:T(8,128)(2,1)S(1)}, u32[]{:S(2)}, u32[]{:S(2)}) collective-permute-start(bf16[16,2,48,128]{3,2,1,0:T(8,128)(2,1)S(1)} %all_to_all.25.own_ref), channel_id=1, source_target_pairs={{0,1},{1,0},{2,3},{3,2},{4,5},{5,4},{6,7},{7,6},{8,9},{9,8},{10,11... | collective-permute-start | bytes 1179656 | tf_op jit(solution)/shard_map/ppermute | solution.py:197
  25.5 35.3 %copy-start.1 = (bf16[8,2,48,128]{3,2,1,0:T(8,128)(2,1)}, bf16[8,2,48,128]{3,2,1,0:T(8,128)(2,1)S(1)}, u32[]{:S(2)}) copy-start(bf16[8,2,48,128]{3,2,1,0:T(8,128)(2,1)S(1)} %get-tuple-element.37.rest_0_) | copy-start | bytes 589828
  25.5 35.3 %copy-start.2 = (bf16[8,2,48,128]{3,2,1,0:T(8,128)(2,1)}, bf16[8,2,48,128]{3,2,1,0:T(8,128)(2,1)S(1)}, u32[]{:S(2)}) copy-start(bf16[8,2,48,128]{3,2,1,0:T(8,128)(2,1)S(1)} %get-tuple-element.38.rest_1_) | copy-start | bytes 589828
  25.5 10.7 %collective-permute-start.1 = (bf16[8,2,48,128]{3,2,1,0:T(8,128)(2,1)S(1)}, bf16[8,2,48,128]{3,2,1,0:T(8,128)(2,1)S(1)}, u32[]{:S(2)}, u32[]{:S(2)}) collective-permute-start(bf16[8,2,48,128]{3,2,1,0:T(8,128)(2,1)S(1)} %get-tuple-element.37.rest_0_), channel_id=1, source_target_pairs={{0,32},{32,2},{2,34},{34,4},{4,36},{36,6},{6,38},{38,0},{1,33},{33... | collective-permute-start | bytes 589832 | tf_op jit(solution)/shard_map/ppermute | solution.py:204
  27.2 9.0 %collective-permute-start.4 = (bf16[8,2,48,128]{3,2,1,0:T(8,128)(2,1)S(1)}, bf16[8,2,48,128]{3,2,1,0:T(8,128)(2,1)S(1)}, u32[]{:S(2)}, u32[]{:S(2)}) collective-permute-start(bf16[8,2,48,128]{3,2,1,0:T(8,128)(2,1)S(1)} %get-tuple-element.38.rest_1_), channel_id=1, source_target_pairs={{0,38},{32,0},{2,32},{34,2},{4,34},{36,4},{6,36},{38,6},{1,39},{33... | collective-permute-start | bytes 589832 | tf_op jit(solution)/shard_map/ppermute | solution.py:204
  31.2 9.2 %collective-permute-start.2 = (bf16[8,2,48,128]{3,2,1,0:T(8,128)(2,1)S(1)}, bf16[8,2,48,128]{3,2,1,0:T(8,128)(2,1)S(1)}, u32[]{:S(2)}, u32[]{:S(2)}) collective-permute-start(bf16[8,2,48,128]{3,2,1,0:T(8,128)(2,1)S(1)} %get-tuple-element.38.rest_1_), channel_id=1, source_target_pairs={{0,32},{32,2},{2,34},{34,4},{4,36},{36,6},{6,38},{38,0},{1,33},{33... | collective-permute-start | bytes 589832 | tf_op jit(solution)/shard_map/ppermute | solution.py:204
  31.2 9.2 %collective-permute-start.3 = (bf16[8,2,48,128]{3,2,1,0:T(8,128)(2,1)S(1)}, bf16[8,2,48,128]{3,2,1,0:T(8,128)(2,1)S(1)}, u32[]{:S(2)}, u32[]{:S(2)}) collective-permute-start(bf16[8,2,48,128]{3,2,1,0:T(8,128)(2,1)S(1)} %get-tuple-element.37.rest_0_), channel_id=1, source_target_pairs={{0,38},{32,0},{2,32},{34,2},{4,34},{36,4},{6,36},{38,6},{1,39},{33... | collective-permute-start | bytes 589832 | tf_op jit(solution)/shard_map/ppermute | solution.py:204
  36.2 24.6 %copy-start.7 = (bf16[8,2,48,128]{3,2,1,0:T(8,128)(2,1)}, bf16[8,2,48,128]{3,2,1,0:T(8,128)(2,1)S(1)}, u32[]{:S(2)}) copy-start(bf16[8,2,48,128]{3,2,1,0:T(8,128)(2,1)S(1)} %collective-permute-done.1.rest_2_) | copy-start | bytes 589828
  36.2 7.8 %collective-permute-start.5 = (bf16[8,2,48,128]{3,2,1,0:T(8,128)(2,1)S(1)}, bf16[8,2,48,128]{3,2,1,0:T(8,128)(2,1)S(1)}, u32[]{:S(2)}, u32[]{:S(2)}) collective-permute-start(bf16[8,2,48,128]{3,2,1,0:T(8,128)(2,1)S(1)} %collective-permute-done.1.rest_2_), channel_id=1, source_target_pairs={{0,32},{32,2},{2,34},{34,4},{4,36},{36,6},{6,38},{38,0},{1,33},{33... | collective-permute-start | bytes 589832 | tf_op jit(solution)/shard_map/ppermute | solution.py:204
  36.2 24.6 %copy-start.8 = (bf16[8,2,48,128]{3,2,1,0:T(8,128)(2,1)}, bf16[8,2,48,128]{3,2,1,0:T(8,128)(2,1)S(1)}, u32[]{:S(2)}) copy-start(bf16[8,2,48,128]{3,2,1,0:T(8,128)(2,1)S(1)} %collective-permute-done.4.rest_5_) | copy-start | bytes 589828
  36.2 7.8 %collective-permute-start.8 = (bf16[8,2,48,128]{3,2,1,0:T(8,128)(2,1)S(1)}, bf16[8,2,48,128]{3,2,1,0:T(8,128)(2,1)S(1)}, u32[]{:S(2)}, u32[]{:S(2)}) collective-permute-start(bf16[8,2,48,128]{3,2,1,0:T(8,128)(2,1)S(1)} %collective-permute-done.4.rest_5_), channel_id=1, source_target_pairs={{0,38},{32,0},{2,32},{34,2},{4,34},{36,4},{6,36},{38,6},{1,39},{33... | collective-permute-start | bytes 589832 | tf_op jit(solution)/shard_map/ppermute | solution.py:204
  40.4 20.4 %copy-start.9 = (bf16[8,2,48,128]{3,2,1,0:T(8,128)(2,1)}, bf16[8,2,48,128]{3,2,1,0:T(8,128)(2,1)S(1)}, u32[]{:S(2)}) copy-start(bf16[8,2,48,128]{3,2,1,0:T(8,128)(2,1)S(1)} %collective-permute-done.2.rest_3_) | copy-start | bytes 589828
  40.4 7.8 %collective-permute-start.6 = (bf16[8,2,48,128]{3,2,1,0:T(8,128)(2,1)S(1)}, bf16[8,2,48,128]{3,2,1,0:T(8,128)(2,1)S(1)}, u32[]{:S(2)}, u32[]{:S(2)}) collective-permute-start(bf16[8,2,48,128]{3,2,1,0:T(8,128)(2,1)S(1)} %collective-permute-done.2.rest_3_), channel_id=1, source_target_pairs={{0,32},{32,2},{2,34},{34,4},{4,36},{36,6},{6,38},{38,0},{1,33},{33... | collective-permute-start | bytes 589832 | tf_op jit(solution)/shard_map/ppermute | solution.py:204
  40.4 20.4 %copy-start.10 = (bf16[8,2,48,128]{3,2,1,0:T(8,128)(2,1)}, bf16[8,2,48,128]{3,2,1,0:T(8,128)(2,1)S(1)}, u32[]{:S(2)}) copy-start(bf16[8,2,48,128]{3,2,1,0:T(8,128)(2,1)S(1)} %collective-permute-done.3.rest_4_) | copy-start | bytes 589828
  40.4 7.8 %collective-permute-start.7 = (bf16[8,2,48,128]{3,2,1,0:T(8,128)(2,1)S(1)}, bf16[8,2,48,128]{3,2,1,0:T(8,128)(2,1)S(1)}, u32[]{:S(2)}, u32[]{:S(2)}) collective-permute-start(bf16[8,2,48,128]{3,2,1,0:T(8,128)(2,1)S(1)} %collective-permute-done.3.rest_4_), channel_id=1, source_target_pairs={{0,38},{32,0},{2,32},{34,2},{4,34},{36,4},{6,36},{38,6},{1,39},{33... | collective-permute-start | bytes 589832 | tf_op jit(solution)/shard_map/ppermute | solution.py:204
  44.0 16.8 %copy-start.11 = (bf16[8,2,48,128]{3,2,1,0:T(8,128)(2,1)}, bf16[8,2,48,128]{3,2,1,0:T(8,128)(2,1)S(1)}, u32[]{:S(2)}) copy-start(bf16[8,2,48,128]{3,2,1,0:T(8,128)(2,1)S(1)} %collective-permute-done.5.rest_6_) | copy-start | bytes 589828
  44.0 8.3 %collective-permute-start.9 = (bf16[8,2,48,128]{3,2,1,0:T(8,128)(2,1)S(1)}, bf16[8,2,48,128]{3,2,1,0:T(8,128)(2,1)S(1)}, u32[]{:S(2)}, u32[]{:S(2)}) collective-permute-start(bf16[8,2,48,128]{3,2,1,0:T(8,128)(2,1)S(1)} %collective-permute-done.5.rest_6_), channel_id=1, source_target_pairs={{0,32},{32,2},{2,34},{34,4},{4,36},{36,6},{6,38},{38,0},{1,33},{33... | collective-permute-start | bytes 589832 | tf_op jit(solution)/shard_map/ppermute | solution.py:204
  44.0 8.3 %copy-start.12 = (bf16[8,2,48,128]{3,2,1,0:T(8,128)(2,1)}, bf16[8,2,48,128]{3,2,1,0:T(8,128)(2,1)S(1)}, u32[]{:S(2)}) copy-start(bf16[8,2,48,128]{3,2,1,0:T(8,128)(2,1)S(1)} %collective-permute-done.8.rest_9_) | copy-start | bytes 589828
  44.0 8.3 %collective-permute-start.12 = (bf16[8,2,48,128]{3,2,1,0:T(8,128)(2,1)S(1)}, bf16[8,2,48,128]{3,2,1,0:T(8,128)(2,1)S(1)}, u32[]{:S(2)}, u32[]{:S(2)}) collective-permute-start(bf16[8,2,48,128]{3,2,1,0:T(8,128)(2,1)S(1)} %collective-permute-done.8.rest_9_), channel_id=1, source_target_pairs={{0,38},{32,0},{2,32},{34,2},{4,34},{36,4},{6,36},{38,6},{1,39},{33... | collective-permute-start | bytes 589832 | tf_op jit(solution)/shard_map/ppermute | solution.py:204
  48.2 11.9 %copy-start.13 = (bf16[8,2,48,128]{3,2,1,0:T(8,128)(2,1)}, bf16[8,2,48,128]{3,2,1,0:T(8,128)(2,1)S(1)}, u32[]{:S(2)}) copy-start(bf16[8,2,48,128]{3,2,1,0:T(8,128)(2,1)S(1)} %collective-permute-done.6.rest_7_) | copy-start | bytes 589828
  48.2 10.8 %collective-permute-start.10 = (bf16[8,2,48,128]{3,2,1,0:T(8,128)(2,1)S(1)}, bf16[8,2,48,128]{3,2,1,0:T(8,128)(2,1)S(1)}, u32[]{:S(2)}, u32[]{:S(2)}) collective-permute-start(bf16[8,2,48,128]{3,2,1,0:T(8,128)(2,1)S(1)} %collective-permute-done.6.rest_7_), channel_id=1, source_target_pairs={{0,32},{32,2},{2,34},{34,4},{4,36},{36,6},{6,38},{38,0},{1,33},{33... | collective-permute-start | bytes 589832 | tf_op jit(solution)/shard_map/ppermute | solution.py:204
  48.2 11.9 %copy-start.14 = (bf16[8,2,48,128]{3,2,1,0:T(8,128)(2,1)}, bf16[8,2,48,128]{3,2,1,0:T(8,128)(2,1)S(1)}, u32[]{:S(2)}) copy-start(bf16[8,2,48,128]{3,2,1,0:T(8,128)(2,1)S(1)} %collective-permute-done.7.rest_8_) | copy-start | bytes 589828
  48.2 10.8 %collective-permute-start.11 = (bf16[8,2,48,128]{3,2,1,0:T(8,128)(2,1)S(1)}, bf16[8,2,48,128]{3,2,1,0:T(8,128)(2,1)S(1)}, u32[]{:S(2)}, u32[]{:S(2)}) collective-permute-start(bf16[8,2,48,128]{3,2,1,0:T(8,128)(2,1)S(1)} %collective-permute-done.7.rest_8_), channel_id=1, source_target_pairs={{0,38},{32,0},{2,32},{34,2},{4,34},{36,4},{6,36},{38,6},{1,39},{33... | collective-permute-start | bytes 589832 | tf_op jit(solution)/shard_map/ppermute | solution.py:204
  52.3 7.8 %copy-start.15 = (bf16[8,2,48,128]{3,2,1,0:T(8,128)(2,1)}, bf16[8,2,48,128]{3,2,1,0:T(8,128)(2,1)S(1)}, u32[]{:S(2)}) copy-start(bf16[8,2,48,128]{3,2,1,0:T(8,128)(2,1)S(1)} %collective-permute-done.9.rest_10_) | copy-start | bytes 589828
  52.3 7.7 %collective-permute-start.13 = (bf16[8,2,48,128]{3,2,1,0:T(8,128)(2,1)S(1)}, bf16[8,2,48,128]{3,2,1,0:T(8,128)(2,1)S(1)}, u32[]{:S(2)}, u32[]{:S(2)}) collective-permute-start(bf16[8,2,48,128]{3,2,1,0:T(8,128)(2,1)S(1)} %collective-permute-done.9.rest_10_), channel_id=1, source_target_pairs={{0,32},{32,2},{2,34},{34,4},{4,36},{36,6},{6,38},{38,0},{1,33},{33... | collective-permute-start | bytes 589832 | tf_op jit(solution)/shard_map/ppermute | solution.py:204
  52.3 7.8 %copy-start.16 = (bf16[8,2,48,128]{3,2,1,0:T(8,128)(2,1)}, bf16[8,2,48,128]{3,2,1,0:T(8,128)(2,1)S(1)}, u32[]{:S(2)}) copy-start(bf16[8,2,48,128]{3,2,1,0:T(8,128)(2,1)S(1)} %collective-permute-done.12.rest_13_) | copy-start | bytes 589828
  52.3 7.7 %collective-permute-start.14 = (bf16[8,2,48,128]{3,2,1,0:T(8,128)(2,1)S(1)}, bf16[8,2,48,128]{3,2,1,0:T(8,128)(2,1)S(1)}, u32[]{:S(2)}, u32[]{:S(2)}) collective-permute-start(bf16[8,2,48,128]{3,2,1,0:T(8,128)(2,1)S(1)} %collective-permute-done.12.rest_13_), channel_id=1, source_target_pairs={{0,38},{32,0},{2,32},{34,2},{4,34},{36,4},{6,36},{38,6},{1,39},{33... | collective-permute-start | bytes 589832 | tf_op jit(solution)/shard_map/ppermute | solution.py:204
  59.0 1.2 copy-start.17
  59.0 1.2 copy-start.18
  60.0 0.7 copy-start.19
  60.0 0.8 copy-start.20
  60.8 31.4 %all-to-all-start.2 = ((bf16[32,64,512]{2,1,0:T(8,128)(2,1)}), bf16[32,64,512]{2,1,0:T(8,128)(2,1)S(1)}, u32[]{:S(2)}, u32[]{:S(2)}) async-start(bf16[32,64,512]{2,1,0:T(8,128)(2,1)} %bitcast.11), calls=%async_computation.2 | async-start | bytes 4194304 | tf_op jit(solution)/shard_map/all_to_all | solution.py:193
  67.9 9.0 %collective-permute-start.16 = (bf16[16,4,16,1536]{3,2,1,0:T(8,128)(2,1)}, bf16[16,4,16,1536]{3,2,1,0:T(8,128)(2,1)S(1)}, u32[]{:S(2)}, u32[]{:S(2)}) collective-permute-start(bf16[16,4,16,1536]{3,2,1,0:T(8,128)(2,1)} %bitcast.4.own_f), channel_id=1, source_target_pairs={{0,1},{1,0},{2,3},{3,2},{4,5},{5,4},{6,7},{7,6},{8,9},{9,8},{10,11... | collective-permute-start | bytes 9437192 | tf_op jit(solution)/shard_map/ppermute | solution.py:197
  87.4 1.4 %copy-start.3 = (bf16[4,2,256,512]{3,2,1,0:T(8,128)(2,1)}, bf16[4,2,256,512]{3,2,1,0:T(8,128)(2,1)S(1)}, u32[]{:S(2)}) copy-start(bf16[4,2,256,512]{3,2,1,0:T(8,128)(2,1)S(1)} %get-tuple-element.53.v_ref) | copy-start | bytes 6291460
  88.8 1.3 copy-start.5
  92.2 9.4 %collective-permute-start.15 = (bf16[32,4,16,512]{3,2,1,0:T(8,128)(2,1)S(1)}, bf16[32,4,16,512]{3,2,1,0:T(8,128)(2,1)S(1)}, u32[]{:S(2)}, u32[]{:S(2)}) collective-permute-start(bf16[32,4,16,512]{3,2,1,0:T(8,128)(2,1)S(1)} %bitcast.8), channel_id=1, source_target_pairs={{0,1},{1,0},{2,3},{3,2},{4,5},{5,4},{6,7},{7,6},{8,9},{9,8},{10,11... | collective-permute-start | bytes 6291464 | tf_op jit(solution)/shard_map/ppermute | solution.py:197
  97.8 1.6 %copy-start.6 = (bf16[4,2,256,512]{3,2,1,0:T(8,128)(2,1)S(1)}, bf16[4,2,256,512]{3,2,1,0:T(8,128)(2,1)}, u32[]{:S(2)}) copy-start(bf16[4,2,256,512]{3,2,1,0:T(8,128)(2,1)} %copy-done.5) | copy-start | bytes 6291460
  99.4 2.2 %copy-start.4 = (bf16[4,2,256,512]{3,2,1,0:T(8,128)(2,1)S(1)}, bf16[4,2,256,512]{3,2,1,0:T(8,128)(2,1)}, u32[]{:S(2)}) copy-start(bf16[4,2,256,512]{3,2,1,0:T(8,128)(2,1)} %copy-done.3) | copy-start | bytes 6291460

commit v10 on v9

--- a/solution.py
+++ b/solution.py
@@ -115,7 +115,7 @@
 def build_integrals(own_f, far_f, blocks):
     return pl.pallas_call(
         integrals_kernel,
-        out_shape=[pltpu.VMEM((4, 2, 256, 512), BF16)] * 2,
+        out_shape=[pltpu.HBM((4, 2, 256, 512), BF16)] * 2,
         grid=(4,),
         in_specs=[
             pl.BlockSpec((16, 2, 16, 1536), lambda g: (0, jnp.minimum(g, 1), 0, 0)),

time: 134 us -> 134 us (level)
  local copies, waits for them, and re-layouts: 5.75 us -> 3.06 us
  Pallas kernels: 18.1 us -> 19.5 us
    unnamed x42 -> x38, local copies, waits for them, and re-layouts: 5.75 us -> 3.06 us
    pallas_call x1, Pallas kernels: 10.5 us -> 11.9 us  [build_integrals(): pl.pallas_call(integrals_kernel, out_shape=[pltpu.HBM((4, 2, 256, 512), B...]
  transfers between devices with their start and end apart: 19 -> 19, of which waited for: 11 -> 11; matrix products, arithmetic and copies ran while one was open for 0% -> 0% of each run, Pallas kernels for 12% -> 13%
where the time goes in v10:
time: 134 us
  blocking collectives  46.8 us (35%)
  starting transfers between devices  44.4 us (33%)
  waiting for transfers between devices  20 us (15%)
  Pallas kernels  19.5 us (15%)
  local copies, waits for them, and re-layouts  3.06 us (2%)
    all_to_all x3, blocking collectives, exchange(): return lax.all_to_all(x, axis, split_axis=0, concat_axis=0, tiled=True)  46.8 us
    ppermute x14, starting transfers between devices, shift(): lax.ppermute(x, RING, [(flat(z), flat((z + step) % 8)) for z in range(8)])  21.7 us
    pallas_call x1, Pallas kernels, build_integrals(): pl.pallas_call(integrals_kernel, out_shape=[pltpu.HBM((4, 2, 256, 512), B...  11.9 us
    all_to_all x2, starting transfers between devices, exchange(): return lax.all_to_all(x, axis, split_axis=0, concat_axis=0, tiled=True)  11.5 us
    ppermute x3, starting transfers between devices, other(): return lax.ppermute(x, axis, [(0, 1), (1, 0)])  11.2 us
    ppermute x14, waiting for transfers between devices, shift(): lax.ppermute(x, RING, [(flat(z), flat((z + step) % 8)) for z in range(8)])  8.67 us
    ppermute x3, waiting for transfers between devices, other(): return lax.ppermute(x, axis, [(0, 1), (1, 0)])  7.8 us
    pallas_call x1, Pallas kernels, regroup(): pl.pallas_call(regroup_kernel, out_shape=jax.ShapeDtypeStruct((4, 2, 4, 4...  4.01 us
  transfers between devices with their start and end apart: 19, of which 11 were waited for; matrix products, arithmetic and copies ran while one was open for 0% of the time, Pallas kernels for 13%

profile of v10, /device:TPU:1, one launch (start us, length us, event | category | flops | bytes accessed | tf_op | source)
XLA Modules:
  0.0 134.0 jit_solution(6896333694635435068)
XLA Ops:
  0.0 0.8 copy-done
  0.8 0.1 spread_window.1
  0.9 16.6 %all_to_all.25.own_ref = bf16[16,2,48,128]{3,2,1,0:T(8,128)(2,1)S(1)} all-to-all(bf16[16,2,48,128]{3,2,1,0:T(8,128)(2,1)S(1)} %spread_window.1), channel_id=1, replica_groups=mesh['y'=4,'zl'=2,'x'=4,'zh'=4,'core'=2] {'y','x'}, dimensions={0} | all-to-all | bytes 786432 | tf_op jit(solution)/shard_map/all_to_all | solution.py:193
  17.5 4.5 %all-to-all-start.1 = ((bf16[16,64,1536]{2,1,0:T(8,128)(2,1)}), bf16[16,64,1536]{2,1,0:T(8,128)(2,1)}, u32[]{:S(2)}, u32[]{:S(2)}) async-start(bf16[16,64,1536]{2,1,0:T(8,128)(2,1)} %bitcast.12), calls=%async_computation.1 | async-start | bytes 6291456 | tf_op jit(solution)/shard_map/all_to_all | solution.py:193
  22.0 2.0 %collective-permute-start = (bf16[16,2,48,128]{3,2,1,0:T(8,128)(2,1)S(1)}, bf16[16,2,48,128]{3,2,1,0:T(8,128)(2,1)S(1)}, u32[]{:S(2)}, u32[]{:S(2)}) collective-permute-start(bf16[16,2,48,128]{3,2,1,0:T(8,128)(2,1)S(1)} %all_to_all.25.own_ref), channel_id=1, source_target_pairs={{0,1},{1,0},{2,3},{3,2},{4,5},{5,4},{6,7},{7,6},{8,9},{9,8},{10,11... | collective-permute-start | bytes 1179656 | tf_op jit(solution)/shard_map/ppermute | solution.py:197
  23.9 1.3 %collective-permute-done.far_ref = bf16[16,2,48,128]{3,2,1,0:T(8,128)(2,1)S(1)} collective-permute-done((bf16[16,2,48,128]{3,2,1,0:T(8,128)(2,1)S(1)}, bf16[16,2,48,128]{3,2,1,0:T(8,128)(2,1)S(1)}, u32[]{:S(2)}, u32[]{:S(2)}) %collective-permute-start) | collective-permute-done | bytes 393248 | tf_op jit(solution)/shard_map/ppermute | solution.py:197
  25.3 0.2 join_window.1
  25.5 1.7 %collective-permute-start.1 = (bf16[8,2,48,128]{3,2,1,0:T(8,128)(2,1)S(1)}, bf16[8,2,48,128]{3,2,1,0:T(8,128)(2,1)S(1)}, u32[]{:S(2)}, u32[]{:S(2)}) collective-permute-start(bf16[8,2,48,128]{3,2,1,0:T(8,128)(2,1)S(1)} %get-tuple-element.37.rest_0_), channel_id=1, source_target_pairs={{0,32},{32,2},{2,34},{34,4},{4,36},{36,6},{6,38},{38,0},{1,33},{33... | collective-permute-start | bytes 589832 | tf_op jit(solution)/shard_map/ppermute | solution.py:204
  27.2 4.0 %collective-permute-start.4 = (bf16[8,2,48,128]{3,2,1,0:T(8,128)(2,1)S(1)}, bf16[8,2,48,128]{3,2,1,0:T(8,128)(2,1)S(1)}, u32[]{:S(2)}, u32[]{:S(2)}) collective-permute-start(bf16[8,2,48,128]{3,2,1,0:T(8,128)(2,1)S(1)} %get-tuple-element.38.rest_1_), channel_id=1, source_target_pairs={{0,38},{32,0},{2,32},{34,2},{4,34},{36,4},{6,36},{38,6},{1,39},{33... | collective-permute-start | bytes 589832 | tf_op jit(solution)/shard_map/ppermute | solution.py:204
  31.2 0.0 collective-permute-start.2
  31.2 2.7 %collective-permute-start.3 = (bf16[8,2,48,128]{3,2,1,0:T(8,128)(2,1)S(1)}, bf16[8,2,48,128]{3,2,1,0:T(8,128)(2,1)S(1)}, u32[]{:S(2)}, u32[]{:S(2)}) collective-permute-start(bf16[8,2,48,128]{3,2,1,0:T(8,128)(2,1)S(1)} %get-tuple-element.37.rest_0_), channel_id=1, source_target_pairs={{0,38},{32,0},{2,32},{34,2},{4,34},{36,4},{6,36},{38,6},{1,39},{33... | collective-permute-start | bytes 589832 | tf_op jit(solution)/shard_map/ppermute | solution.py:204
  33.9 2.3 %collective-permute-done.1.rest_2_ = bf16[8,2,48,128]{3,2,1,0:T(8,128)(2,1)S(1)} collective-permute-done((bf16[8,2,48,128]{3,2,1,0:T(8,128)(2,1)S(1)}, bf16[8,2,48,128]{3,2,1,0:T(8,128)(2,1)S(1)}, u32[]{:S(2)}, u32[]{:S(2)}) %collective-permute-start.1) | collective-permute-done | bytes 196640 | tf_op jit(solution)/shard_map/ppermute | solution.py:204
  36.2 0.0 collective-permute-start.5
  36.2 2.7 %collective-permute-start.8 = (bf16[8,2,48,128]{3,2,1,0:T(8,128)(2,1)S(1)}, bf16[8,2,48,128]{3,2,1,0:T(8,128)(2,1)S(1)}, u32[]{:S(2)}, u32[]{:S(2)}) collective-permute-start(bf16[8,2,48,128]{3,2,1,0:T(8,128)(2,1)S(1)} %collective-permute-done.4.rest_5_), channel_id=1, source_target_pairs={{0,38},{32,0},{2,32},{34,2},{4,34},{36,4},{6,36},{38,6},{1,39},{33... | collective-permute-start | bytes 589832 | tf_op jit(solution)/shard_map/ppermute | solution.py:204
  38.9 1.5 %collective-permute-done.2.rest_3_ = bf16[8,2,48,128]{3,2,1,0:T(8,128)(2,1)S(1)} collective-permute-done((bf16[8,2,48,128]{3,2,1,0:T(8,128)(2,1)S(1)}, bf16[8,2,48,128]{3,2,1,0:T(8,128)(2,1)S(1)}, u32[]{:S(2)}, u32[]{:S(2)}) %collective-permute-start.2) | collective-permute-done | bytes 196640 | tf_op jit(solution)/shard_map/ppermute | solution.py:204
  40.4 2.7 %collective-permute-start.7 = (bf16[8,2,48,128]{3,2,1,0:T(8,128)(2,1)S(1)}, bf16[8,2,48,128]{3,2,1,0:T(8,128)(2,1)S(1)}, u32[]{:S(2)}, u32[]{:S(2)}) collective-permute-start(bf16[8,2,48,128]{3,2,1,0:T(8,128)(2,1)S(1)} %collective-permute-done.3.rest_4_), channel_id=1, source_target_pairs={{0,38},{32,0},{2,32},{34,2},{4,34},{36,4},{6,36},{38,6},{1,39},{33... | collective-permute-start | bytes 589832 | tf_op jit(solution)/shard_map/ppermute | solution.py:204
  43.1 0.9 collective-permute-done.5.rest_6_
  44.0 0.0 collective-permute-start.9
  44.0 0.0 collective-permute-done.8.rest_9_
  44.0 2.7 %collective-permute-start.12 = (bf16[8,2,48,128]{3,2,1,0:T(8,128)(2,1)S(1)}, bf16[8,2,48,128]{3,2,1,0:T(8,128)(2,1)S(1)}, u32[]{:S(2)}, u32[]{:S(2)}) collective-permute-start(bf16[8,2,48,128]{3,2,1,0:T(8,128)(2,1)S(1)} %collective-permute-done.8.rest_9_), channel_id=1, source_target_pairs={{0,38},{32,0},{2,32},{34,2},{4,34},{36,4},{6,36},{38,6},{1,39},{33... | collective-permute-start | bytes 589832 | tf_op jit(solution)/shard_map/ppermute | solution.py:204
  46.7 1.5 %collective-permute-done.6.rest_7_ = bf16[8,2,48,128]{3,2,1,0:T(8,128)(2,1)S(1)} collective-permute-done((bf16[8,2,48,128]{3,2,1,0:T(8,128)(2,1)S(1)}, bf16[8,2,48,128]{3,2,1,0:T(8,128)(2,1)S(1)}, u32[]{:S(2)}, u32[]{:S(2)}) %collective-permute-start.6) | collective-permute-done | bytes 196640 | tf_op jit(solution)/shard_map/ppermute | solution.py:204
  48.2 0.0 collective-permute-start.10
  48.2 0.0 collective-permute-done.7.rest_8_
  48.2 2.7 %collective-permute-start.11 = (bf16[8,2,48,128]{3,2,1,0:T(8,128)(2,1)S(1)}, bf16[8,2,48,128]{3,2,1,0:T(8,128)(2,1)S(1)}, u32[]{:S(2)}, u32[]{:S(2)}) collective-permute-start(bf16[8,2,48,128]{3,2,1,0:T(8,128)(2,1)S(1)} %collective-permute-done.7.rest_8_), channel_id=1, source_target_pairs={{0,38},{32,0},{2,32},{34,2},{4,34},{36,4},{6,36},{38,6},{1,39},{33... | collective-permute-start | bytes 589832 | tf_op jit(solution)/shard_map/ppermute | solution.py:204
  50.9 1.4 %collective-permute-done.9.rest_10_ = bf16[8,2,48,128]{3,2,1,0:T(8,128)(2,1)S(1)} collective-permute-done((bf16[8,2,48,128]{3,2,1,0:T(8,128)(2,1)S(1)}, bf16[8,2,48,128]{3,2,1,0:T(8,128)(2,1)S(1)}, u32[]{:S(2)}, u32[]{:S(2)}) %collective-permute-start.9) | collective-permute-done | bytes 196640 | tf_op jit(solution)/shard_map/ppermute | solution.py:204
  52.3 0.0 collective-permute-start.13
  52.3 2.7 %collective-permute-start.14 = (bf16[8,2,48,128]{3,2,1,0:T(8,128)(2,1)S(1)}, bf16[8,2,48,128]{3,2,1,0:T(8,128)(2,1)S(1)}, u32[]{:S(2)}, u32[]{:S(2)}) collective-permute-start(bf16[8,2,48,128]{3,2,1,0:T(8,128)(2,1)S(1)} %collective-permute-done.12.rest_13_), channel_id=1, source_target_pairs={{0,38},{32,0},{2,32},{34,2},{4,34},{36,4},{6,36},{38,6},{1,39},{33... | collective-permute-start | bytes 589832 | tf_op jit(solution)/shard_map/ppermute | solution.py:204
  55.0 4.0 %regroup_amplitudes.1 = bf16[4,2,4,4,16,512]{5,4,3,2,1,0:T(8,128)(2,1)} custom-call(bf16[16,64,512]{2,1,0:T(8,128)(2,1)} %bitcast.13), custom_call_target="tpu_custom_call" | custom-call | tf_op jit(solution)/shard_map/regroup_amplitudes/pallas_call | solution.py:74
  59.0 0.0 collective-permute-done.10.rest_11_
  59.0 1.0 collective-permute-done.13.rest_14_
  60.0 0.0 collective-permute-done.14.rest_15_
  60.0 0.1 all-to-all-done.1
  60.2 0.5 copy-done.17
  60.7 0.1 copy-done.18
  60.8 7.0 %all-to-all-start.2 = ((bf16[32,64,512]{2,1,0:T(8,128)(2,1)}), bf16[32,64,512]{2,1,0:T(8,128)(2,1)S(1)}, u32[]{:S(2)}, u32[]{:S(2)}) async-start(bf16[32,64,512]{2,1,0:T(8,128)(2,1)} %bitcast.11), calls=%async_computation.2 | async-start | bytes 4194304 | tf_op jit(solution)/shard_map/all_to_all | solution.py:193
  67.9 3.5 %collective-permute-start.16 = (bf16[16,4,16,1536]{3,2,1,0:T(8,128)(2,1)}, bf16[16,4,16,1536]{3,2,1,0:T(8,128)(2,1)S(1)}, u32[]{:S(2)}, u32[]{:S(2)}) collective-permute-start(bf16[16,4,16,1536]{3,2,1,0:T(8,128)(2,1)} %bitcast.4.own_f), channel_id=1, source_target_pairs={{0,1},{1,0},{2,3},{3,2},{4,5},{5,4},{6,7},{7,6},{8,9},{9,8},{10,11... | collective-permute-start | bytes 9437192 | tf_op jit(solution)/shard_map/ppermute | solution.py:197
  71.4 5.5 %collective-permute-done.16.far_f = bf16[16,4,16,1536]{3,2,1,0:T(8,128)(2,1)S(1)} collective-permute-done((bf16[16,4,16,1536]{3,2,1,0:T(8,128)(2,1)}, bf16[16,4,16,1536]{3,2,1,0:T(8,128)(2,1)S(1)}, u32[]{:S(2)}, u32[]{:S(2)}) %collective-permute-start.16) | collective-permute-done | bytes 3145760 | tf_op jit(solution)/shard_map/ppermute | solution.py:197
  76.9 11.9 %build_integrals.1 = (bf16[4,2,256,512]{3,2,1,0:T(8,128)(2,1)}, bf16[4,2,256,512]{3,2,1,0:T(8,128)(2,1)}) custom-call(bf16[16,4,16,1536]{3,2,1,0:T(8,128)(2,1)} %bitcast.4.own_f, bf16[16,4,16,1536]{3,2,1,0:T(8,128)(2,1)S(1)} %collective-permute-done.16.far_f, bf16[8,2,48,128]{3,2,1,0:T(8,128)(2,1)} %copy-done.1, bf16[8,2,48,128]{3,2,1,0:T(8,128)(2,1)} %copy-done.2, ...), custom_call_target="tpu_custom_call" | custom-call | flops 6499999744 | bytes 14000000 | tf_op jit(solution)/shard_map/build_integrals/pallas_call | solution.py:116
  88.8 3.4 %all-to-all-done.2 = bf16[32,64,512]{2,1,0:T(8,128)(2,1)S(1)} async-done(((bf16[32,64,512]{2,1,0:T(8,128)(2,1)}), bf16[32,64,512]{2,1,0:T(8,128)(2,1)S(1)}, u32[]{:S(2)}, u32[]{:S(2)}) %all-to-all-start.2) | async-done | bytes 2097184 | tf_op jit(solution)/shard_map/all_to_all | solution.py:193
  92.2 5.7 %collective-permute-start.15 = (bf16[32,4,16,512]{3,2,1,0:T(8,128)(2,1)S(1)}, bf16[32,4,16,512]{3,2,1,0:T(8,128)(2,1)S(1)}, u32[]{:S(2)}, u32[]{:S(2)}) collective-permute-start(bf16[32,4,16,512]{3,2,1,0:T(8,128)(2,1)S(1)} %bitcast.8), channel_id=1, source_target_pairs={{0,1},{1,0},{2,3},{3,2},{4,5},{5,4},{6,7},{7,6},{8,9},{9,8},{10,11... | collective-permute-start | bytes 6291464 | tf_op jit(solution)/shard_map/ppermute | solution.py:197
  97.9 1.6 %copy-done.4 = bf16[4,2,256,512]{3,2,1,0:T(8,128)(2,1)S(1)} copy-done((bf16[4,2,256,512]{3,2,1,0:T(8,128)(2,1)S(1)}, bf16[4,2,256,512]{3,2,1,0:T(8,128)(2,1)}, u32[]{:S(2)}) %copy-start.4) | copy-done | bytes 2097176
  99.4 1.2 ladder_part.2.rest_0_
  100.7 0.9 collective-permute-done.15.t_ref
  101.6 1.2 ladder_part.3
  102.9 13.8 %all_to_all.26.parts_ref = bf16[16,2,16,512]{3,2,1,0:T(8,128)(2,1)S(1)} all-to-all(bf16[16,2,16,512]{3,2,1,0:T(8,128)(2,1)S(1)} %ladder_part.3), channel_id=1, replica_groups=mesh['y'=4,'zl'=2,'x'=4,'zh'=4,'core'=2] {'x','y'}, dimensions={0} | all-to-all | bytes 1048576 | tf_op jit(solution)/shard_map/all_to_all | solution.py:193
  116.7 0.2 sum_parts.1
  116.9 16.5 %all_to_all.27.parts_ref = f32[8,16,128]{2,1,0:T(8,128)S(1)} all-to-all(f32[8,16,128]{2,1,0:T(8,128)S(1)} %sum_parts.1), channel_id=1, replica_groups=mesh['y'=4,'zl'=2,'x'=4,'zh'=4,'core'=2] {'core','zh'}, dimensions={0} | all-to-all | bytes 131072 | tf_op jit(solution)/shard_map/all_to_all | solution.py:193
  133.3 0.7 finish.1
  (39 shorter events, 0.1 us)
Async XLA Ops:
  0.0 0.8 copy-start
  17.5 42.6 %all-to-all-start.1 = ((bf16[16,64,1536]{2,1,0:T(8,128)(2,1)}), bf16[16,64,1536]{2,1,0:T(8,128)(2,1)}, u32[]{:S(2)}, u32[]{:S(2)}) async-start(bf16[16,64,1536]{2,1,0:T(8,128)(2,1)} %bitcast.12), calls=%async_computation.1 | async-start | bytes 6291456 | tf_op jit(solution)/shard_map/all_to_all | solution.py:193
  22.0 3.3 %collective-permute-start = (bf16[16,2,48,128]{3,2,1,0:T(8,128)(2,1)S(1)}, bf16[16,2,48,128]{3,2,1,0:T(8,128)(2,1)S(1)}, u32[]{:S(2)}, u32[]{:S(2)}) collective-permute-start(bf16[16,2,48,128]{3,2,1,0:T(8,128)(2,1)S(1)} %all_to_all.25.own_ref), channel_id=1, source_target_pairs={{0,1},{1,0},{2,3},{3,2},{4,5},{5,4},{6,7},{7,6},{8,9},{9,8},{10,11... | collective-permute-start | bytes 1179656 | tf_op jit(solution)/shard_map/ppermute | solution.py:197
  25.4 35.3 %copy-start.1 = (bf16[8,2,48,128]{3,2,1,0:T(8,128)(2,1)}, bf16[8,2,48,128]{3,2,1,0:T(8,128)(2,1)S(1)}, u32[]{:S(2)}) copy-start(bf16[8,2,48,128]{3,2,1,0:T(8,128)(2,1)S(1)} %get-tuple-element.37.rest_0_) | copy-start | bytes 589828
  25.5 35.3 %copy-start.2 = (bf16[8,2,48,128]{3,2,1,0:T(8,128)(2,1)}, bf16[8,2,48,128]{3,2,1,0:T(8,128)(2,1)S(1)}, u32[]{:S(2)}) copy-start(bf16[8,2,48,128]{3,2,1,0:T(8,128)(2,1)S(1)} %get-tuple-element.38.rest_1_) | copy-start | bytes 589828
  25.5 10.7 %collective-permute-start.1 = (bf16[8,2,48,128]{3,2,1,0:T(8,128)(2,1)S(1)}, bf16[8,2,48,128]{3,2,1,0:T(8,128)(2,1)S(1)}, u32[]{:S(2)}, u32[]{:S(2)}) collective-permute-start(bf16[8,2,48,128]{3,2,1,0:T(8,128)(2,1)S(1)} %get-tuple-element.37.rest_0_), channel_id=1, source_target_pairs={{0,32},{32,2},{2,34},{34,4},{4,36},{36,6},{6,38},{38,0},{1,33},{33... | collective-permute-start | bytes 589832 | tf_op jit(solution)/shard_map/ppermute | solution.py:204
  27.2 9.0 %collective-permute-start.4 = (bf16[8,2,48,128]{3,2,1,0:T(8,128)(2,1)S(1)}, bf16[8,2,48,128]{3,2,1,0:T(8,128)(2,1)S(1)}, u32[]{:S(2)}, u32[]{:S(2)}) collective-permute-start(bf16[8,2,48,128]{3,2,1,0:T(8,128)(2,1)S(1)} %get-tuple-element.38.rest_1_), channel_id=1, source_target_pairs={{0,38},{32,0},{2,32},{34,2},{4,34},{36,4},{6,36},{38,6},{1,39},{33... | collective-permute-start | bytes 589832 | tf_op jit(solution)/shard_map/ppermute | solution.py:204
  31.2 9.2 %collective-permute-start.2 = (bf16[8,2,48,128]{3,2,1,0:T(8,128)(2,1)S(1)}, bf16[8,2,48,128]{3,2,1,0:T(8,128)(2,1)S(1)}, u32[]{:S(2)}, u32[]{:S(2)}) collective-permute-start(bf16[8,2,48,128]{3,2,1,0:T(8,128)(2,1)S(1)} %get-tuple-element.38.rest_1_), channel_id=1, source_target_pairs={{0,32},{32,2},{2,34},{34,4},{4,36},{36,6},{6,38},{38,0},{1,33},{33... | collective-permute-start | bytes 589832 | tf_op jit(solution)/shard_map/ppermute | solution.py:204
  31.2 9.2 %collective-permute-start.3 = (bf16[8,2,48,128]{3,2,1,0:T(8,128)(2,1)S(1)}, bf16[8,2,48,128]{3,2,1,0:T(8,128)(2,1)S(1)}, u32[]{:S(2)}, u32[]{:S(2)}) collective-permute-start(bf16[8,2,48,128]{3,2,1,0:T(8,128)(2,1)S(1)} %get-tuple-element.37.rest_0_), channel_id=1, source_target_pairs={{0,38},{32,0},{2,32},{34,2},{4,34},{36,4},{6,36},{38,6},{1,39},{33... | collective-permute-start | bytes 589832 | tf_op jit(solution)/shard_map/ppermute | solution.py:204
  36.2 24.6 %copy-start.5 = (bf16[8,2,48,128]{3,2,1,0:T(8,128)(2,1)}, bf16[8,2,48,128]{3,2,1,0:T(8,128)(2,1)S(1)}, u32[]{:S(2)}) copy-start(bf16[8,2,48,128]{3,2,1,0:T(8,128)(2,1)S(1)} %collective-permute-done.1.rest_2_) | copy-start | bytes 589828
  36.2 7.8 %collective-permute-start.5 = (bf16[8,2,48,128]{3,2,1,0:T(8,128)(2,1)S(1)}, bf16[8,2,48,128]{3,2,1,0:T(8,128)(2,1)S(1)}, u32[]{:S(2)}, u32[]{:S(2)}) collective-permute-start(bf16[8,2,48,128]{3,2,1,0:T(8,128)(2,1)S(1)} %collective-permute-done.1.rest_2_), channel_id=1, source_target_pairs={{0,32},{32,2},{2,34},{34,4},{4,36},{36,6},{6,38},{38,0},{1,33},{33... | collective-permute-start | bytes 589832 | tf_op jit(solution)/shard_map/ppermute | solution.py:204
  36.2 24.6 %copy-start.6 = (bf16[8,2,48,128]{3,2,1,0:T(8,128)(2,1)}, bf16[8,2,48,128]{3,2,1,0:T(8,128)(2,1)S(1)}, u32[]{:S(2)}) copy-start(bf16[8,2,48,128]{3,2,1,0:T(8,128)(2,1)S(1)} %collective-permute-done.4.rest_5_) | copy-start | bytes 589828
  36.2 7.8 %collective-permute-start.8 = (bf16[8,2,48,128]{3,2,1,0:T(8,128)(2,1)S(1)}, bf16[8,2,48,128]{3,2,1,0:T(8,128)(2,1)S(1)}, u32[]{:S(2)}, u32[]{:S(2)}) collective-permute-start(bf16[8,2,48,128]{3,2,1,0:T(8,128)(2,1)S(1)} %collective-permute-done.4.rest_5_), channel_id=1, source_target_pairs={{0,38},{32,0},{2,32},{34,2},{4,34},{36,4},{6,36},{38,6},{1,39},{33... | collective-permute-start | bytes 589832 | tf_op jit(solution)/shard_map/ppermute | solution.py:204
  40.4 20.4 %copy-start.7 = (bf16[8,2,48,128]{3,2,1,0:T(8,128)(2,1)}, bf16[8,2,48,128]{3,2,1,0:T(8,128)(2,1)S(1)}, u32[]{:S(2)}) copy-start(bf16[8,2,48,128]{3,2,1,0:T(8,128)(2,1)S(1)} %collective-permute-done.2.rest_3_) | copy-start | bytes 589828
  40.4 7.8 %collective-permute-start.6 = (bf16[8,2,48,128]{3,2,1,0:T(8,128)(2,1)S(1)}, bf16[8,2,48,128]{3,2,1,0:T(8,128)(2,1)S(1)}, u32[]{:S(2)}, u32[]{:S(2)}) collective-permute-start(bf16[8,2,48,128]{3,2,1,0:T(8,128)(2,1)S(1)} %collective-permute-done.2.rest_3_), channel_id=1, source_target_pairs={{0,32},{32,2},{2,34},{34,4},{4,36},{36,6},{6,38},{38,0},{1,33},{33... | collective-permute-start | bytes 589832 | tf_op jit(solution)/shard_map/ppermute | solution.py:204
  40.4 20.4 %copy-start.8 = (bf16[8,2,48,128]{3,2,1,0:T(8,128)(2,1)}, bf16[8,2,48,128]{3,2,1,0:T(8,128)(2,1)S(1)}, u32[]{:S(2)}) copy-start(bf16[8,2,48,128]{3,2,1,0:T(8,128)(2,1)S(1)} %collective-permute-done.3.rest_4_) | copy-start | bytes 589828
  40.4 7.8 %collective-permute-start.7 = (bf16[8,2,48,128]{3,2,1,0:T(8,128)(2,1)S(1)}, bf16[8,2,48,128]{3,2,1,0:T(8,128)(2,1)S(1)}, u32[]{:S(2)}, u32[]{:S(2)}) collective-permute-start(bf16[8,2,48,128]{3,2,1,0:T(8,128)(2,1)S(1)} %collective-permute-done.3.rest_4_), channel_id=1, source_target_pairs={{0,38},{32,0},{2,32},{34,2},{4,34},{36,4},{6,36},{38,6},{1,39},{33... | collective-permute-start | bytes 589832 | tf_op jit(solution)/shard_map/ppermute | solution.py:204
  44.0 16.8 %copy-start.9 = (bf16[8,2,48,128]{3,2,1,0:T(8,128)(2,1)}, bf16[8,2,48,128]{3,2,1,0:T(8,128)(2,1)S(1)}, u32[]{:S(2)}) copy-start(bf16[8,2,48,128]{3,2,1,0:T(8,128)(2,1)S(1)} %collective-permute-done.5.rest_6_) | copy-start | bytes 589828
  44.0 8.3 %collective-permute-start.9 = (bf16[8,2,48,128]{3,2,1,0:T(8,128)(2,1)S(1)}, bf16[8,2,48,128]{3,2,1,0:T(8,128)(2,1)S(1)}, u32[]{:S(2)}, u32[]{:S(2)}) collective-permute-start(bf16[8,2,48,128]{3,2,1,0:T(8,128)(2,1)S(1)} %collective-permute-done.5.rest_6_), channel_id=1, source_target_pairs={{0,32},{32,2},{2,34},{34,4},{4,36},{36,6},{6,38},{38,0},{1,33},{33... | collective-permute-start | bytes 589832 | tf_op jit(solution)/shard_map/ppermute | solution.py:204
  44.0 8.3 %copy-start.10 = (bf16[8,2,48,128]{3,2,1,0:T(8,128)(2,1)}, bf16[8,2,48,128]{3,2,1,0:T(8,128)(2,1)S(1)}, u32[]{:S(2)}) copy-start(bf16[8,2,48,128]{3,2,1,0:T(8,128)(2,1)S(1)} %collective-permute-done.8.rest_9_) | copy-start | bytes 589828
  44.0 8.3 %collective-permute-start.12 = (bf16[8,2,48,128]{3,2,1,0:T(8,128)(2,1)S(1)}, bf16[8,2,48,128]{3,2,1,0:T(8,128)(2,1)S(1)}, u32[]{:S(2)}, u32[]{:S(2)}) collective-permute-start(bf16[8,2,48,128]{3,2,1,0:T(8,128)(2,1)S(1)} %collective-permute-done.8.rest_9_), channel_id=1, source_target_pairs={{0,38},{32,0},{2,32},{34,2},{4,34},{36,4},{6,36},{38,6},{1,39},{33... | collective-permute-start | bytes 589832 | tf_op jit(solution)/shard_map/ppermute | solution.py:204
  48.2 11.9 %copy-start.11 = (bf16[8,2,48,128]{3,2,1,0:T(8,128)(2,1)}, bf16[8,2,48,128]{3,2,1,0:T(8,128)(2,1)S(1)}, u32[]{:S(2)}) copy-start(bf16[8,2,48,128]{3,2,1,0:T(8,128)(2,1)S(1)} %collective-permute-done.6.rest_7_) | copy-start | bytes 589828
  48.2 10.8 %collective-permute-start.10 = (bf16[8,2,48,128]{3,2,1,0:T(8,128)(2,1)S(1)}, bf16[8,2,48,128]{3,2,1,0:T(8,128)(2,1)S(1)}, u32[]{:S(2)}, u32[]{:S(2)}) collective-permute-start(bf16[8,2,48,128]{3,2,1,0:T(8,128)(2,1)S(1)} %collective-permute-done.6.rest_7_), channel_id=1, source_target_pairs={{0,32},{32,2},{2,34},{34,4},{4,36},{36,6},{6,38},{38,0},{1,33},{33... | collective-permute-start | bytes 589832 | tf_op jit(solution)/shard_map/ppermute | solution.py:204
  48.2 11.9 %copy-start.12 = (bf16[8,2,48,128]{3,2,1,0:T(8,128)(2,1)}, bf16[8,2,48,128]{3,2,1,0:T(8,128)(2,1)S(1)}, u32[]{:S(2)}) copy-start(bf16[8,2,48,128]{3,2,1,0:T(8,128)(2,1)S(1)} %collective-permute-done.7.rest_8_) | copy-start | bytes 589828
  48.2 10.8 %collective-permute-start.11 = (bf16[8,2,48,128]{3,2,1,0:T(8,128)(2,1)S(1)}, bf16[8,2,48,128]{3,2,1,0:T(8,128)(2,1)S(1)}, u32[]{:S(2)}, u32[]{:S(2)}) collective-permute-start(bf16[8,2,48,128]{3,2,1,0:T(8,128)(2,1)S(1)} %collective-permute-done.7.rest_8_), channel_id=1, source_target_pairs={{0,38},{32,0},{2,32},{34,2},{4,34},{36,4},{6,36},{38,6},{1,39},{33... | collective-permute-start | bytes 589832 | tf_op jit(solution)/shard_map/ppermute | solution.py:204
  52.3 7.8 %copy-start.13 = (bf16[8,2,48,128]{3,2,1,0:T(8,128)(2,1)}, bf16[8,2,48,128]{3,2,1,0:T(8,128)(2,1)S(1)}, u32[]{:S(2)}) copy-start(bf16[8,2,48,128]{3,2,1,0:T(8,128)(2,1)S(1)} %collective-permute-done.9.rest_10_) | copy-start | bytes 589828
  52.3 7.7 %collective-permute-start.13 = (bf16[8,2,48,128]{3,2,1,0:T(8,128)(2,1)S(1)}, bf16[8,2,48,128]{3,2,1,0:T(8,128)(2,1)S(1)}, u32[]{:S(2)}, u32[]{:S(2)}) collective-permute-start(bf16[8,2,48,128]{3,2,1,0:T(8,128)(2,1)S(1)} %collective-permute-done.9.rest_10_), channel_id=1, source_target_pairs={{0,32},{32,2},{2,34},{34,4},{4,36},{36,6},{6,38},{38,0},{1,33},{33... | collective-permute-start | bytes 589832 | tf_op jit(solution)/shard_map/ppermute | solution.py:204
  52.3 7.8 %copy-start.14 = (bf16[8,2,48,128]{3,2,1,0:T(8,128)(2,1)}, bf16[8,2,48,128]{3,2,1,0:T(8,128)(2,1)S(1)}, u32[]{:S(2)}) copy-start(bf16[8,2,48,128]{3,2,1,0:T(8,128)(2,1)S(1)} %collective-permute-done.12.rest_13_) | copy-start | bytes 589828
  52.3 7.7 %collective-permute-start.14 = (bf16[8,2,48,128]{3,2,1,0:T(8,128)(2,1)S(1)}, bf16[8,2,48,128]{3,2,1,0:T(8,128)(2,1)S(1)}, u32[]{:S(2)}, u32[]{:S(2)}) collective-permute-start(bf16[8,2,48,128]{3,2,1,0:T(8,128)(2,1)S(1)} %collective-permute-done.12.rest_13_), channel_id=1, source_target_pairs={{0,38},{32,0},{2,32},{34,2},{4,34},{36,4},{6,36},{38,6},{1,39},{33... | collective-permute-start | bytes 589832 | tf_op jit(solution)/shard_map/ppermute | solution.py:204
  59.0 1.1 copy-start.15
  59.0 1.1 copy-start.16
  60.0 0.7 copy-start.17
  60.0 0.8 copy-start.18
  60.8 31.4 %all-to-all-start.2 = ((bf16[32,64,512]{2,1,0:T(8,128)(2,1)}), bf16[32,64,512]{2,1,0:T(8,128)(2,1)S(1)}, u32[]{:S(2)}, u32[]{:S(2)}) async-start(bf16[32,64,512]{2,1,0:T(8,128)(2,1)} %bitcast.11), calls=%async_computation.2 | async-start | bytes 4194304 | tf_op jit(solution)/shard_map/all_to_all | solution.py:193
  67.9 9.0 %collective-permute-start.16 = (bf16[16,4,16,1536]{3,2,1,0:T(8,128)(2,1)}, bf16[16,4,16,1536]{3,2,1,0:T(8,128)(2,1)S(1)}, u32[]{:S(2)}, u32[]{:S(2)}) collective-permute-start(bf16[16,4,16,1536]{3,2,1,0:T(8,128)(2,1)} %bitcast.4.own_f), channel_id=1, source_target_pairs={{0,1},{1,0},{2,3},{3,2},{4,5},{5,4},{6,7},{7,6},{8,9},{9,8},{10,11... | collective-permute-start | bytes 9437192 | tf_op jit(solution)/shard_map/ppermute | solution.py:197
  92.2 9.5 %collective-permute-start.15 = (bf16[32,4,16,512]{3,2,1,0:T(8,128)(2,1)S(1)}, bf16[32,4,16,512]{3,2,1,0:T(8,128)(2,1)S(1)}, u32[]{:S(2)}, u32[]{:S(2)}) collective-permute-start(bf16[32,4,16,512]{3,2,1,0:T(8,128)(2,1)S(1)} %bitcast.8), channel_id=1, source_target_pairs={{0,1},{1,0},{2,3},{3,2},{4,5},{5,4},{6,7},{7,6},{8,9},{9,8},{10,11... | collective-permute-start | bytes 6291464 | tf_op jit(solution)/shard_map/ppermute | solution.py:197
  97.8 1.6 %copy-start.4 = (bf16[4,2,256,512]{3,2,1,0:T(8,128)(2,1)S(1)}, bf16[4,2,256,512]{3,2,1,0:T(8,128)(2,1)}, u32[]{:S(2)}) copy-start(bf16[4,2,256,512]{3,2,1,0:T(8,128)(2,1)} %get-tuple-element.54.v_ref) | copy-start | bytes 6291460
  99.4 2.2 %copy-start.3 = (bf16[4,2,256,512]{3,2,1,0:T(8,128)(2,1)S(1)}, bf16[4,2,256,512]{3,2,1,0:T(8,128)(2,1)}, u32[]{:S(2)}) copy-start(bf16[4,2,256,512]{3,2,1,0:T(8,128)(2,1)} %get-tuple-element.53.v_ref) | copy-start | bytes 6291460
